TPU v7x, 128 devices: a whole 4x4x4 slice. The times are simulated.
128 devices in a mesh: pole: 4 (over x_lo, core), tile: 32 (over y, x_hi, z).
Axes of the slice: x: 4 (x_hi: 2, x_lo: 2; x = x_hi * 2 + x_lo), y: 4, z: 4, core: 2. Of those that a mesh axis runs over, the one named last changes fastest.
Arguments:
- psi: float32 [2, 1024, 16, 512], P(None, 'tile', None, 'pole'), may hold values from 0 to 3
- trap: float32 [1024, 16, 512], P('tile', None, 'pole'), may hold values from 0 to 2
- pole_shift: float32 [8, 2], P('pole'), may hold values from 1 to 3
- pole_weight: float32 [8, 2], P('pole'), may hold values from -1 to 1
Outputs:
- evolved: float32 [2, 1024, 16, 512], P(None, 'tile', None, 'pole')
All inputs are finite; a program needn't handle non-finite values.
Results may differ from a plain program's by a relative error of at most 0.0003.
Values sent between devices are 32-bit elements; how exact they have to be, the bound alone decides.
No kernel may reach another device: no remote copies, remote signals or barrier semaphores. Data moves between devices by JAX's collectives and lax.ppermute only.
A program may use at most 128 MiB of HBM per device.

v0:
```python
import jax
import jax.numpy as jnp
from jax import lax
from jax.sharding import PartitionSpec as P

ITERS = 3


COUPLING = 0.5
TIME_STEP = 0.25
WEIGHT_CENTRE = -128.0 / 30.0
WEIGHT_FACE = 14.0 / 30.0
WEIGHT_EDGE = 3.0 / 30.0
WEIGHT_CORNER = 1.0 / 30.0


def with_halo(x, sides, width):
    for axis, dim in sides:
        devices, length = (lax.axis_size(axis), x.shape[dim])
        up = [(i, (i + 1) % devices) for i in range(devices - 1)]
        down = [(j, i) for i, j in up]
        last = lax.slice_in_dim(x, length - width, length, axis=dim)
        leading = lax.slice_in_dim(x, 0, width, axis=dim)
        before = lax.ppermute(last, axis, up)
        after = lax.ppermute(leading, axis, down)
        x = jnp.concatenate([before, x, after], axis=dim)
    return x


def laplace(extended):
    padded = jnp.pad(extended, ((0, 0), (0, 0), (0, 0), (1, 1), (0, 0)))
    edges = (
        padded[:, :, :, :-2, 1:-1]
        + padded[:, :, :, 2:, 1:-1]
        + padded[:, :, :, 1:-1, :-2]
        + padded[:, :, :, 1:-1, 2:]
    )
    corners = (
        padded[:, :, :, :-2, :-2]
        + padded[:, :, :, :-2, 2:]
        + padded[:, :, :, 2:, :-2]
        + padded[:, :, :, 2:, 2:]
    )
    centre = extended[:, :, :, :, 1:-1]
    in_plane = WEIGHT_CENTRE * centre + WEIGHT_FACE * edges + WEIGHT_EDGE * corners
    off_plane = WEIGHT_FACE * centre + WEIGHT_EDGE * edges + WEIGHT_CORNER * corners
    return in_plane[:, :, 1:-1] + off_plane[:, :, :-2] + off_plane[:, :, 2:]


def operate(extended, potential, shift_re, shift_im):
    current = extended[:, :, 1:-1, :, 1:-1]
    kinetic = -0.5 * laplace(extended) + potential * current
    real_part = shift_re * current[:, 0] - shift_im * current[:, 1] - TIME_STEP * kinetic[:, 1]
    imag_part = shift_re * current[:, 1] + shift_im * current[:, 0] + TIME_STEP * kinetic[:, 0]
    return jnp.stack([real_part, imag_part], axis=1)


def bilinear_terms(left, right):
    real_sum = jnp.sum(left[:, 0] * right[:, 0] - left[:, 1] * right[:, 1], axis=(1, 2, 3))
    imag_sum = jnp.sum(left[:, 0] * right[:, 1] + left[:, 1] * right[:, 0], axis=(1, 2, 3))
    return (real_sum, imag_sum)


def divide(numer, denom):
    norm_sq = denom[0] * denom[0] + denom[1] * denom[1]
    return (
        (numer[0] * denom[0] + numer[1] * denom[1]) / norm_sq,
        (numer[1] * denom[0] - numer[0] * denom[1]) / norm_sq,
    )


def scaled(coef, vector):
    coef_re = coef[0][:, None, None, None]
    coef_im = coef[1][:, None, None, None]
    return jnp.stack(
        [
            coef_re * vector[:, 0] - coef_im * vector[:, 1],
            coef_re * vector[:, 1] + coef_im * vector[:, 0],
        ],
        axis=1,
    )


def on_device(psi, trap, pole_shift, pole_weight):
    local_potential = trap + COUPLING * (psi[0] * psi[0] + psi[1] * psi[1])
    full_psi, potential = (
        lax.all_gather(psi, "pole", axis=3, tiled=True),
        lax.all_gather(local_potential, "pole", axis=2, tiled=True),
    )
    shifts, weights = (pole_shift, pole_weight)

    def reduce_forms(values):
        return lax.psum((values[0], values[1]), "tile")

    count = shifts.shape[0]
    shift_re = shifts[:, 0][:, None, None, None]
    shift_im = shifts[:, 1][:, None, None, None]
    rhs = jnp.broadcast_to(full_psi[None], (count,) + full_psi.shape)
    iterate = jnp.zeros_like(rhs)
    remain = rhs
    search = rhs
    rho = reduce_forms(bilinear_terms(remain, remain))
    for step in range(ITERS):
        grown = with_halo(search, (("tile", 2),), 1)
        image = operate(
            jnp.pad(grown, ((0, 0), (0, 0), (0, 0), (0, 0), (1, 1))), potential, shift_re, shift_im
        )
        curv = reduce_forms(bilinear_terms(search, image))
        alpha = divide(rho, curv)
        iterate = iterate + scaled(alpha, search)
        remain = remain - scaled(alpha, image)
        if step + 1 < ITERS:
            rho_next = reduce_forms(bilinear_terms(remain, remain))
            beta = divide(rho_next, rho)
            search = remain + scaled(beta, search)
            rho = rho_next
    term = jnp.sum(scaled((weights[:, 0], weights[:, 1]), iterate), axis=0)
    width = psi.shape[3]
    total = lax.psum(term, "pole")
    return lax.dynamic_slice_in_dim(total, lax.axis_index("pole") * width, width, 3)


def solution(mesh):
    placed = (
        P(None, "tile", None, "pole"),
        P("tile", None, "pole"),
        P("pole", None),
        P("pole", None),
    )
    return jax.shard_map(
        on_device,
        mesh=mesh,
        in_specs=placed,
        out_specs=P(None, "tile", None, "pole"),
        check_vma=False,
    )
```

profile of v0, /device:TPU:1, one launch (start us, length us, event | category | flops | bytes accessed | tf_op | source)
XLA Modules:
  0.0 709.7 jit_solution(12410667322798381919)
XLA Ops:
  6.5 0.7 all-gather.3.cloned.1.call-update
  7.3 1.9 bitcast_add_fusion.2
  9.2 1.0 slice_reduce_fusion.2
  10.2 31.5 %all-gather.3.cloned.1.call-done = f32[2,32,16,512]{3,2,1,0:T(8,128)} async-done(((f32[2,32,16,128]{3,2,1,0:T(8,128)}), f32[2,32,16,512]{3,2,1,0:T(8,128)}) %all-gather.3.cloned.1.call-update) | async-done | bytes 2097168 | tf_op jit(solution)/shard_map/all_gather | solution.py:87
  41.7 1.0 slice_bitcast_fusion.3
  42.7 1.3 collective-permute-start.1
  44.0 4.0 collective-permute-start
  48.0 2.8 slice_bitcast_fusion.1
  50.8 0.9 multiply_reduce_fusion.2
  52.3 0.9 pad_maximum_fusion
  53.2 1.5 pad.20
  55.2 8.3 %multiply_add_fusion.2 = (f32[2,2,34,16,512]{4,3,2,0,1:T(8,128)}, f32[2,2,34,16,512]{4,3,2,0,1:T(8,128)}, f32[2,2,34,16,512]{4,3,2,0,1:T(8,128)}) fusion(f32[2,2,1,16,512]{4,3,2,0,1:T(8,128)S(1)} %collective-permute-done.1, f32[2,2,32,16,512]{4,3,2,0,1:T(8,128)S(1)} %broadcast_in_dim.44, f32[2,2,1,16,512]{4,3,2,0,1:T(8,128)S(1)} %collective-permute-done, ...), kind=kLoop, calls=%fused_computation.41 | loop fusion | flops 14483456 | bytes 32309248 | tf_op jit(solution)/shard_map/add | solution.py:46
  63.5 1.2 all-gather.5.cloned.1.call-done
  64.7 9.0 %fusion.27 = f32[2,2,32,16,512]{4,3,2,0,1:T(8,128)S(1)} fusion(f32[2,2,34,16,512]{4,3,2,0,1:T(8,128)} %get-tuple-element.42, f32[2,2,34,16,512]{4,3,2,0,1:T(8,128)} %get-tuple-element.44, f32[2,2,34,16,512]{4,3,2,0,1:T(8,128)} %get-tuple-element.43, f32[2,2,34,16,512]{4,3,2,0,1:T(8,128)} %copy-done.11, f32[32,16,512]{2,1,0:T(8,128)} %all-gather.5.cloned.1.call-done, ...), kind=kLoop, calls=%fused_computation.62 | loop fusion | flops 10485760 | bytes 28311552 | tf_op jit(solution)/shard_map/add | solution.py:52
  73.7 1.9 copy-done.14
  75.7 2.0 subtract_reduce_fusion.2
  77.7 0.6 reduce_sum.122
  78.3 0.6 reduce_sum.125
  79.0 83.1 %all-reduce.10 = (f32[2]{0:T(128)S(1)}, f32[2]{0:T(128)S(1)}, f32[2]{0:T(128)S(1)}, f32[2]{0:T(128)S(1)}) all-reduce(f32[2]{0:T(128)S(1)} %reduce_sum.122, f32[2]{0:T(128)S(1)} %get-tuple-element.10, f32[2]{0:T(128)S(1)} %reduce_sum.125, f32[2]{0:T(128)S(1)} %get-tuple-element.9), channel_id=1, replica_groups=mesh['pole'=4,'tile'=32] {'tile'}, use_global_device_ids=true, to_apply=%region_1.0 | all-reduce | flops 8 | bytes 64 | tf_op jit(solution)/shard_map/psum | solution.py:93
  162.1 4.7 multiply_subtract_fusion.5
  166.7 1.0 maximum_subtract_fusion
  167.7 0.9 copy-done.5
  168.7 0.8 multiply_reduce_fusion.1
  169.5 85.7 %all-reduce.9 = (f32[2]{0:T(128)S(1)}, f32[2]{0:T(128)S(1)}) all-reduce(f32[2]{0:T(128)S(1)} %get-tuple-element.14, f32[2]{0:T(128)S(1)} %get-tuple-element.13), channel_id=1, replica_groups=mesh['pole'=4,'tile'=32] {'tile'}, use_global_device_ids=true, to_apply=%region_9.10 | all-reduce | flops 4 | bytes 32 | tf_op jit(solution)/shard_map/psum | solution.py:93
  255.2 2.0 multiply_subtract_fusion.4
  257.7 1.5 maximum_add_fusion.1
  259.2 0.6 copy-done.15
  260.3 1.3 collective-permute-start.3
  261.6 4.2 collective-permute-start.2
  266.2 1.5 collective-permute-done.2
  267.7 0.6 pad_maximum_fusion.1
  268.2 2.0 copy-done.12
  270.3 1.5 pad.22
  271.8 8.2 %multiply_add_fusion.1 = (f32[2,2,34,16,512]{4,3,2,0,1:T(8,128)}, f32[2,2,34,16,512]{4,3,2,0,1:T(8,128)}, f32[2,2,34,16,512]{4,3,2,0,1:T(8,128)}) fusion(f32[2,2,1,16,512]{4,3,2,0,1:T(8,128)S(1)} %collective-permute-done.3, f32[2,2,32,16,512]{4,3,2,0,1:T(8,128)S(1)} %maximum_add_fusion.1, f32[2,2,1,16,512]{4,3,2,0,1:T(8,128)S(1)} %collective-permute-done.2, ...), kind=kLoop, calls=%fused_computation.40 | loop fusion | flops 14483456 | bytes 32309248 | tf_op jit(solution)/shard_map/add | solution.py:46
  280.0 10.3 %fusion.23 = f32[2,2,32,16,512]{4,3,2,0,1:T(8,128)S(1)} fusion(f32[2,2,34,16,512]{4,3,2,0,1:T(8,128)} %get-tuple-element.39, f32[2,2,34,16,512]{4,3,2,0,1:T(8,128)} %get-tuple-element.41, f32[2,2,34,16,512]{4,3,2,0,1:T(8,128)} %get-tuple-element.40, f32[2,2,34,16,512]{4,3,2,0,1:T(8,128)} %copy-done.12, f32[32,16,512]{2,1,0:T(8,128)S(1)} %copy-done.21, ...), kind=kLoop, calls=%fused_computation.53 | loop fusion | flops 14680064 | bytes 36700160 | tf_op jit(solution)/shard_map/add | solution.py:52
  290.3 2.1 fusion.45
  292.4 76.8 %all-reduce.8 = (f32[2]{0:T(128)S(1)}, f32[2]{0:T(128)S(1)}) all-reduce(f32[2]{0:T(128)S(1)} %get-tuple-element.8, f32[2]{0:T(128)S(1)} %get-tuple-element.7), channel_id=1, replica_groups=mesh['pole'=4,'tile'=32] {'tile'}, use_global_device_ids=true, to_apply=%region_15.16 | all-reduce | flops 4 | bytes 32 | tf_op jit(solution)/shard_map/psum | solution.py:93
  369.3 4.4 multiply_subtract_fusion.3
  373.7 0.6 multiply_add_fusion.5
  374.3 1.0 copy-done.7
  375.3 0.6 copy-done.10
  375.9 0.6 copy-done.22
  376.6 3.9 maximum_add_fusion
  380.4 1.9 copy-done.3
  382.4 0.8 multiply_reduce_fusion
  383.2 74.9 %all-reduce.7 = (f32[2]{0:T(128)S(1)}, f32[2]{0:T(128)S(1)}) all-reduce(f32[2]{0:T(128)S(1)} %get-tuple-element.12, f32[2]{0:T(128)S(1)} %get-tuple-element.11), channel_id=1, replica_groups=mesh['pole'=4,'tile'=32] {'tile'}, use_global_device_ids=true, to_apply=%region_17.18 | all-reduce | flops 4 | bytes 32 | tf_op jit(solution)/shard_map/psum | solution.py:93
  458.1 3.0 multiply_subtract_fusion.1
  461.6 1.1 maximum_add_fusion.2
  462.6 0.7 copy-done.18
  463.4 1.3 collective-permute-start.5
  464.7 4.2 collective-permute-start.4
  469.5 1.2 collective-permute-done.4
  470.7 0.9 pad_maximum_fusion.2
  471.6 1.5 pad.24
  473.1 8.3 %multiply_add_fusion = (f32[2,2,34,16,512]{4,3,2,0,1:T(8,128)}, f32[2,2,34,16,512]{4,3,2,0,1:T(8,128)}, f32[2,2,34,16,512]{4,3,2,0,1:T(8,128)}) fusion(f32[2,2,1,16,512]{4,3,2,0,1:T(8,128)S(1)} %collective-permute-done.5, f32[2,2,32,16,512]{4,3,2,0,1:T(8,128)S(1)} %maximum_add_fusion.2, f32[2,2,1,16,512]{4,3,2,0,1:T(8,128)S(1)} %collective-permute-done.4, ...), kind=kLoop, calls=%fused_computation.39 | loop fusion | flops 14483456 | bytes 32309248 | tf_op jit(solution)/shard_map/add | solution.py:46
  481.4 9.3 %fusion.19 = f32[2,2,32,16,512]{4,3,2,0,1:T(8,128)S(1)} fusion(f32[2,2,34,16,512]{4,3,2,0,1:T(8,128)} %get-tuple-element.33, f32[2,2,34,16,512]{4,3,2,0,1:T(8,128)} %get-tuple-element.35, f32[2,2,34,16,512]{4,3,2,0,1:T(8,128)} %get-tuple-element.34, f32[2,2,34,16,512]{4,3,2,0,1:T(8,128)S(1)} %pad_maximum_fusion.2, ...), kind=kLoop, calls=%fused_computation.44 | loop fusion | flops 12582912 | bytes 34603008 | tf_op jit(solution)/shard_map/add | solution.py:52
  490.7 2.1 fusion.37
  492.9 77.0 %all-reduce.6 = (f32[2]{0:T(128)S(1)}, f32[2]{0:T(128)S(1)}) all-reduce(f32[2]{0:T(128)S(1)} %get-tuple-element.6, f32[2]{0:T(128)S(1)} %get-tuple-element.5), channel_id=1, replica_groups=mesh['pole'=4,'tile'=32] {'tile'}, use_global_device_ids=true, to_apply=%region_23.24 | all-reduce | flops 4 | bytes 32 | tf_op jit(solution)/shard_map/psum | solution.py:93
  569.9 3.0 fusion.41
  573.4 1.5 maximum_add_fusion.3
  574.8 0.7 multiply_subtract_fusion
  575.5 1.8 maximum_reduce_fusion
  577.4 123.5 %all-reduce.13.cloned.1.call-done = f32[2,32,16,512]{3,2,1,0:T(8,128)} async-done(((f32[2,32,16,512]{3,2,1,0:T(8,128)}), f32[2,32,16,512]{3,2,1,0:T(8,128)}) %all-reduce.13.cloned.1.call-update) | async-done | bytes 2097168 | tf_op jit(solution)/shard_map/psum | solution.py:119
  700.9 1.9 constant_dynamic-slice_fusion
  (61 shorter events, 4.2 us)
Async XLA Ops:
  6.5 35.1 %all-gather.3.cloned.1.call-start = ((), (), s32[]{:S(2)}) async-start(), calls=%async_computation | async-start | bytes 2621440 | tf_op jit(solution)/shard_map/all_gather | solution.py:87
  7.3 57.5 %all-gather.5.cloned.1.call-start = ((), (), s32[]{:S(2)}) async-start(), calls=%async_computation.1 | async-start | bytes 1310720 | tf_op jit(solution)/shard_map/all_gather | solution.py:88
  9.2 691.7 %all-reduce.13.cloned.1.call-start = ((), (), s32[]{:S(2)}) async-start(), calls=%async_computation.2 | async-start | bytes 4194304 | tf_op jit(solution)/shard_map/psum | solution.py:119
  41.7 9.2 %copy-start.1 = (f32[2,32,16,512]{3,2,1,0:T(8,128)S(1)}, f32[2,32,16,512]{3,2,1,0:T(8,128)}, u32[]{:S(2)}) copy-start(f32[2,32,16,512]{3,2,1,0:T(8,128)} %all-gather.3.cloned.1.call-done) | copy-start | bytes 6291460
  42.7 9.1 %collective-permute-start.1 = (f32[2,2,1,16,512]{4,3,2,0,1:T(8,128)S(1)}, f32[2,2,1,16,512]{4,3,2,0,1:T(8,128)S(1)}, u32[]{:S(2)}, u32[]{:S(2)}) collective-permute-start(f32[2,2,1,16,512]{4,3,2,0,1:T(8,128)S(1)} %broadcast_in_dim.45), channel_id=1, source_target_pairs={{1,0},{2,1},{3,2},{4,3},{5,4},{6,5},{7,6},{8,7},{9,8},{10,9},{11,1... | collective-permute-start | bytes 393224 | tf_op jit(solution)/shard_map/ppermute | solution.py:25
  44.0 7.7 %collective-permute-start = (f32[2,2,1,16,512]{4,3,2,0,1:T(8,128)S(1)}, f32[2,2,1,16,512]{4,3,2,0,1:T(8,128)S(1)}, u32[]{:S(2)}, u32[]{:S(2)}) collective-permute-start(f32[2,2,1,16,512]{4,3,2,0,1:T(8,128)S(1)} %broadcast_in_dim.43), channel_id=1, source_target_pairs={{0,1},{1,2},{2,3},{3,4},{4,5},{5,6},{6,7},{7,8},{8,9},{9,10},{10,1... | collective-permute-start | bytes 393224 | tf_op jit(solution)/shard_map/ppermute | solution.py:24
  53.2 2.0 copy-start.11
  64.7 10.9 %copy-start.20 = (f32[32,16,512]{2,1,0:T(8,128)S(1)}, f32[32,16,512]{2,1,0:T(8,128)}, u32[]{:S(2)}) copy-start(f32[32,16,512]{2,1,0:T(8,128)} %get-tuple-element.67) | copy-start | bytes 3145732
  73.7 1.9 copy-start.14
  166.7 1.8 copy-start.5
  166.7 2.0 copy-start.8
  255.2 2.1 copy-start.6
  255.2 2.5 copy-start.9
  257.2 2.6 copy-start.15
  257.2 3.0 copy-start.16
  260.3 30.0 %copy-start = (f32[2,2,32,16,512]{4,3,2,0,1:T(8,128)}, f32[2,2,32,16,512]{4,3,2,0,1:T(8,128)S(1)}, u32[]{:S(2)}) copy-start(f32[2,2,32,16,512]{4,3,2,0,1:T(8,128)S(1)} %maximum_add_fusion.1) | copy-start | bytes 12582916
  260.3 5.9 collective-permute-start.3
  261.6 6.1 collective-permute-start.2
  268.2 2.0 copy-start.12
  271.8 8.2 %copy-start.21 = (f32[32,16,512]{2,1,0:T(8,128)S(1)}, f32[32,16,512]{2,1,0:T(8,128)}, u32[]{:S(2)}) copy-start(f32[32,16,512]{2,1,0:T(8,128)} %all-gather.5.cloned.1.call-done) | copy-start | bytes 3145732
  290.3 2.2 copy-start.13
  369.3 5.0 copy-start.23
  373.7 1.6 copy-start.7
  373.7 2.2 copy-start.10
  373.7 2.8 copy-start.22
  380.4 1.9 copy-start.3
  458.1 3.5 copy-start.4
  461.1 1.5 copy-start.17
  461.2 2.2 copy-start.18
  461.5 7.4 %copy-start.24 = (f32[2,2]{1,0:T(2,128)S(1)}, f32[2,2]{1,0:T(2,128)}, u32[]{:S(2)}) copy-start(f32[2,2]{1,0:T(2,128)} %param.7) | copy-start | bytes 52
  463.4 27.4 %copy-start.2 = (f32[2,2,32,16,512]{4,3,2,0,1:T(8,128)}, f32[2,2,32,16,512]{4,3,2,0,1:T(8,128)S(1)}, u32[]{:S(2)}) copy-start(f32[2,2,32,16,512]{4,3,2,0,1:T(8,128)S(1)} %maximum_add_fusion.2) | copy-start | bytes 12582916
  463.4 6.1 collective-permute-start.5
  464.7 6.0 collective-permute-start.4
  569.9 3.5 copy-start.19
Sparse Core Ops, SparseCore 0:
  9.0 32.6 all-gather.2
  43.3 21.3 all-gather.4
  577.5 123.3 all-reduce.12
where the time goes:
time: 718 us; the launch traced here: 710 us
  blocking collectives  398 us (55%)
  waiting for transfers between devices  160 us (22%)
  other arithmetic  95.6 us (13%)
  local copies, waits for them, and re-layouts  25.9 us (4%)
  starting transfers between devices  16.3 us (2%)
  between operations  13.9 us (2%)
    psum x5, blocking collectives, reduce_forms(): return lax.psum((values[0], values[1]), 'tile')  398 us
    psum x1, waiting for transfers between devices, on_device(): total = lax.psum(term, 'pole')  124 us
    all_gather x1, waiting for transfers between devices, on_device(): lax.all_gather(psi, 'pole', axis=3, tiled=True)  31.5 us
    add x3, other arithmetic, operate(): kinetic = -0.5 * laplace(extended) + potential * current  28.6 us
    add x3, other arithmetic, laplace(): WEIGHT_FACE * centre + WEIGHT_EDGE * edges + WEIGHT_CORNER * corners  24.8 us
    sub x6, other arithmetic, scaled(): coef_re * vector[:, 0] - coef_im * vector[:, 1]  17.9 us
  transfers between devices with their start and end apart: 9, of which 7 were waited for; matrix products, arithmetic and copies ran while one was open for 3% of the time, Pallas kernels for 0%

commit v1 on v0

v1 whole, which is shorter than its diff:
```python
import functools

import jax
import jax.numpy as jnp
from jax import lax
from jax.experimental import pallas as pl
from jax.experimental.pallas import tpu as pltpu
from jax.sharding import PartitionSpec as P

COUPLING = 0.5
TIME_STEP = 0.25
SIGMA = 3.0
HALO = 3
K = -0.5 / 30.0
DIAGONAL = -128.0 * K - SIGMA
MOMENTS = 6
SHIFT_LANE, WEIGHT_LANE = 16, 48
VMEM = pl.BlockSpec(memory_space=pltpu.VMEM)
SMEM = pl.BlockSpec(memory_space=pltpu.SMEM)


def lanes(shape):
    return lax.broadcasted_iota(jnp.int32, shape, len(shape) - 1)


def pack_kernel(psi_ref, trap_ref, packed_ref):
    depth = psi_ref.shape[2]
    group = lanes((depth, 128)) // 8
    for half in range(2):
        packs = [jnp.zeros((depth, 128), jnp.float32)] * 3
        for g in range(16):
            row = half * 16 + g
            re, im = psi_ref[0, row], psi_ref[1, row]
            diag = trap_ref[row] + COUPLING * (re * re + im * im) + DIAGONAL
            for f, field in enumerate((re, im, diag)):
                moved = pltpu.roll(field, (8 * g + HALO) % 128, 1)
                packs[f] = jnp.where(group == g, moved, packs[f])
        for f in range(3):
            packed_ref[f, half] = packs[f]


def merged(where_ref, y1_ref, y2_ref, f, half):
    odd = lax.rem(where_ref[1], 2)
    left = (lanes(y1_ref.shape[2:]) % 8 < HALO).astype(jnp.int32)
    return jnp.where(left == odd, y1_ref[f, half], y2_ref[f, half])


def spread(pack, g):
    return pltpu.roll(pack, (128 - HALO - 8 * g) % 128, 1)


def edge_kernel(where_ref, psi_ref, trap_ref, y1_ref, y2_ref, s1_ref, s2_ref):
    rows = psi_ref.shape[1]
    even = lax.rem(where_ref[0], 2) == 0
    for f in range(3):
        for i in range(HALO):
            ends = []
            for row in (i, rows - HALO + i):
                re, im = psi_ref[0, row], psi_ref[1, row]
                own = (re, im, trap_ref[row] + COUPLING * (re * re + im * im) + DIAGONAL)[f]
                side = spread(merged(where_ref, y1_ref, y2_ref, f, row // 16), row % 16)
                ends.append(jnp.concatenate([own, side], axis=1))
            s1_ref[f, i] = jnp.where(even, ends[1], ends[0])
            s2_ref[f, i] = jnp.where(even, ends[0], ends[1])


def neighbours_z(b, first, last):
    depth = b.shape[0]
    return jnp.where(first, 0.0, pltpu.roll(b, 1, 0)) + jnp.where(last, 0.0, pltpu.roll(b, depth - 1, 0))


def products(a, b):
    return a[0] * b[0] - a[1] * b[1], a[0] * b[1] + a[1] * b[0]


def apply_kernel(
    where_ref, shift_ref, weight_ref, psi_ref, trap_ref, y1_ref, y2_ref, x1_ref, x2_ref,
    u1_ref, u2_ref, out_ref, field, first_power, second_power,
):
    rows, depth = psi_ref.shape[1:3]
    tile, pole = where_ref[0], where_ref[1]
    tiles, poles = where_ref[2], where_ref[3]
    even = lax.rem(tile, 2) == 0
    for half in range(2):
        packs = [merged(where_ref, y1_ref, y2_ref, f, half) for f in range(3)]
        for g in range(16):
            row = half * 16 + g
            re, im = psi_ref[0, row], psi_ref[1, row]
            diag = trap_ref[row] + COUPLING * (re * re + im * im) + DIAGONAL
            for f, own in enumerate((re, im, diag)):
                field[f, HALO + row, :, 0:128] = own
                field[f, HALO + row, :, 128:256] = spread(packs[f], g)
    for f in range(3):
        for i in range(HALO):
            x1, x2 = x1_ref[f, i], x2_ref[f, i]
            field[f, i] = jnp.where(even, x2, x1)
            field[f, HALO + rows + i] = jnp.where(even, x1, x2)

    z = lax.broadcasted_iota(jnp.int32, (depth, 256), 0)
    first, last = z == 0, z == depth - 1
    lane = lanes((depth, 128))
    inside = jnp.where(lane < 64, (pole < poles - 1).astype(jnp.float32), (pole > 0).astype(jnp.float32))

    def image(source, x):
        diag = field[2, x]
        result = []
        for c in range(2):
            v = source[c, x]
            s = source[c, x - 1] + source[c, x + 1]
            p = (3.0 * K) * v + K * s
            e = 3.0 * p + (5.0 * K) * v
            w = e + neighbours_z(p, first, last)
            flat = diag * v + (14.0 * K) * s + neighbours_z(e, first, last)
            total = flat + pltpu.roll(w, 1, 1) + pltpu.roll(w, 255, 1)
            result.append(jnp.concatenate([total[:, :128], total[:, 128:] * inside], axis=1))
        return result

    def fold(a):
        return a[0:8] + a[8:16]

    def sweep(source, target, reach):
        for start, there in ((HALO - reach, tile > 0), (HALO + rows, tile < tiles - 1)):
            keep = there.astype(jnp.float32)
            for i in range(reach):
                for c, value in enumerate(image(source, start + i)):
                    target[c, start + i] = value * keep

        def step(i, sums):
            x = HALO + i
            new = image(source, x)
            if target is not None:
                for c in range(2):
                    target[c, x] = new[c]
            old = [source[c, x, :, 0:128] for c in range(2)]
            new = [a[:, 0:128] for a in new]
            forms = products(old, old) + products(old, new)
            return tuple(a + fold(b) for a, b in zip(sums, forms))

        zero = jnp.zeros((8, 128), jnp.float32)
        return lax.fori_loop(0, rows, step, (zero,) * 4, unroll=2)

    sums = sweep(field, first_power, 2)
    sums += sweep(first_power, second_power, 1)
    sums += sweep(second_power, None, 0)
    for c in range(2):
        u1_ref[c] = first_power[c, HALO:HALO + rows, :, 0:128]
        u2_ref[c] = second_power[c, HALO:HALO + rows, :, 0:128]

    at = lanes((1, 128))
    line = jnp.zeros((1, 128), jnp.float32)
    for j, part in enumerate(sums):
        line = jnp.where(at == j, jnp.sum(part, keepdims=True), line)
    mine = shift_ref.shape[0]
    for i in range(mine):
        for c in range(2):
            for base, ref in ((SHIFT_LANE, shift_ref), (WEIGHT_LANE, weight_ref)):
                here = (at == base + 16 * c + mine * pole + i) & (tile == 0)
                line = jnp.where(here, ref[i, c], line)
    out_ref[...] = jnp.broadcast_to(line, out_ref.shape)


def mul(a, b):
    return a[0] * b[0] - a[1] * b[1], a[0] * b[1] + a[1] * b[0]


def add(a, b):
    return a[0] + b[0], a[1] + b[1]


def sub(a, b):
    return a[0] - b[0], a[1] - b[1]


def div(a, b):
    size = jnp.maximum(jnp.abs(b[0]), jnp.abs(b[1]))
    inverse = jnp.where(size > 0.0, 1.0 / size, 0.0)
    b = (b[0] * inverse, b[1] * inverse)
    norm = b[0] * b[0] + b[1] * b[1]
    factor = jnp.where(size > 0.0, inverse / norm, 0.0)
    return (a[0] * b[0] + a[1] * b[1]) * factor, (a[1] * b[0] - a[0] * b[1]) * factor


def coefficients(line, poles):
    at = lanes((1, 128))

    def spot(j):
        return jnp.sum(jnp.where(at == j, line, 0.0), axis=1, keepdims=True) + jnp.zeros((1, 128), jnp.float32)

    m = [(spot(2 * j), spot(2 * j + 1)) for j in range(MOMENTS)]
    shift = tuple(pltpu.roll(line, (128 - SHIFT_LANE - 16 * c) % 128, 1) for c in range(2))
    weight = tuple(pltpu.roll(line, (128 - WEIGHT_LANE - 16 * c) % 128, 1) for c in range(2))
    mean = div(m[1], m[0])
    rest = list(m)
    for level in range(1, MOMENTS):
        for j in range(MOMENTS - 1, level - 1, -1):
            rest[j] = sub(rest[j], mul(mean, rest[j - 1]))
    c0, c2, c3, c4, c5 = rest[0], rest[2], rest[3], rest[4], rest[5]
    b1, e1 = div(c2, c0), div(c3, c2)
    d2 = sub(sub(c4, mul(e1, c3)), mul(b1, c2))
    b2 = div(d2, c2)
    e2 = div(sub(sub(sub(c5, mul(e1, c4)), mul(b1, c3)), mul(e1, d2)), d2)
    base = add((shift[1] / TIME_STEP + SIGMA, -shift[0] / TIME_STEP), mean)
    g2 = add(base, e2)
    g1 = sub(add(base, e1), div(b2, g2))
    y0 = div((jnp.zeros_like(line), jnp.full_like(line, -1.0 / TIME_STEP)), sub(base, div(b1, g1)))
    y1 = div((-y0[0], -y0[1]), g1)
    y2 = div((-y1[0], -y1[1]), g2)
    k1 = sub(y1, mul(e1, y2))
    k0 = sub(y0, mul(b1, y2))
    k0 = add(sub(k0, mul(mean, k1)), mul(mul(mean, mean), y2))
    twice = mul(mean, y2)
    k1 = sub(k1, (2.0 * twice[0], 2.0 * twice[1]))
    found = []
    for k in (k0, k1, y2):
        term = mul(weight, k)
        found.append(tuple(jnp.sum(jnp.where(at < poles, part, 0.0), axis=1, keepdims=True) for part in term))
    return found


def combine_kernel(poles, psi_ref, u1_ref, u2_ref, sums_ref, out_ref):
    line = jnp.sum(sums_ref[...], axis=0, keepdims=True)
    k = coefficients(line, poles)
    rows = psi_ref.shape[1]
    k = [tuple(jnp.broadcast_to(part, (8, 128)) for part in pair) for pair in k]
    for i in range(rows):
        for h in range(psi_ref.shape[2] // 8):
            at = slice(8 * h, 8 * h + 8)
            total = None
            for pair, ref in zip(k, (psi_ref, u1_ref, u2_ref)):
                term = mul(pair, (ref[0, i, at], ref[1, i, at]))
                total = term if total is None else add(total, term)
            out_ref[0, i, at] = total[0]
            out_ref[1, i, at] = total[1]


def call(kernel, out_shape, specs, scratch=(), flops=0, bytes_accessed=0):
    return pl.pallas_call(
        kernel,
        out_shape=out_shape,
        in_specs=specs,
        out_specs=jax.tree.map(lambda _: VMEM, out_shape),
        scratch_shapes=list(scratch),
        compiler_params=pltpu.CompilerParams(vmem_limit_bytes=40 * 2**20),
        cost_estimate=pl.CostEstimate(flops=flops, bytes_accessed=bytes_accessed, transcendentals=0),
    )


def on_device(psi, trap, pole_shift, pole_weight):
    tiles, poles = lax.axis_size("tile"), lax.axis_size("pole")
    rows, depth, width = trap.shape
    f32 = functools.partial(jax.ShapeDtypeStruct, dtype=jnp.float32)
    where = jnp.stack([lax.axis_index("tile"), lax.axis_index("pole"), tiles, poles]).astype(jnp.int32)

    packed = call(pack_kernel, f32((3, 2, depth, 128)), [VMEM] * 2)(psi, trap)
    pairs = [(i, i ^ 1) for i in range(poles)]
    gaps = [(i, i + 1) for i in range(1, poles - 1, 2)]
    y2 = lax.ppermute(packed, "pole", gaps + [(b, a) for a, b in gaps])
    y1 = lax.ppermute(packed, "pole", pairs)

    edge = f32((3, HALO, depth, 256))
    s1, s2 = call(edge_kernel, (edge, edge), [SMEM] + [VMEM] * 4)(where, psi, trap, y1, y2)
    pairs = [(i, i ^ 1) for i in range(tiles)]
    gaps = [(i, i + 1) for i in range(1, tiles - 1, 2)]
    x2 = lax.ppermute(s2, "tile", gaps + [(b, a) for a, b in gaps])
    x1 = lax.ppermute(s1, "tile", pairs)

    devices = tiles * poles
    grown = pltpu.VMEM((3, rows + 2 * HALO, depth, 256), jnp.float32)
    power = pltpu.VMEM((2, rows + 2 * HALO, depth, 256), jnp.float32)
    u1, u2, line = call(
        apply_kernel,
        (f32(psi.shape), f32(psi.shape), f32((devices, 128))),
        [SMEM] * 3 + [VMEM] * 6,
        [grown, power, power],
    )(where, pole_shift, pole_weight, psi, trap, y1, y2, x1, x2)

    lines = lax.all_to_all(line.reshape(devices, 1, 128), ("pole", "tile"), 0, 0, tiled=True)
    combine = functools.partial(combine_kernel, pole_shift.shape[0] * poles)
    return call(combine, f32(psi.shape), [VMEM] * 4)(psi, u1, u2, lines.reshape(devices, 128))


def solution(mesh):
    placed = (
        P(None, "tile", None, "pole"),
        P("tile", None, "pole"),
        P("pole", None),
        P("pole", None),
    )
    return jax.shard_map(
        on_device,
        mesh=mesh,
        in_specs=placed,
        out_specs=P(None, "tile", None, "pole"),
        check_vma=False,
    )
```

time: 718 us -> 50 us (0.07); the launches traced: 710 us -> 49.7 us
  blocking collectives: 398 us -> 26.1 us
  waiting for transfers between devices: 160 us -> 5.3 us
  other arithmetic: 95.6 us -> 0.08 us
  local copies, waits for them, and re-layouts: 25.9 us -> 2.01 us
  between operations: 13.9 us -> 0.08 us
  starting transfers between devices: 16.3 us -> 6.97 us
  Pallas kernels: 0 us -> 9.24 us
    psum x5 -> x0, blocking collectives: 398 us -> none  [reduce_forms(): return lax.psum((values[0], values[1]), 'tile')]
    psum x1 -> x0, waiting for transfers between devices: 124 us -> none  [on_device(): total = lax.psum(term, 'pole')]
    add x12 -> x0, other arithmetic: 63.8 us -> none  [the longest x3 28.6 us: operate(): kinetic = -0.5 * laplace(extended) + potential * current]
    all_gather x2 -> x0, waiting for transfers between devices: 32.7 us -> none  [the longest x1 31.5 us: on_device(): lax.all_gather(psi, 'pole', axis=3, tiled=True)]
    all_to_all x0 -> x1, blocking collectives: none -> 26.1 us  [on_device(): lax.all_to_all(line.reshape(devices, 1, 128), ('pole', 'tile'), 0, 0, til...]
    sub x7 -> x0, other arithmetic: 18.8 us -> none  [the longest x6 17.9 us: scaled(): coef_re * vector[:, 0] - coef_im * vector[:, 1]]
    unnamed x50 -> x12, local copies, waits for them, and re-layouts: 12.7 us -> 2.01 us
    reduce_sum x7 -> x0, other arithmetic: 10.6 us -> none  [the longest x3 6.28 us: bilinear_terms(): jnp.sum(left[:, 0] * right[:, 0] - left[:, 1] * right[:, 1], axis=(1, 2, 3))]
  transfers between devices with their start and end apart: 9 -> 4, of which waited for: 7 -> 2; matrix products, arithmetic and copies ran while one was open for 3% -> 0% of each run, Pallas kernels for 0% -> 0%
where the time goes in v1:
time: 50 us; the launch traced here: 49.7 us
  blocking collectives  26.1 us (52%)
  Pallas kernels  9.24 us (18%)
  starting transfers between devices  6.97 us (14%)
  waiting for transfers between devices  5.3 us (11%)
  local copies, waits for them, and re-layouts  2.01 us (4%)
    all_to_all x1, blocking collectives, on_device(): lax.all_to_all(line.reshape(devices, 1, 128), ('pole', 'tile'), 0, 0, til...  26.1 us
    pallas_call x1, Pallas kernels, on_device(): call(apply_kernel, (f32(psi.shape), f32(psi.shape), f32((devices, 128))),...  7.02 us
    ppermute x1, starting transfers between devices, on_device(): y2 = lax.ppermute(packed, 'pole', gaps + [(b, a) for a, b in gaps])  4.51 us
    ppermute x1, waiting for transfers between devices, on_device(): x1 = lax.ppermute(s1, 'tile', pairs)  3.71 us
    unnamed x12, local copies, waits for them, and re-layouts  2.01 us
    ppermute x1, starting transfers between devices, on_device(): x1 = lax.ppermute(s1, 'tile', pairs)  1.72 us
    ppermute x1, waiting for transfers between devices, on_device(): y2 = lax.ppermute(packed, 'pole', gaps + [(b, a) for a, b in gaps])  1.58 us
    pallas_call x1, Pallas kernels, on_device(): call(combine, f32(psi.shape), [VMEM] * 4)  1.31 us
  transfers between devices with their start and end apart: 4, of which 2 were waited for; matrix products, arithmetic and copies ran while one was open for 0% of the time, Pallas kernels for 0%

profile of v1, /device:TPU:1, one launch (start us, length us, event | category | flops | bytes accessed | tf_op | source)
XLA Modules:
  0.0 49.7 jit_solution(6653367517745647095)
XLA Ops:
  0.0 0.0 copy-start
  0.0 1.0 %copy-done = f32[2,32,16,128]{3,2,1,0:T(8,128)S(1)} copy-done((f32[2,32,16,128]{3,2,1,0:T(8,128)S(1)}, f32[2,32,16,128]{3,2,1,0:T(8,128)}, u32[]{:S(2)}) %copy-start) | copy-done | bytes 524312
  1.0 0.0 copy-start.2
  1.0 0.9 %copy-done.2 = f32[32,16,128]{2,1,0:T(8,128)S(1)} copy-done((f32[32,16,128]{2,1,0:T(8,128)S(1)}, f32[32,16,128]{2,1,0:T(8,128)}, u32[]{:S(2)}) %copy-start.2) | copy-done | bytes 262168
  2.0 0.0 copy-start.1
  2.0 0.0 copy-start.3
  2.0 0.3 shard_map.46
  2.3 4.5 %collective-permute-start.1 = (f32[3,2,16,128]{3,2,1,0:T(8,128)S(1)}, f32[3,2,16,128]{3,2,1,0:T(8,128)S(1)}, u32[]{:S(2)}, u32[]{:S(2)}) collective-permute-start(f32[3,2,16,128]{3,2,1,0:T(8,128)S(1)} %shard_map.46), channel_id=1, source_target_pairs={{32,64},{64,32},{33,65},{65,33},{34,66},{66,34},{35,67},{67,35},{3... | collective-permute-start | bytes 147464 | tf_op jit(solution)/shard_map/ppermute | solution.py:257
  6.8 0.1 collective-permute-start
  6.9 0.1 pad_add_fusion.where_ref
  7.0 1.6 %collective-permute-done.1.y2_ref = f32[3,2,16,128]{3,2,1,0:T(8,128)S(1)} collective-permute-done((f32[3,2,16,128]{3,2,1,0:T(8,128)S(1)}, f32[3,2,16,128]{3,2,1,0:T(8,128)S(1)}, u32[]{:S(2)}, u32[]{:S(2)}) %collective-permute-start.1) | collective-permute-done | bytes 49184 | tf_op jit(solution)/shard_map/ppermute | solution.py:257
  8.5 0.0 collective-permute-done.y1_ref
  8.5 0.0 copy-done.1
  8.6 0.0 copy-done.3
  8.6 0.6 %shard_map.47 = (f32[3,3,16,256]{3,2,1,0:T(8,128)S(1)}, f32[3,3,16,256]{3,2,1,0:T(8,128)S(1)}) custom-call(s32[4]{0:T(128)S(1)} %pad_add_fusion.where_ref, f32[2,32,16,128]{3,2,1,0:T(8,128)S(1)} %copy-done.1, f32[32,16,128]{2,1,0:T(8,128)S(1)} %copy-done.3, f32[3,2,16,128]{3,2,1,0:T(8,128)S(1)} %collective-permute-done.y1_ref, ...), custom_call_target="tpu_custom_call" | custom-call | tf_op jit(solution)/shard_map/pallas_call | solution.py:261
  9.2 0.0 copy-start.5
  9.2 0.0 copy-start.4
  9.2 1.7 %collective-permute-start.2 = (f32[3,3,16,256]{3,2,1,0:T(8,128)S(1)}, f32[3,3,16,256]{3,2,1,0:T(8,128)S(1)}, u32[]{:S(2)}, u32[]{:S(2)}) collective-permute-start(f32[3,3,16,256]{3,2,1,0:T(8,128)S(1)} %get-tuple-element.10), channel_id=1, source_target_pairs={{0,1},{1,0},{2,3},{3,2},{4,5},{5,4},{6,7},{7,6},{8,9},{9,8},{10,11... | collective-permute-start | bytes 442376 | tf_op jit(solution)/shard_map/ppermute | solution.py:265
  11.0 0.7 %collective-permute-start.3 = (f32[3,3,16,256]{3,2,1,0:T(8,128)S(1)}, f32[3,3,16,256]{3,2,1,0:T(8,128)S(1)}, u32[]{:S(2)}, u32[]{:S(2)}) collective-permute-start(f32[3,3,16,256]{3,2,1,0:T(8,128)S(1)} %get-tuple-element.11), channel_id=1, source_target_pairs={{1,2},{3,4},{5,6},{7,8},{9,10},{11,12},{13,14},{15,16},{17,18},{19... | collective-permute-start | bytes 442376 | tf_op jit(solution)/shard_map/ppermute | solution.py:264
  11.6 3.7 %collective-permute-done.2.x1_ref = f32[3,3,16,256]{3,2,1,0:T(8,128)S(1)} collective-permute-done((f32[3,3,16,256]{3,2,1,0:T(8,128)S(1)}, f32[3,3,16,256]{3,2,1,0:T(8,128)S(1)}, u32[]{:S(2)}, u32[]{:S(2)}) %collective-permute-start.2) | collective-permute-done | bytes 147488 | tf_op jit(solution)/shard_map/ppermute | solution.py:265
  15.3 0.0 collective-permute-done.3.x2_ref
  15.3 0.0 copy-done.5
  15.3 0.0 copy-done.4
  15.3 7.0 %shard_map.48 = (f32[2,32,16,128]{3,2,1,0:T(8,128)S(1)}, f32[2,32,16,128]{3,2,1,0:T(8,128)S(1)}, f32[128,128]{1,0:T(8,128)S(1)}) custom-call(s32[4]{0:T(128)S(1)} %pad_add_fusion.where_ref, f32[2,2]{1,0:T(2,128)S(1)} %copy-done.4, f32[2,2]{1,0:T(2,128)S(1)} %copy-done.5, f32[2,32,16,128]{3,2,1,0:T(8,128)S(1)} %copy-done.1, f32[32,16,128]{2,1,0:T(8,128)S(1)} %copy-done.3, ...), custom_call_target="tpu_custom_call" | custom-call | tf_op jit(solution)/shard_map/pallas_call | solution.py:270
  22.4 26.1 %all_to_all.5 = f32[128,1,128]{2,1,0:T(1,128)S(1)} all-to-all(f32[128,1,128]{2,1,0:T(1,128)S(1)} %bitcast.7), channel_id=1, replica_groups=mesh['pole'=4,'tile'=32] {'pole','tile'}, dimensions={0} | all-to-all | bytes 131072 | tf_op jit(solution)/shard_map/all_to_all | solution.py:277
  48.4 1.3 %shard_map.49 = f32[2,32,16,128]{3,2,1,0:T(8,128)} custom-call(f32[2,32,16,128]{3,2,1,0:T(8,128)S(1)} %copy-done.1, f32[2,32,16,128]{3,2,1,0:T(8,128)S(1)} %get-tuple-element.12.u1_ref, f32[2,32,16,128]{3,2,1,0:T(8,128)S(1)} %get-tuple-element.13.u2_ref, f32[128,128]{1,0:T(8,128)S(1)} %bitcast.6), custom_call_target="tpu_custom_call" | custom-call | tf_op jit(solution)/shard_map/pallas_call | solution.py:279
Async XLA Ops:
  0.0 1.0 %copy-start = (f32[2,32,16,128]{3,2,1,0:T(8,128)S(1)}, f32[2,32,16,128]{3,2,1,0:T(8,128)}, u32[]{:S(2)}) copy-start(f32[2,32,16,128]{3,2,1,0:T(8,128)} %psi_ref.7) | copy-start | bytes 1572868
  1.0 0.9 %copy-start.2 = (f32[32,16,128]{2,1,0:T(8,128)S(1)}, f32[32,16,128]{2,1,0:T(8,128)}, u32[]{:S(2)}) copy-start(f32[32,16,128]{2,1,0:T(8,128)} %trap_ref.5) | copy-start | bytes 786436
  2.0 6.6 %copy-start.1 = (f32[2,32,16,128]{3,2,1,0:T(8,128)S(1)}, f32[2,32,16,128]{3,2,1,0:T(8,128)}, u32[]{:S(2)}) copy-start(f32[2,32,16,128]{3,2,1,0:T(8,128)} %psi_ref.7) | copy-start | bytes 1572868
  2.0 6.6 %copy-start.3 = (f32[32,16,128]{2,1,0:T(8,128)S(1)}, f32[32,16,128]{2,1,0:T(8,128)}, u32[]{:S(2)}) copy-start(f32[32,16,128]{2,1,0:T(8,128)} %trap_ref.5) | copy-start | bytes 786436
  2.3 6.3 %collective-permute-start.1 = (f32[3,2,16,128]{3,2,1,0:T(8,128)S(1)}, f32[3,2,16,128]{3,2,1,0:T(8,128)S(1)}, u32[]{:S(2)}, u32[]{:S(2)}) collective-permute-start(f32[3,2,16,128]{3,2,1,0:T(8,128)S(1)} %shard_map.46), channel_id=1, source_target_pairs={{32,64},{64,32},{33,65},{65,33},{34,66},{66,34},{35,67},{67,35},{3... | collective-permute-start | bytes 147464 | tf_op jit(solution)/shard_map/ppermute | solution.py:257
  6.8 1.8 %collective-permute-start = (f32[3,2,16,128]{3,2,1,0:T(8,128)S(1)}, f32[3,2,16,128]{3,2,1,0:T(8,128)S(1)}, u32[]{:S(2)}, u32[]{:S(2)}) collective-permute-start(f32[3,2,16,128]{3,2,1,0:T(8,128)S(1)} %shard_map.46), channel_id=1, source_target_pairs={{0,32},{32,0},{64,96},{96,64},{1,33},{33,1},{65,97},{97,65},{2,34}... | collective-permute-start | bytes 147464 | tf_op jit(solution)/shard_map/ppermute | solution.py:258
  9.2 6.1 %copy-start.5 = (f32[2,2]{1,0:T(2,128)S(1)}, f32[2,2]{1,0:T(2,128)}, u32[]{:S(2)}) copy-start(f32[2,2]{1,0:T(2,128)} %weight_ref.1) | copy-start | bytes 52
  9.2 6.1 %copy-start.4 = (f32[2,2]{1,0:T(2,128)S(1)}, f32[2,2]{1,0:T(2,128)}, u32[]{:S(2)}) copy-start(f32[2,2]{1,0:T(2,128)} %shift_ref.1) | copy-start | bytes 52
  9.2 6.1 %collective-permute-start.2 = (f32[3,3,16,256]{3,2,1,0:T(8,128)S(1)}, f32[3,3,16,256]{3,2,1,0:T(8,128)S(1)}, u32[]{:S(2)}, u32[]{:S(2)}) collective-permute-start(f32[3,3,16,256]{3,2,1,0:T(8,128)S(1)} %get-tuple-element.10), channel_id=1, source_target_pairs={{0,1},{1,0},{2,3},{3,2},{4,5},{5,4},{6,7},{7,6},{8,9},{9,8},{10,11... | collective-permute-start | bytes 442376 | tf_op jit(solution)/shard_map/ppermute | solution.py:265
  11.0 4.4 %collective-permute-start.3 = (f32[3,3,16,256]{3,2,1,0:T(8,128)S(1)}, f32[3,3,16,256]{3,2,1,0:T(8,128)S(1)}, u32[]{:S(2)}, u32[]{:S(2)}) collective-permute-start(f32[3,3,16,256]{3,2,1,0:T(8,128)S(1)} %get-tuple-element.11), channel_id=1, source_target_pairs={{1,2},{3,4},{5,6},{7,8},{9,10},{11,12},{13,14},{15,16},{17,18},{19... | collective-permute-start | bytes 442376 | tf_op jit(solution)/shard_map/ppermute | solution.py:264

commit v2 on v1

v2 whole, which is shorter than its diff:
```python
import functools

import jax
import jax.numpy as jnp
from jax import lax
from jax.experimental import pallas as pl
from jax.experimental.pallas import tpu as pltpu
from jax.sharding import PartitionSpec as P

COUPLING = 0.5
TIME_STEP = 0.25
SIGMA = 3.0
HALO = 3
K = -0.5 / 30.0
DIAGONAL = -128.0 * K - SIGMA
MOMENTS = 6
SHIFT_LANE, WEIGHT_LANE = 16, 48
VMEM = pl.BlockSpec(memory_space=pltpu.VMEM)


def lanes(shape):
    return lax.broadcasted_iota(jnp.int32, shape, len(shape) - 1)


def position():
    return lax.axis_index("tile"), lax.axis_index("pole")


def is_odd(index):
    return lax.rem(index, 2) == 1


def load_kernel(psi_ref, trap_ref, packed_ref, field_ref, sems):
    rows, depth = trap_ref.shape[:2]
    half_rows = rows // 2
    copies = []
    for half in range(2):
        at = pl.ds(half * half_rows, half_rows)
        pair = (
            pltpu.make_async_copy(psi_ref.at[:, at], field_ref.at[0:2, at], sems.at[half, 0]),
            pltpu.make_async_copy(trap_ref.at[at], field_ref.at[2, at], sems.at[half, 1]),
        )
        for copy in pair:
            copy.start()
        copies.append(pair)
    group = lanes((depth, 128)) // 8
    for half in range(2):
        for copy in copies[half]:
            copy.wait()
        packs = [jnp.zeros((depth, 128), jnp.float32)] * 3
        for g in range(half_rows):
            row = half * half_rows + g
            re, im = field_ref[0, row], field_ref[1, row]
            diag = field_ref[2, row] + COUPLING * (re * re + im * im) + DIAGONAL
            field_ref[2, row] = diag
            for f, field in enumerate((re, im, diag)):
                moved = pltpu.roll(field, (8 * g + HALO) % 128, 1)
                packs[f] = jnp.where(group == g, moved, packs[f])
        for f in range(3):
            packed_ref[f, half] = packs[f]


def merged(y1_ref, y2_ref, f, half):
    odd = is_odd(position()[1]).astype(jnp.int32)
    left = (lanes(y1_ref.shape[2:]) % 8 < HALO).astype(jnp.int32)
    return jnp.where(left == odd, y1_ref[f, half], y2_ref[f, half])


def spread(pack, g):
    return pltpu.roll(pack, (128 - HALO - 8 * g) % 128, 1)


def edge_items(rows, high):
    start = rows - HALO if high else 0
    skip = 1 if high else 0
    return [(f, start + i) for f in range(2) for i in range(HALO)] + [(2, start + skip + i) for i in range(HALO - 1)]


def edge_kernel(field_ref, y1_ref, y2_ref, s1_ref, s2_ref):
    rows, depth = field_ref.shape[1:3]
    even = jnp.logical_not(is_odd(position()[0]))
    group = lanes((depth, 128)) // 8
    ends = []
    for high in (False, True):
        items = edge_items(rows, high)
        sides = jnp.zeros((depth, 128), jnp.float32)
        for f, first in ((0, 0), (1, HALO), (2, 2 * HALO)):
            row = items[first][1]
            pack = merged(y1_ref, y2_ref, f, row // 16)
            moved = pltpu.roll(pack, (8 * (first - row)) % 128, 1)
            sides = jnp.where(group >= first, moved, sides)
        ends.append([field_ref[f, row] for f, row in items] + [sides])
    for i, (low, high) in enumerate(zip(*ends)):
        s1_ref[i] = jnp.where(even, high, low)
        s2_ref[i] = jnp.where(even, low, high)


def neighbours_z(b):
    depth = b.shape[0]
    z = lax.broadcasted_iota(jnp.int32, b.shape, 0)
    below = jnp.where(z == 0, 0.0, pltpu.roll(b, 1, 0))
    return below + jnp.where(z == depth - 1, 0.0, pltpu.roll(b, depth - 1, 0))


def inside_mask(depth):
    pole, poles = position()[1], lax.axis_size("pole")
    lane = lanes((depth, 128))
    return jnp.where(lane < 64, (pole < poles - 1).astype(jnp.float32), (pole > 0).astype(jnp.float32))


def image(before, v, after, diag, inside):
    s = before + after
    p = (3.0 * K) * v + K * s
    e = 3.0 * p + (5.0 * K) * v
    w = e + neighbours_z(p)
    flat = diag * v + (14.0 * K) * s + neighbours_z(e)
    total = flat + pltpu.roll(w, 1, 1) + pltpu.roll(w, 255, 1)
    return jnp.concatenate([total[:, :128], total[:, 128:] * inside], axis=1)


def fold(a):
    return a[0:8, 0:128] + a[8:16, 0:128]


def forms(a, b):
    return fold(a[0] * b[0] - a[1] * b[1]), fold(a[0] * b[1] + a[1] * b[0])


def inner_kernel(field_ref, y1_ref, y2_ref, grown_ref, u1_ref, u2_ref, sums_ref):
    rows, depth = field_ref.shape[1:3]
    for half in range(2):
        packs = [merged(y1_ref, y2_ref, f, half) for f in range(3)]
        for g in range(16):
            row = half * 16 + g
            for f in range(3):
                grown_ref[f, row, :, 0:128] = field_ref[f, row]
                grown_ref[f, row, :, 128:256] = spread(packs[f], g)
    inside = inside_mask(depth)

    def sweep(source, target, reach):
        def step(i, sums):
            x = reach + i
            old = [source[c, x] for c in range(2)]
            new = [image(source[c, x - 1], old[c], source[c, x + 1], grown_ref[2, x], inside) for c in range(2)]
            if target is not None:
                for c in range(2):
                    target[c, x] = new[c]
            return tuple(a + b for a, b in zip(sums, forms(old, old) + forms(old, new)))

        zero = jnp.zeros((8, 128), jnp.float32)
        return lax.fori_loop(0, rows - 2 * reach, step, (zero,) * 4, unroll=2)

    sums = sweep(grown_ref, u1_ref, 1) + sweep(u1_ref, u2_ref, 2) + sweep(u2_ref, None, 3)
    for j, part in enumerate(sums):
        sums_ref[j] = part


def outer_kernel(
    shift_ref, weight_ref, grown_ref, u1_ref, u2_ref, sums_ref, x1_ref, x2_ref, b1_ref, b2_ref, line_ref,
):
    rows, depth = grown_ref.shape[1:3]
    tile, pole = position()
    tiles = lax.axis_size("tile")
    even = jnp.logical_not(is_odd(tile))
    inside = inside_mask(depth)
    sums = [sums_ref[j] for j in range(2 * MOMENTS)]

    def count(j, parts):
        for i, part in enumerate(parts):
            sums[j + i] += part

    for high in (False, True):
        own = (lambda i: rows - 1 + HALO - i) if high else (lambda i: i - HALO)
        there = (tile < tiles - 1) if high else (tile > 0)
        keep = jnp.where(there, inside, 0.0)
        keep = jnp.concatenate([jnp.broadcast_to(there.astype(jnp.float32), inside.shape), keep], axis=1)
        ones = jnp.concatenate([jnp.ones_like(inside), inside], axis=1)
        near, far = (x1_ref, x2_ref) if high else (x2_ref, x1_ref)
        sides = jnp.where(even, near[8], far[8])
        v, diag = [{}, {}], {}
        for item, (f, row) in enumerate(edge_items(rows, not high)):
            value = jnp.concatenate([jnp.where(even, near[item], far[item]), spread(sides, item)], axis=1)
            place = HALO - 1 - row if high else row - (rows - HALO)
            if f < 2:
                v[f][place] = value
            else:
                diag[place] = value
        for i in range(HALO, 2 * HALO):
            for c in range(2):
                v[c][i] = grown_ref[c, own(i)]
            diag[i] = grown_ref[2, own(i)]

        def powers(source, first, last):
            return [
                {
                    i: image(source[c][i - 1], source[c][i], source[c][i + 1], diag[i], inside)
                    for i in range(first, last)
                }
                for c in range(2)
            ]

        def cut(found):
            for c in range(2):
                for i in found[c]:
                    if i < HALO:
                        found[c][i] = found[c][i] * keep
            return found

        def at(source, i):
            return [source[c][i] for c in range(2)]

        u1 = cut(powers(v, 1, HALO + 1))
        for c in range(2):
            for i in range(HALO + 1, HALO + 3):
                u1[c][i] = u1_ref[c, own(i)]
        u2 = cut(powers(u1, 2, HALO + 2))
        for c in range(2):
            for i in range(HALO + 2, HALO + 4):
                u2[c][i] = u2_ref[c, own(i)]
        u3 = powers(u2, HALO, HALO + 3)

        count(0, forms(at(v, HALO), at(v, HALO)))
        count(2, forms(at(v, HALO), at(u1, HALO)))
        for i in range(HALO, HALO + 2):
            count(4, forms(at(u1, i), at(u1, i)))
            count(6, forms(at(u1, i), at(u2, i)))
        for i in range(HALO, HALO + 3):
            count(8, forms(at(u2, i), at(u2, i)))
            count(10, forms(at(u2, i), at(u3, i)))
        for c in range(2):
            b1_ref[c, 1 if high else 0] = u1[c][HALO][:, 0:128]
            for i in range(2):
                b2_ref[c, 3 - i if high else i] = u2[c][HALO + i][:, 0:128]

    lane = lanes((1, 128))
    line = jnp.zeros((1, 128), jnp.float32)
    for j, part in enumerate(sums):
        line = jnp.where(lane == j, jnp.sum(part, keepdims=True), line)
    mine = shift_ref.shape[0]
    for i in range(mine):
        for c in range(2):
            for base, ref in ((SHIFT_LANE, shift_ref), (WEIGHT_LANE, weight_ref)):
                here = (lane == base + 16 * c + mine * pole + i) & (tile == 0)
                line = jnp.where(here, ref[i:i + 1, c:c + 1], line)
    line_ref[...] = jnp.broadcast_to(line, line_ref.shape)


def mul(a, b):
    return a[0] * b[0] - a[1] * b[1], a[0] * b[1] + a[1] * b[0]


def add(a, b):
    return a[0] + b[0], a[1] + b[1]


def sub(a, b):
    return a[0] - b[0], a[1] - b[1]


def div(a, b):
    size = jnp.maximum(jnp.abs(b[0]), jnp.abs(b[1]))
    inverse = jnp.where(size > 0.0, 1.0 / size, 0.0)
    b = (b[0] * inverse, b[1] * inverse)
    norm = b[0] * b[0] + b[1] * b[1]
    factor = jnp.where(size > 0.0, inverse / norm, 0.0)
    return (a[0] * b[0] + a[1] * b[1]) * factor, (a[1] * b[0] - a[0] * b[1]) * factor


def coefficients(line, poles):
    at = lanes((1, 128))

    def spot(j):
        return jnp.sum(jnp.where(at == j, line, 0.0), axis=1, keepdims=True) + jnp.zeros((1, 128), jnp.float32)

    m = [(spot(2 * j), spot(2 * j + 1)) for j in range(MOMENTS)]
    shift = tuple(pltpu.roll(line, (128 - SHIFT_LANE - 16 * c) % 128, 1) for c in range(2))
    weight = tuple(pltpu.roll(line, (128 - WEIGHT_LANE - 16 * c) % 128, 1) for c in range(2))
    mean = div(m[1], m[0])
    rest = list(m)
    for level in range(1, MOMENTS):
        for j in range(MOMENTS - 1, level - 1, -1):
            rest[j] = sub(rest[j], mul(mean, rest[j - 1]))
    c0, c2, c3, c4, c5 = rest[0], rest[2], rest[3], rest[4], rest[5]
    b1, e1 = div(c2, c0), div(c3, c2)
    d2 = sub(sub(c4, mul(e1, c3)), mul(b1, c2))
    b2 = div(d2, c2)
    e2 = div(sub(sub(sub(c5, mul(e1, c4)), mul(b1, c3)), mul(e1, d2)), d2)
    base = add((shift[1] / TIME_STEP + SIGMA, -shift[0] / TIME_STEP), mean)
    g2 = add(base, e2)
    g1 = sub(add(base, e1), div(b2, g2))
    y0 = div((jnp.zeros_like(line), jnp.full_like(line, -1.0 / TIME_STEP)), sub(base, div(b1, g1)))
    y1 = div((-y0[0], -y0[1]), g1)
    y2 = div((-y1[0], -y1[1]), g2)
    k1 = sub(y1, mul(e1, y2))
    k0 = sub(y0, mul(b1, y2))
    k0 = add(sub(k0, mul(mean, k1)), mul(mul(mean, mean), y2))
    twice = mul(mean, y2)
    k1 = sub(k1, (2.0 * twice[0], 2.0 * twice[1]))
    found = []
    for k in (k0, k1, y2):
        term = mul(weight, k)
        found.append(tuple(jnp.sum(jnp.where(at < poles, part, 0.0), axis=1, keepdims=True) for part in term))
    return found


def combine_kernel(poles, field_ref, u1_ref, u2_ref, b1_ref, b2_ref, sums_ref, out_ref):
    line = jnp.sum(sums_ref[...], axis=0, keepdims=True)
    k = coefficients(line, poles)
    rows = field_ref.shape[1]
    k = [tuple(jnp.broadcast_to(part, (8, 128)) for part in pair) for pair in k]

    def source(inner, outer, reach, i):
        if i < reach:
            return outer, i
        if i >= rows - reach:
            return outer, i - rows + 2 * reach
        return inner, i

    for i in range(rows):
        places = ((field_ref, i), source(u1_ref, b1_ref, 1, i), source(u2_ref, b2_ref, 2, i))
        for h in range(field_ref.shape[2] // 8):
            at = slice(8 * h, 8 * h + 8)
            total = None
            for pair, (ref, x) in zip(k, places):
                term = mul(pair, (ref[0, x, at, 0:128], ref[1, x, at, 0:128]))
                total = term if total is None else add(total, term)
            out_ref[0, i, at] = total[0]
            out_ref[1, i, at] = total[1]


def call(kernel, out_shape, specs, scratch=(), flops=0, bytes_accessed=0):
    return pl.pallas_call(
        kernel,
        out_shape=out_shape,
        in_specs=specs,
        out_specs=jax.tree.map(lambda _: VMEM, out_shape),
        scratch_shapes=list(scratch),
        compiler_params=pltpu.CompilerParams(vmem_limit_bytes=32 * 2**20),
        cost_estimate=pl.CostEstimate(flops=flops, bytes_accessed=bytes_accessed, transcendentals=0),
    )


def swaps(axis):
    size = lax.axis_size(axis)
    gaps = [(i, i + 1) for i in range(1, size - 1, 2)]
    return [(i, i ^ 1) for i in range(size)], gaps + [(b, a) for a, b in gaps]


def on_device(psi, trap, pole_shift, pole_weight):
    tiles, poles = lax.axis_size("tile"), lax.axis_size("pole")
    rows, depth, width = trap.shape
    f32 = functools.partial(jax.ShapeDtypeStruct, dtype=jnp.float32)
    anywhere = pl.BlockSpec(memory_space=pl.ANY)

    packed, field = call(
        load_kernel, (f32((3, 2, depth, 128)), f32((3, rows, depth, width))), [anywhere] * 2,
        [pltpu.SemaphoreType.DMA((2, 2))],
    )(psi, trap)
    near, across = swaps("pole")
    y2 = lax.ppermute(packed, "pole", across)
    y1 = lax.ppermute(packed, "pole", near)

    edge = f32((3 * HALO, depth, 128))
    s1, s2 = call(edge_kernel, (edge, edge), [VMEM] * 3)(field, y1, y2)
    near, across = swaps("tile")
    x2 = lax.ppermute(s2, "tile", across)
    x1 = lax.ppermute(s1, "tile", near)

    wide = f32((2, rows, depth, 2 * width))
    grown, u1, u2, sums = call(
        inner_kernel,
        (f32((3, rows, depth, 2 * width)), wide, wide, f32((2 * MOMENTS, 8, 128))),
        [VMEM] * 3, flops=20_000_000, bytes_accessed=8_000_000,
    )(field, y1, y2)
    devices = tiles * poles
    b1, b2, line = call(
        outer_kernel,
        (f32((2, 2, depth, width)), f32((2, 4, depth, width)), f32((devices, 128))),
        [VMEM] * 8,
    )(pole_shift, pole_weight, grown, u1, u2, sums, x1, x2)

    lines = lax.all_to_all(line.reshape(devices, 1, 128), ("pole", "tile"), 0, 0, tiled=True)
    combine = functools.partial(combine_kernel, pole_shift.shape[0] * poles)
    return call(combine, f32(psi.shape), [VMEM] * 6)(field, u1, u2, b1, b2, lines.reshape(devices, 128))


def solution(mesh):
    placed = (
        P(None, "tile", None, "pole"),
        P("tile", None, "pole"),
        P("pole", None),
        P("pole", None),
    )
    return jax.shard_map(
        on_device,
        mesh=mesh,
        in_specs=placed,
        out_specs=P(None, "tile", None, "pole"),
        check_vma=False,
    )
```

time: 50 us -> 42.4 us (0.85)
  waiting for transfers between devices: 5.3 us -> 1.67 us
  blocking collectives: 26.1 us -> 23.1 us
  Pallas kernels: 9.24 us -> 8.41 us
    ppermute x4, waiting for transfers between devices: 5.3 us -> 1.67 us  [the longest x1 1.67 us: on_device(): y2 = lax.ppermute(packed, 'pole', across)]
    all_to_all x1, blocking collectives: 26.1 us -> 23.1 us  [on_device(): lax.all_to_all(line.reshape(devices, 1, 128), ('pole', 'tile'), 0, 0, til...]
    pallas_call x4 -> x5, Pallas kernels: 9.24 us -> 8.41 us  [the longest x1 5.43 us: on_device(): call(inner_kernel, (f32((3, rows, depth, 2 * width)), wide, wide, f32((2...]
    unnamed x12 -> x8, local copies, waits for them, and re-layouts: 2.01 us -> 2 us
  transfers between devices with their start and end apart: 4 -> 4, of which waited for: 2 -> 1; matrix products, arithmetic and copies ran while one was open for 0% -> 0% of each run, Pallas kernels for 0% -> 13%
where the time goes in v2:
time: 42.4 us; the launch traced here: 42.2 us
  blocking collectives  23.1 us (54%)
  Pallas kernels  8.41 us (20%)
  starting transfers between devices  6.91 us (16%)
  local copies, waits for them, and re-layouts  2 us (5%)
  waiting for transfers between devices  1.67 us (4%)
    all_to_all x1, blocking collectives, on_device(): lax.all_to_all(line.reshape(devices, 1, 128), ('pole', 'tile'), 0, 0, til...  23.1 us
    pallas_call x1, Pallas kernels, on_device(): call(inner_kernel, (f32((3, rows, depth, 2 * width)), wide, wide, f32((2...  5.43 us
    ppermute x1, starting transfers between devices, on_device(): y2 = lax.ppermute(packed, 'pole', across)  4.51 us
    unnamed x8, local copies, waits for them, and re-layouts  2 us
    ppermute x1, waiting for transfers between devices, on_device(): y2 = lax.ppermute(packed, 'pole', across)  1.67 us
    ppermute x1, starting transfers between devices, on_device(): x1 = lax.ppermute(s1, 'tile', near)  1.66 us
    pallas_call x1, Pallas kernels, on_device(): call(combine, f32(psi.shape), [VMEM] * 6)  1.31 us
  transfers between devices with their start and end apart: 4, of which 1 were waited for; matrix products, arithmetic and copies ran while one was open for 0% of the time, Pallas kernels for 13%

profile of v2, /device:TPU:1, one launch (start us, length us, event | category | flops | bytes accessed | tf_op | source)
XLA Modules:
  0.0 42.2 jit_solution(2004630582057449143)
XLA Ops:
  0.0 0.0 copy-start
  0.0 1.0 %copy-done = f32[2,32,16,128]{3,2,1,0:T(8,128)S(1)} copy-done((f32[2,32,16,128]{3,2,1,0:T(8,128)S(1)}, f32[2,32,16,128]{3,2,1,0:T(8,128)}, u32[]{:S(2)}) %copy-start) | copy-done | bytes 524312
  1.0 0.0 copy-start.1
  1.0 0.9 %copy-done.1 = f32[32,16,128]{2,1,0:T(8,128)S(1)} copy-done((f32[32,16,128]{2,1,0:T(8,128)S(1)}, f32[32,16,128]{2,1,0:T(8,128)}, u32[]{:S(2)}) %copy-start.1) | copy-done | bytes 262168
  2.0 0.0 copy-start.2
  2.0 0.0 copy-start.3
  2.0 0.8 %shard_map.46 = (f32[3,2,16,128]{3,2,1,0:T(8,128)S(1)}, f32[3,32,16,128]{3,2,1,0:T(8,128)S(1)}) custom-call(f32[2,32,16,128]{3,2,1,0:T(8,128)S(1)} %copy-done, f32[32,16,128]{2,1,0:T(8,128)S(1)} %copy-done.1), custom_call_target="tpu_custom_call" | custom-call | tf_op jit(solution)/shard_map/pallas_call | solution.py:355
  2.8 4.5 %collective-permute-start.1 = (f32[3,2,16,128]{3,2,1,0:T(8,128)S(1)}, f32[3,2,16,128]{3,2,1,0:T(8,128)S(1)}, u32[]{:S(2)}, u32[]{:S(2)}) collective-permute-start(f32[3,2,16,128]{3,2,1,0:T(8,128)S(1)} %get-tuple-element.17), channel_id=1, source_target_pairs={{32,64},{64,32},{33,65},{65,33},{34,66},{66,34},{35,67},{67,35},{3... | collective-permute-start | bytes 147464 | tf_op jit(solution)/shard_map/ppermute | solution.py:360
  7.3 0.1 collective-permute-start
  7.4 1.7 %collective-permute-done.1.y2_ref = f32[3,2,16,128]{3,2,1,0:T(8,128)S(1)} collective-permute-done((f32[3,2,16,128]{3,2,1,0:T(8,128)S(1)}, f32[3,2,16,128]{3,2,1,0:T(8,128)S(1)}, u32[]{:S(2)}, u32[]{:S(2)}) %collective-permute-start.1) | collective-permute-done | bytes 49184 | tf_op jit(solution)/shard_map/ppermute | solution.py:360
  9.0 0.0 collective-permute-done.y1_ref
  9.0 0.1 shard_map.48
  9.1 1.7 %collective-permute-start.2 = (f32[9,16,128]{2,1,0:T(8,128)S(1)}, f32[9,16,128]{2,1,0:T(8,128)S(1)}, u32[]{:S(2)}, u32[]{:S(2)}) collective-permute-start(f32[9,16,128]{2,1,0:T(8,128)S(1)} %get-tuple-element.22), channel_id=1, source_target_pairs={{0,1},{1,0},{2,3},{3,2},{4,5},{5,4},{6,7},{7,6},{8,9},{9,8},{10,11... | collective-permute-start | bytes 221192 | tf_op jit(solution)/shard_map/ppermute | solution.py:367
  10.8 0.7 %collective-permute-start.3 = (f32[9,16,128]{2,1,0:T(8,128)S(1)}, f32[9,16,128]{2,1,0:T(8,128)S(1)}, u32[]{:S(2)}, u32[]{:S(2)}) collective-permute-start(f32[9,16,128]{2,1,0:T(8,128)S(1)} %get-tuple-element.23), channel_id=1, source_target_pairs={{1,2},{3,4},{5,6},{7,8},{9,10},{11,12},{13,14},{15,16},{17,18},{19... | collective-permute-start | bytes 221192 | tf_op jit(solution)/shard_map/ppermute | solution.py:366
  11.5 5.4 %shard_map.47 = (f32[3,32,16,256]{3,2,1,0:T(8,128)S(1)}, f32[2,32,16,256]{3,2,1,0:T(8,128)S(1)}, f32[2,32,16,256]{3,2,1,0:T(8,128)S(1)}, f32[12,8,128]{2,1,0:T(8,128)S(1)}) custom-call(f32[3,32,16,128]{3,2,1,0:T(8,128)S(1)} %get-tuple-element.16.field_ref, f32[3,2,16,128]{3,2,1,0:T(8,128)S(1)} %collective-permute-done.y1_ref, ...), custom_call_target="tpu_custom_call" | custom-call | flops 20000000 | bytes 8000000 | tf_op jit(solution)/shard_map/pallas_call | solution.py:370
  16.9 0.0 collective-permute-done.2.x1_ref
  16.9 0.0 collective-permute-done.3.x2_ref
  16.9 0.0 copy-done.2
  16.9 0.0 copy-done.3
  16.9 0.8 %shard_map.49 = (f32[2,2,16,128]{3,2,1,0:T(8,128)S(1)}, f32[2,4,16,128]{3,2,1,0:T(8,128)S(1)}, f32[128,128]{1,0:T(8,128)S(1)}) custom-call(f32[2,2]{1,0:T(2,128)S(1)} %copy-done.2, f32[2,2]{1,0:T(2,128)S(1)} %copy-done.3, f32[3,32,16,256]{3,2,1,0:T(8,128)S(1)} %get-tuple-element.20.grown_ref, f32[2,32,16,256]{3,2,1,0:T(8,128)S(1)} %get-tuple-element.18.u1_ref, ...), custom_call_target="tpu_custom_call" | custom-call | tf_op jit(solution)/shard_map/pallas_call | solution.py:376
  17.8 23.1 %all_to_all.5 = f32[128,1,128]{2,1,0:T(1,128)S(1)} all-to-all(f32[128,1,128]{2,1,0:T(1,128)S(1)} %bitcast.5), channel_id=1, replica_groups=mesh['pole'=4,'tile'=32] {'pole','tile'}, dimensions={0} | all-to-all | bytes 131072 | tf_op jit(solution)/shard_map/all_to_all | solution.py:382
  40.9 1.3 %shard_map.50 = f32[2,32,16,128]{3,2,1,0:T(8,128)} custom-call(f32[3,32,16,128]{3,2,1,0:T(8,128)S(1)} %get-tuple-element.16.field_ref, f32[2,32,16,256]{3,2,1,0:T(8,128)S(1)} %get-tuple-element.18.u1_ref, f32[2,32,16,256]{3,2,1,0:T(8,128)S(1)} %get-tuple-element.19.u2_ref, f32[2,2,16,128]{3,2,1,0:T(8,128)S(1)} %get-tuple-element.24.b1_ref, ...), custom_call_target="tpu_custom_call" | custom-call | tf_op jit(solution)/shard_map/pallas_call | solution.py:384
Async XLA Ops:
  0.0 1.0 %copy-start = (f32[2,32,16,128]{3,2,1,0:T(8,128)S(1)}, f32[2,32,16,128]{3,2,1,0:T(8,128)}, u32[]{:S(2)}) copy-start(f32[2,32,16,128]{3,2,1,0:T(8,128)} %psi_ref.1) | copy-start | bytes 1572868
  1.0 0.9 %copy-start.1 = (f32[32,16,128]{2,1,0:T(8,128)S(1)}, f32[32,16,128]{2,1,0:T(8,128)}, u32[]{:S(2)}) copy-start(f32[32,16,128]{2,1,0:T(8,128)} %trap_ref.1) | copy-start | bytes 786436
  2.0 14.9 %copy-start.2 = (f32[2,2]{1,0:T(2,128)S(1)}, f32[2,2]{1,0:T(2,128)}, u32[]{:S(2)}) copy-start(f32[2,2]{1,0:T(2,128)} %shift_ref.1) | copy-start | bytes 52
  2.0 14.9 %copy-start.3 = (f32[2,2]{1,0:T(2,128)S(1)}, f32[2,2]{1,0:T(2,128)}, u32[]{:S(2)}) copy-start(f32[2,2]{1,0:T(2,128)} %weight_ref.1) | copy-start | bytes 52
  2.8 6.3 %collective-permute-start.1 = (f32[3,2,16,128]{3,2,1,0:T(8,128)S(1)}, f32[3,2,16,128]{3,2,1,0:T(8,128)S(1)}, u32[]{:S(2)}, u32[]{:S(2)}) collective-permute-start(f32[3,2,16,128]{3,2,1,0:T(8,128)S(1)} %get-tuple-element.17), channel_id=1, source_target_pairs={{32,64},{64,32},{33,65},{65,33},{34,66},{66,34},{35,67},{67,35},{3... | collective-permute-start | bytes 147464 | tf_op jit(solution)/shard_map/ppermute | solution.py:360
  7.3 1.8 %collective-permute-start = (f32[3,2,16,128]{3,2,1,0:T(8,128)S(1)}, f32[3,2,16,128]{3,2,1,0:T(8,128)S(1)}, u32[]{:S(2)}, u32[]{:S(2)}) collective-permute-start(f32[3,2,16,128]{3,2,1,0:T(8,128)S(1)} %get-tuple-element.17), channel_id=1, source_target_pairs={{0,32},{32,0},{64,96},{96,64},{1,33},{33,1},{65,97},{97,65},{2,34}... | collective-permute-start | bytes 147464 | tf_op jit(solution)/shard_map/ppermute | solution.py:361
  9.1 7.8 %collective-permute-start.2 = (f32[9,16,128]{2,1,0:T(8,128)S(1)}, f32[9,16,128]{2,1,0:T(8,128)S(1)}, u32[]{:S(2)}, u32[]{:S(2)}) collective-permute-start(f32[9,16,128]{2,1,0:T(8,128)S(1)} %get-tuple-element.22), channel_id=1, source_target_pairs={{0,1},{1,0},{2,3},{3,2},{4,5},{5,4},{6,7},{7,6},{8,9},{9,8},{10,11... | collective-permute-start | bytes 221192 | tf_op jit(solution)/shard_map/ppermute | solution.py:367
  10.8 6.1 %collective-permute-start.3 = (f32[9,16,128]{2,1,0:T(8,128)S(1)}, f32[9,16,128]{2,1,0:T(8,128)S(1)}, u32[]{:S(2)}, u32[]{:S(2)}) collective-permute-start(f32[9,16,128]{2,1,0:T(8,128)S(1)} %get-tuple-element.23), channel_id=1, source_target_pairs={{1,2},{3,4},{5,6},{7,8},{9,10},{11,12},{13,14},{15,16},{17,18},{19... | collective-permute-start | bytes 221192 | tf_op jit(solution)/shard_map/ppermute | solution.py:366

commit v3 on v2

--- a/solution.py
+++ b/solution.py
@@ -16,6 +16,7 @@
 MOMENTS = 6
 SHIFT_LANE, WEIGHT_LANE = 16, 48
 VMEM = pl.BlockSpec(memory_space=pltpu.VMEM)
+ANYWHERE = pl.BlockSpec(memory_space=pl.ANY)
 
 
 def lanes(shape):
@@ -33,20 +34,16 @@
 def load_kernel(psi_ref, trap_ref, packed_ref, field_ref, sems):
     rows, depth = trap_ref.shape[:2]
     half_rows = rows // 2
-    copies = []
-    for half in range(2):
-        at = pl.ds(half * half_rows, half_rows)
-        pair = (
-            pltpu.make_async_copy(psi_ref.at[:, at], field_ref.at[0:2, at], sems.at[half, 0]),
-            pltpu.make_async_copy(trap_ref.at[at], field_ref.at[2, at], sems.at[half, 1]),
-        )
-        for copy in pair:
-            copy.start()
-        copies.append(pair)
+    copies = (
+        pltpu.make_async_copy(psi_ref, field_ref.at[0:2], sems.at[0]),
+        pltpu.make_async_copy(trap_ref, field_ref.at[2], sems.at[1]),
+    )
+    for copy in copies:
+        copy.start()
+    for copy in copies:
+        copy.wait()
     group = lanes((depth, 128)) // 8
     for half in range(2):
-        for copy in copies[half]:
-            copy.wait()
         packs = [jnp.zeros((depth, 128), jnp.float32)] * 3
         for g in range(half_rows):
             row = half * half_rows + g
@@ -96,10 +93,17 @@
 
 
 def neighbours_z(b):
-    depth = b.shape[0]
-    z = lax.broadcasted_iota(jnp.int32, b.shape, 0)
-    below = jnp.where(z == 0, 0.0, pltpu.roll(b, 1, 0))
-    return below + jnp.where(z == depth - 1, 0.0, pltpu.roll(b, depth - 1, 0))
+    z = lax.broadcasted_iota(jnp.int32, (8, b.shape[1]), 0)
+    low, high = b[0:8], b[8:16]
+    low_up, high_up = pltpu.roll(low, 1, 0), pltpu.roll(high, 1, 0)
+    low_down, high_down = pltpu.roll(low, 7, 0), pltpu.roll(high, 7, 0)
+    return jnp.concatenate(
+        [
+            jnp.where(z == 0, 0.0, low_up) + jnp.where(z == 7, high_down, low_down),
+            jnp.where(z == 0, low_up, high_up) + jnp.where(z == 7, 0.0, high_down),
+        ],
+        axis=0,
+    )
 
 
 def inside_mask(depth):
@@ -148,7 +152,7 @@
             return tuple(a + b for a, b in zip(sums, forms(old, old) + forms(old, new)))
 
         zero = jnp.zeros((8, 128), jnp.float32)
-        return lax.fori_loop(0, rows - 2 * reach, step, (zero,) * 4, unroll=2)
+        return lax.fori_loop(0, rows - 2 * reach, step, (zero,) * 4, unroll=True)
 
     sums = sweep(grown_ref, u1_ref, 1) + sweep(u1_ref, u2_ref, 2) + sweep(u2_ref, None, 3)
     for j, part in enumerate(sums):
@@ -156,7 +160,7 @@
 
 
 def outer_kernel(
-    shift_ref, weight_ref, grown_ref, u1_ref, u2_ref, sums_ref, x1_ref, x2_ref, b1_ref, b2_ref, line_ref,
+    shift_ref, weight_ref, grown_ref, u1_ref, u2_ref, sums_ref, x2_ref, x1_ref, b1_ref, b2_ref, line_ref,
 ):
     rows, depth = grown_ref.shape[1:3]
     tile, pole = position()
@@ -257,12 +261,9 @@
     return a[0] - b[0], a[1] - b[1]
 
 
-def div(a, b):
-    size = jnp.maximum(jnp.abs(b[0]), jnp.abs(b[1]))
-    inverse = jnp.where(size > 0.0, 1.0 / size, 0.0)
-    b = (b[0] * inverse, b[1] * inverse)
+def over(a, b):
     norm = b[0] * b[0] + b[1] * b[1]
-    factor = jnp.where(size > 0.0, inverse / norm, 0.0)
+    factor = jnp.where(norm > 0.0, 1.0 / norm, 0.0)
     return (a[0] * b[0] + a[1] * b[1]) * factor, (a[1] * b[0] - a[0] * b[1]) * factor
 
 
@@ -275,22 +276,23 @@
     m = [(spot(2 * j), spot(2 * j + 1)) for j in range(MOMENTS)]
     shift = tuple(pltpu.roll(line, (128 - SHIFT_LANE - 16 * c) % 128, 1) for c in range(2))
     weight = tuple(pltpu.roll(line, (128 - WEIGHT_LANE - 16 * c) % 128, 1) for c in range(2))
-    mean = div(m[1], m[0])
+    scale = 1.0 / jnp.maximum(jnp.abs(m[0][0]), jnp.abs(m[0][1]))
+    m = [(re * scale, im * scale) for re, im in m]
+    mean = over(m[1], m[0])
     rest = list(m)
     for level in range(1, MOMENTS):
         for j in range(MOMENTS - 1, level - 1, -1):
             rest[j] = sub(rest[j], mul(mean, rest[j - 1]))
     c0, c2, c3, c4, c5 = rest[0], rest[2], rest[3], rest[4], rest[5]
-    b1, e1 = div(c2, c0), div(c3, c2)
+    b1, e1 = over(c2, c0), over(c3, c2)
     d2 = sub(sub(c4, mul(e1, c3)), mul(b1, c2))
-    b2 = div(d2, c2)
-    e2 = div(sub(sub(sub(c5, mul(e1, c4)), mul(b1, c3)), mul(e1, d2)), d2)
+    b2 = over(d2, c2)
+    e2 = over(sub(sub(sub(c5, mul(e1, c4)), mul(b1, c3)), mul(e1, d2)), d2)
     base = add((shift[1] / TIME_STEP + SIGMA, -shift[0] / TIME_STEP), mean)
     g2 = add(base, e2)
-    g1 = sub(add(base, e1), div(b2, g2))
-    y0 = div((jnp.zeros_like(line), jnp.full_like(line, -1.0 / TIME_STEP)), sub(base, div(b1, g1)))
-    y1 = div((-y0[0], -y0[1]), g1)
-    y2 = div((-y1[0], -y1[1]), g2)
+    g1 = sub(mul(add(base, e1), g2), b2)
+    source = over((jnp.zeros_like(line), jnp.full_like(line, -1.0 / TIME_STEP)), sub(mul(base, g1), mul(b1, g2)))
+    y0, y1, y2 = mul(source, g1), mul((-source[0], -source[1]), g2), source
     k1 = sub(y1, mul(e1, y2))
     k0 = sub(y0, mul(b1, y2))
     k0 = add(sub(k0, mul(mean, k1)), mul(mul(mean, mean), y2))
@@ -303,7 +305,7 @@
     return found
 
 
-def combine_kernel(poles, field_ref, u1_ref, u2_ref, b1_ref, b2_ref, sums_ref, out_ref):
+def combine_kernel(poles, field_ref, u1_ref, u2_ref, b1_ref, b2_ref, sums_ref, out_ref, held, sems):
     line = jnp.sum(sums_ref[...], axis=0, keepdims=True)
     k = coefficients(line, poles)
     rows = field_ref.shape[1]
@@ -316,6 +318,8 @@
             return outer, i - rows + 2 * reach
         return inner, i
 
+    parts = 2
+    copies = []
     for i in range(rows):
         places = ((field_ref, i), source(u1_ref, b1_ref, 1, i), source(u2_ref, b2_ref, 2, i))
         for h in range(field_ref.shape[2] // 8):
@@ -324,17 +328,26 @@
             for pair, (ref, x) in zip(k, places):
                 term = mul(pair, (ref[0, x, at, 0:128], ref[1, x, at, 0:128]))
                 total = term if total is None else add(total, term)
-            out_ref[0, i, at] = total[0]
-            out_ref[1, i, at] = total[1]
-
-
-def call(kernel, out_shape, specs, scratch=(), flops=0, bytes_accessed=0):
+            held[0, i, at] = total[0]
+            held[1, i, at] = total[1]
+        if (i + 1) % (rows // parts) == 0:
+            part = pl.ds(i + 1 - rows // parts, rows // parts)
+            for c in range(2):
+                copy = pltpu.make_async_copy(held.at[c, part], out_ref.at[c, part], sems.at[c, len(copies) // 2])
+                copy.start()
+                copies.append(copy)
+    for copy in copies:
+        copy.wait()
+
+
+def call(kernel, out_shape, specs, scratch=(), flops=0, bytes_accessed=0, aliases={}, out_spec=VMEM):
     return pl.pallas_call(
         kernel,
         out_shape=out_shape,
         in_specs=specs,
-        out_specs=jax.tree.map(lambda _: VMEM, out_shape),
+        out_specs=jax.tree.map(lambda _: out_spec, out_shape),
         scratch_shapes=list(scratch),
+        input_output_aliases=aliases,
         compiler_params=pltpu.CompilerParams(vmem_limit_bytes=32 * 2**20),
         cost_estimate=pl.CostEstimate(flops=flops, bytes_accessed=bytes_accessed, transcendentals=0),
     )
@@ -350,11 +363,11 @@
     tiles, poles = lax.axis_size("tile"), lax.axis_size("pole")
     rows, depth, width = trap.shape
     f32 = functools.partial(jax.ShapeDtypeStruct, dtype=jnp.float32)
-    anywhere = pl.BlockSpec(memory_space=pl.ANY)
-
+
+    psi, trap = (pltpu.with_memory_space_constraint(x, pltpu.HBM) for x in (psi, trap))
     packed, field = call(
-        load_kernel, (f32((3, 2, depth, 128)), f32((3, rows, depth, width))), [anywhere] * 2,
-        [pltpu.SemaphoreType.DMA((2, 2))],
+        load_kernel, (f32((3, 2, depth, 128)), f32((3, rows, depth, width))), [ANYWHERE] * 2,
+        [pltpu.SemaphoreType.DMA((2,))],
     )(psi, trap)
     near, across = swaps("pole")
     y2 = lax.ppermute(packed, "pole", across)
@@ -377,11 +390,14 @@
         outer_kernel,
         (f32((2, 2, depth, width)), f32((2, 4, depth, width)), f32((devices, 128))),
         [VMEM] * 8,
-    )(pole_shift, pole_weight, grown, u1, u2, sums, x1, x2)
+    )(pole_shift, pole_weight, grown, u1, u2, sums, x2, x1)
 
     lines = lax.all_to_all(line.reshape(devices, 1, 128), ("pole", "tile"), 0, 0, tiled=True)
     combine = functools.partial(combine_kernel, pole_shift.shape[0] * poles)
-    return call(combine, f32(psi.shape), [VMEM] * 6)(field, u1, u2, b1, b2, lines.reshape(devices, 128))
+    return call(
+        combine, f32((2, rows, depth, width)), [VMEM] * 6,
+        [pltpu.VMEM((2, rows, depth, width), jnp.float32), pltpu.SemaphoreType.DMA((2, 2))], out_spec=ANYWHERE,
+    )(field, u1, u2, b1, b2, lines.reshape(devices, 128))
 
 
 def solution(mesh):

time: 42.4 us -> 40.4 us (0.953)
  starting transfers between devices: 6.91 us -> 9.85 us
  Pallas kernels: 8.41 us -> 6.15 us
  local copies, waits for them, and re-layouts: 2 us -> 0.01 us
  blocking collectives: 23.1 us -> 22.5 us
    ppermute x1, starting transfers between devices: 1.66 us -> 4.6 us  [on_device(): x1 = lax.ppermute(s1, 'tile', near)]
    pallas_call x1, Pallas kernels: 5.43 us -> 2.65 us  [on_device(): call(inner_kernel, (f32((3, rows, depth, 2 * width)), wide, wide, f32((2...]
    unnamed x8 -> x4, local copies, waits for them, and re-layouts: 2 us -> 0.01 us
    pallas_call x1, Pallas kernels: 0.76 us -> 1.42 us  [on_device(): call(load_kernel, (f32((3, 2, depth, 128)), f32((3, rows, depth, width)))...]
    all_to_all x1, blocking collectives: 23.1 us -> 22.5 us  [on_device(): lax.all_to_all(line.reshape(devices, 1, 128), ('pole', 'tile'), 0, 0, til...]
  transfers between devices with their start and end apart: 4 -> 4, of which waited for: 1 -> 1; matrix products, arithmetic and copies ran while one was open for 0% -> 0% of each run, Pallas kernels for 13% -> 7%
where the time goes in v3:
time: 40.4 us; the launch traced here: 40.3 us
  blocking collectives  22.5 us (56%)
  starting transfers between devices  9.85 us (24%)
  Pallas kernels  6.15 us (15%)
  waiting for transfers between devices  1.67 us (4%)
    all_to_all x1, blocking collectives, on_device(): lax.all_to_all(line.reshape(devices, 1, 128), ('pole', 'tile'), 0, 0, til...  22.5 us
    ppermute x1, starting transfers between devices, on_device(): x1 = lax.ppermute(s1, 'tile', near)  4.6 us
    ppermute x1, starting transfers between devices, on_device(): y2 = lax.ppermute(packed, 'pole', across)  4.51 us
    pallas_call x1, Pallas kernels, on_device(): call(inner_kernel, (f32((3, rows, depth, 2 * width)), wide, wide, f32((2...  2.65 us
    ppermute x1, waiting for transfers between devices, on_device(): y2 = lax.ppermute(packed, 'pole', across)  1.67 us
    pallas_call x1, Pallas kernels, on_device(): call(load_kernel, (f32((3, 2, depth, 128)), f32((3, rows, depth, width)))...  1.42 us
    pallas_call x1, Pallas kernels, on_device(): call(combine, f32((2, rows, depth, width)), [VMEM] * 6, [pltpu.VMEM((2, r...  1.17 us
    pallas_call x1, Pallas kernels, on_device(): call(outer_kernel, (f32((2, 2, depth, width)), f32((2, 4, depth, width)),...  0.82 us
  transfers between devices with their start and end apart: 4, of which 1 were waited for; matrix products, arithmetic and copies ran while one was open for 0% of the time, Pallas kernels for 7%

profile of v3, /device:TPU:1, one launch (start us, length us, event | category | flops | bytes accessed | tf_op | source)
XLA Modules:
  0.0 40.3 jit_solution(10561190550379744904)
XLA Ops:
  0.0 0.0 copy-start.1
  0.0 0.0 copy-start
  0.0 1.4 %shard_map.46 = (f32[3,2,16,128]{3,2,1,0:T(8,128)S(1)}, f32[3,32,16,128]{3,2,1,0:T(8,128)S(1)}) custom-call(f32[2,32,16,128]{3,2,1,0:T(8,128)} %psi_ref.1, f32[32,16,128]{2,1,0:T(8,128)} %trap_ref.1), custom_call_target="tpu_custom_call" | custom-call | tf_op jit(solution)/shard_map/pallas_call | solution.py:368
  1.4 4.5 %collective-permute-start.1 = (f32[3,2,16,128]{3,2,1,0:T(8,128)S(1)}, f32[3,2,16,128]{3,2,1,0:T(8,128)S(1)}, u32[]{:S(2)}, u32[]{:S(2)}) collective-permute-start(f32[3,2,16,128]{3,2,1,0:T(8,128)S(1)} %get-tuple-element.17), channel_id=1, source_target_pairs={{32,64},{64,32},{33,65},{65,33},{34,66},{66,34},{35,67},{67,35},{3... | collective-permute-start | bytes 147464 | tf_op jit(solution)/shard_map/ppermute | solution.py:373
  6.0 0.1 collective-permute-start
  6.0 1.7 %collective-permute-done.1.y2_ref = f32[3,2,16,128]{3,2,1,0:T(8,128)S(1)} collective-permute-done((f32[3,2,16,128]{3,2,1,0:T(8,128)S(1)}, f32[3,2,16,128]{3,2,1,0:T(8,128)S(1)}, u32[]{:S(2)}, u32[]{:S(2)}) %collective-permute-start.1) | collective-permute-done | bytes 49184 | tf_op jit(solution)/shard_map/ppermute | solution.py:373
  7.7 0.0 collective-permute-done.y1_ref
  7.7 0.1 shard_map.48
  7.8 0.7 %collective-permute-start.2 = (f32[9,16,128]{2,1,0:T(8,128)S(1)}, f32[9,16,128]{2,1,0:T(8,128)S(1)}, u32[]{:S(2)}, u32[]{:S(2)}) collective-permute-start(f32[9,16,128]{2,1,0:T(8,128)S(1)} %get-tuple-element.22), channel_id=1, source_target_pairs={{1,2},{3,4},{5,6},{7,8},{9,10},{11,12},{13,14},{15,16},{17,18},{19... | collective-permute-start | bytes 221192 | tf_op jit(solution)/shard_map/ppermute | solution.py:379
  8.5 4.6 %collective-permute-start.3 = (f32[9,16,128]{2,1,0:T(8,128)S(1)}, f32[9,16,128]{2,1,0:T(8,128)S(1)}, u32[]{:S(2)}, u32[]{:S(2)}) collective-permute-start(f32[9,16,128]{2,1,0:T(8,128)S(1)} %get-tuple-element.23), channel_id=1, source_target_pairs={{0,1},{1,0},{2,3},{3,2},{4,5},{5,4},{6,7},{7,6},{8,9},{9,8},{10,11... | collective-permute-start | bytes 221192 | tf_op jit(solution)/shard_map/ppermute | solution.py:380
  13.1 2.6 %shard_map.47 = (f32[3,32,16,256]{3,2,1,0:T(8,128)S(1)}, f32[2,32,16,256]{3,2,1,0:T(8,128)S(1)}, f32[2,32,16,256]{3,2,1,0:T(8,128)S(1)}, f32[12,8,128]{2,1,0:T(8,128)S(1)}) custom-call(f32[3,32,16,128]{3,2,1,0:T(8,128)S(1)} %get-tuple-element.16.field_ref, f32[3,2,16,128]{3,2,1,0:T(8,128)S(1)} %collective-permute-done.y1_ref, ...), custom_call_target="tpu_custom_call" | custom-call | flops 20000000 | bytes 8000000 | tf_op jit(solution)/shard_map/pallas_call | solution.py:383
  15.7 0.0 collective-permute-done.2.x2_ref
  15.7 0.0 collective-permute-done.3.x1_ref
  15.7 0.0 copy-done.1
  15.8 0.0 copy-done
  15.8 0.8 %shard_map.49 = (f32[2,2,16,128]{3,2,1,0:T(8,128)S(1)}, f32[2,4,16,128]{3,2,1,0:T(8,128)S(1)}, f32[128,128]{1,0:T(8,128)S(1)}) custom-call(f32[2,2]{1,0:T(2,128)S(1)} %copy-done, f32[2,2]{1,0:T(2,128)S(1)} %copy-done.1, f32[3,32,16,256]{3,2,1,0:T(8,128)S(1)} %get-tuple-element.20.grown_ref, f32[2,32,16,256]{3,2,1,0:T(8,128)S(1)} %get-tuple-element.18.u1_ref, ...), custom_call_target="tpu_custom_call" | custom-call | tf_op jit(solution)/shard_map/pallas_call | solution.py:389
  16.6 22.5 %all_to_all.5 = f32[128,1,128]{2,1,0:T(1,128)S(1)} all-to-all(f32[128,1,128]{2,1,0:T(1,128)S(1)} %bitcast.5), channel_id=1, replica_groups=mesh['pole'=4,'tile'=32] {'pole','tile'}, dimensions={0} | all-to-all | bytes 131072 | tf_op jit(solution)/shard_map/all_to_all | solution.py:395
  39.1 1.2 %shard_map.50 = f32[2,32,16,128]{3,2,1,0:T(8,128)} custom-call(f32[3,32,16,128]{3,2,1,0:T(8,128)S(1)} %get-tuple-element.16.field_ref, f32[2,32,16,256]{3,2,1,0:T(8,128)S(1)} %get-tuple-element.18.u1_ref, f32[2,32,16,256]{3,2,1,0:T(8,128)S(1)} %get-tuple-element.19.u2_ref, f32[2,2,16,128]{3,2,1,0:T(8,128)S(1)} %get-tuple-element.24.b1_ref, ...), custom_call_target="tpu_custom_call" | custom-call | tf_op jit(solution)/shard_map/pallas_call | solution.py:397
Async XLA Ops:
  0.0 15.7 %copy-start.1 = (f32[2,2]{1,0:T(2,128)S(1)}, f32[2,2]{1,0:T(2,128)}, u32[]{:S(2)}) copy-start(f32[2,2]{1,0:T(2,128)} %weight_ref.1) | copy-start | bytes 52
  0.0 15.8 %copy-start = (f32[2,2]{1,0:T(2,128)S(1)}, f32[2,2]{1,0:T(2,128)}, u32[]{:S(2)}) copy-start(f32[2,2]{1,0:T(2,128)} %shift_ref.1) | copy-start | bytes 52
  1.4 6.3 %collective-permute-start.1 = (f32[3,2,16,128]{3,2,1,0:T(8,128)S(1)}, f32[3,2,16,128]{3,2,1,0:T(8,128)S(1)}, u32[]{:S(2)}, u32[]{:S(2)}) collective-permute-start(f32[3,2,16,128]{3,2,1,0:T(8,128)S(1)} %get-tuple-element.17), channel_id=1, source_target_pairs={{32,64},{64,32},{33,65},{65,33},{34,66},{66,34},{35,67},{67,35},{3... | collective-permute-start | bytes 147464 | tf_op jit(solution)/shard_map/ppermute | solution.py:373
  6.0 1.8 %collective-permute-start = (f32[3,2,16,128]{3,2,1,0:T(8,128)S(1)}, f32[3,2,16,128]{3,2,1,0:T(8,128)S(1)}, u32[]{:S(2)}, u32[]{:S(2)}) collective-permute-start(f32[3,2,16,128]{3,2,1,0:T(8,128)S(1)} %get-tuple-element.17), channel_id=1, source_target_pairs={{0,32},{32,0},{64,96},{96,64},{1,33},{33,1},{65,97},{97,65},{2,34}... | collective-permute-start | bytes 147464 | tf_op jit(solution)/shard_map/ppermute | solution.py:374
  7.8 7.9 %collective-permute-start.2 = (f32[9,16,128]{2,1,0:T(8,128)S(1)}, f32[9,16,128]{2,1,0:T(8,128)S(1)}, u32[]{:S(2)}, u32[]{:S(2)}) collective-permute-start(f32[9,16,128]{2,1,0:T(8,128)S(1)} %get-tuple-element.22), channel_id=1, source_target_pairs={{1,2},{3,4},{5,6},{7,8},{9,10},{11,12},{13,14},{15,16},{17,18},{19... | collective-permute-start | bytes 221192 | tf_op jit(solution)/shard_map/ppermute | solution.py:379
  8.5 7.3 %collective-permute-start.3 = (f32[9,16,128]{2,1,0:T(8,128)S(1)}, f32[9,16,128]{2,1,0:T(8,128)S(1)}, u32[]{:S(2)}, u32[]{:S(2)}) collective-permute-start(f32[9,16,128]{2,1,0:T(8,128)S(1)} %get-tuple-element.23), channel_id=1, source_target_pairs={{0,1},{1,0},{2,3},{3,2},{4,5},{5,4},{6,7},{7,6},{8,9},{9,8},{10,11... | collective-permute-start | bytes 221192 | tf_op jit(solution)/shard_map/ppermute | solution.py:380

commit v4 on v3

--- a/solution.py
+++ b/solution.py
@@ -31,36 +31,50 @@
     return lax.rem(index, 2) == 1
 
 
-def load_kernel(psi_ref, trap_ref, packed_ref, field_ref, sems):
+def load_kernel(psi_ref, trap_ref, s1_ref, s2_ref, field_ref, sems):
     rows, depth = trap_ref.shape[:2]
-    half_rows = rows // 2
-    copies = (
-        pltpu.make_async_copy(psi_ref, field_ref.at[0:2], sems.at[0]),
-        pltpu.make_async_copy(trap_ref, field_ref.at[2], sems.at[1]),
-    )
-    for copy in copies:
-        copy.start()
-    for copy in copies:
-        copy.wait()
+    half_rows, part_rows = rows // 2, rows // 2
+    copies = []
+    for part in range(2):
+        at = pl.ds(part * part_rows, part_rows)
+        pair = (
+            pltpu.make_async_copy(psi_ref.at[:, at], field_ref.at[0:2, at], sems.at[part, 0]),
+            pltpu.make_async_copy(trap_ref.at[at], field_ref.at[2, at], sems.at[part, 1]),
+        )
+        for copy in pair:
+            copy.start()
+        copies.append(pair)
     group = lanes((depth, 128)) // 8
-    for half in range(2):
-        packs = [jnp.zeros((depth, 128), jnp.float32)] * 3
-        for g in range(half_rows):
-            row = half * half_rows + g
-            re, im = field_ref[0, row], field_ref[1, row]
-            diag = field_ref[2, row] + COUPLING * (re * re + im * im) + DIAGONAL
-            field_ref[2, row] = diag
-            for f, field in enumerate((re, im, diag)):
-                moved = pltpu.roll(field, (8 * g + HALO) % 128, 1)
-                packs[f] = jnp.where(group == g, moved, packs[f])
-        for f in range(3):
-            packed_ref[f, half] = packs[f]
+    packs = [[jnp.zeros((depth, 128), jnp.float32)] * 2 for _ in range(3)]
+    for row in range(rows):
+        half, g = divmod(row, half_rows)
+        if g == 0:
+            for copy in copies[half]:
+                copy.wait()
+        re, im = field_ref[0, row], field_ref[1, row]
+        diag = field_ref[2, row] + COUPLING * (re * re + im * im) + DIAGONAL
+        field_ref[2, row] = diag
+        for f, field in enumerate((re, im, diag)):
+            moved = pltpu.roll(field, (8 * g + HALO) % 128, 1)
+            packs[f][half] = jnp.where(group == g, moved, packs[f][half])
+    first = lanes((depth, 128)) % 8 < HALO
+    odd = is_odd(position()[1])
+    for f in range(3):
+        low, high = packs[f]
+        to_right = jnp.where(first, low, pltpu.roll(high, HALO, 1))
+        to_left = jnp.where(first, pltpu.roll(low, 128 - HALO, 1), high)
+        s1_ref[f] = jnp.where(odd, to_left, to_right)
+        s2_ref[f] = jnp.where(odd, to_right, to_left)
 
 
 def merged(y1_ref, y2_ref, f, half):
-    odd = is_odd(position()[1]).astype(jnp.int32)
-    left = (lanes(y1_ref.shape[2:]) % 8 < HALO).astype(jnp.int32)
-    return jnp.where(left == odd, y1_ref[f, half], y2_ref[f, half])
+    odd = is_odd(position()[1])
+    first = lanes(y1_ref.shape[1:]) % 8 < HALO
+    left = jnp.where(odd, y1_ref[f], y2_ref[f])
+    right = jnp.where(odd, y2_ref[f], y1_ref[f])
+    if half:
+        return jnp.where(first, pltpu.roll(left, 128 - HALO, 1), right)
+    return jnp.where(first, left, pltpu.roll(right, HALO, 1))
 
 
 def spread(pack, g):
@@ -173,7 +187,7 @@
         for i, part in enumerate(parts):
             sums[j + i] += part
 
-    for high in (False, True):
+    def end(high):
         own = (lambda i: rows - 1 + HALO - i) if high else (lambda i: i - HALO)
         there = (tile < tiles - 1) if high else (tile > 0)
         keep = jnp.where(there, inside, 0.0)
@@ -213,15 +227,19 @@
         def at(source, i):
             return [source[c][i] for c in range(2)]
 
+        yield
         u1 = cut(powers(v, 1, HALO + 1))
+        yield
         for c in range(2):
             for i in range(HALO + 1, HALO + 3):
                 u1[c][i] = u1_ref[c, own(i)]
         u2 = cut(powers(u1, 2, HALO + 2))
+        yield
         for c in range(2):
             for i in range(HALO + 2, HALO + 4):
                 u2[c][i] = u2_ref[c, own(i)]
         u3 = powers(u2, HALO, HALO + 3)
+        yield
 
         count(0, forms(at(v, HALO), at(v, HALO)))
         count(2, forms(at(v, HALO), at(u1, HALO)))
@@ -235,6 +253,10 @@
             b1_ref[c, 1 if high else 0] = u1[c][HALO][:, 0:128]
             for i in range(2):
                 b2_ref[c, 3 - i if high else i] = u2[c][HALO + i][:, 0:128]
+        yield
+
+    for _ in zip(end(False), end(True)):
+        pass
 
     lane = lanes((1, 128))
     line = jnp.zeros((1, 128), jnp.float32)
@@ -365,13 +387,14 @@
     f32 = functools.partial(jax.ShapeDtypeStruct, dtype=jnp.float32)
 
     psi, trap = (pltpu.with_memory_space_constraint(x, pltpu.HBM) for x in (psi, trap))
-    packed, field = call(
-        load_kernel, (f32((3, 2, depth, 128)), f32((3, rows, depth, width))), [ANYWHERE] * 2,
-        [pltpu.SemaphoreType.DMA((2,))],
+    message = f32((3, depth, 128))
+    m1, m2, field = call(
+        load_kernel, (message, message, f32((3, rows, depth, width))), [ANYWHERE] * 2,
+        [pltpu.SemaphoreType.DMA((2, 2))],
     )(psi, trap)
     near, across = swaps("pole")
-    y2 = lax.ppermute(packed, "pole", across)
-    y1 = lax.ppermute(packed, "pole", near)
+    y2 = lax.ppermute(m2, "pole", across)
+    y1 = lax.ppermute(m1, "pole", near)
 
     edge = f32((3 * HALO, depth, 128))
     s1, s2 = call(edge_kernel, (edge, edge), [VMEM] * 3)(field, y1, y2)

time: 40.4 us -> 40.3 us (level)
  blocking collectives: 22.5 us -> 21.8 us
    all_to_all x1, blocking collectives: 22.5 us -> 21.8 us  [on_device(): lax.all_to_all(line.reshape(devices, 1, 128), ('pole', 'tile'), 0, 0, til...]
where the time goes in v4:
time: 40.3 us; the launch traced here: 40.1 us
  blocking collectives  21.8 us (54%)
  starting transfers between devices  9.94 us (25%)
  Pallas kernels  6.27 us (16%)
  waiting for transfers between devices  2.02 us (5%)
    all_to_all x1, blocking collectives, on_device(): lax.all_to_all(line.reshape(devices, 1, 128), ('pole', 'tile'), 0, 0, til...  21.8 us
    ppermute x1, starting transfers between devices, on_device(): x1 = lax.ppermute(s1, 'tile', near)  4.68 us
    ppermute x1, starting transfers between devices, on_device(): y2 = lax.ppermute(m2, 'pole', across)  3.1 us
    pallas_call x1, Pallas kernels, on_device(): call(inner_kernel, (f32((3, rows, depth, 2 * width)), wide, wide, f32((2...  2.74 us
    ppermute x1, waiting for transfers between devices, on_device(): y2 = lax.ppermute(m2, 'pole', across)  2.01 us
    ppermute x1, starting transfers between devices, on_device(): y1 = lax.ppermute(m1, 'pole', near)  1.5 us
    pallas_call x1, Pallas kernels, on_device(): call(load_kernel, (message, message, f32((3, rows, depth, width))), [ANYW...  1.46 us
    pallas_call x1, Pallas kernels, on_device(): call(combine, f32((2, rows, depth, width)), [VMEM] * 6, [pltpu.VMEM((2, r...  1.17 us
  transfers between devices with their start and end apart: 4, of which 1 were waited for; matrix products, arithmetic and copies ran while one was open for 0% of the time, Pallas kernels for 7%

profile of v4, /device:TPU:1, one launch (start us, length us, event | category | flops | bytes accessed | tf_op | source)
XLA Modules:
  0.0 40.1 jit_solution(3234623499800132331)
XLA Ops:
  0.0 0.0 copy-start.1
  0.0 0.0 copy-start
  0.0 1.5 %shard_map.46 = (f32[3,16,128]{2,1,0:T(8,128)S(1)}, f32[3,16,128]{2,1,0:T(8,128)S(1)}, f32[3,32,16,128]{3,2,1,0:T(8,128)S(1)}) custom-call(f32[2,32,16,128]{3,2,1,0:T(8,128)} %psi_ref.1, f32[32,16,128]{2,1,0:T(8,128)} %trap_ref.1), custom_call_target="tpu_custom_call" | custom-call | tf_op jit(solution)/shard_map/pallas_call | solution.py:391
  1.5 1.5 %collective-permute-start = (f32[3,16,128]{2,1,0:T(8,128)S(1)}, f32[3,16,128]{2,1,0:T(8,128)S(1)}, u32[]{:S(2)}, u32[]{:S(2)}) collective-permute-start(f32[3,16,128]{2,1,0:T(8,128)S(1)} %get-tuple-element.18), channel_id=1, source_target_pairs={{0,32},{32,0},{64,96},{96,64},{1,33},{33,1},{65,97},{97,65},{2,34}... | collective-permute-start | bytes 73736 | tf_op jit(solution)/shard_map/ppermute | solution.py:397
  3.0 3.1 %collective-permute-start.1 = (f32[3,16,128]{2,1,0:T(8,128)S(1)}, f32[3,16,128]{2,1,0:T(8,128)S(1)}, u32[]{:S(2)}, u32[]{:S(2)}) collective-permute-start(f32[3,16,128]{2,1,0:T(8,128)S(1)} %get-tuple-element.19), channel_id=1, source_target_pairs={{32,64},{64,32},{33,65},{65,33},{34,66},{66,34},{35,67},{67,35},{3... | collective-permute-start | bytes 73736 | tf_op jit(solution)/shard_map/ppermute | solution.py:396
  6.1 0.0 collective-permute-done.y1_ref
  6.1 2.0 %collective-permute-done.1.y2_ref = f32[3,16,128]{2,1,0:T(8,128)S(1)} collective-permute-done((f32[3,16,128]{2,1,0:T(8,128)S(1)}, f32[3,16,128]{2,1,0:T(8,128)S(1)}, u32[]{:S(2)}, u32[]{:S(2)}) %collective-permute-start.1) | collective-permute-done | bytes 24608 | tf_op jit(solution)/shard_map/ppermute | solution.py:396
  8.1 0.2 shard_map.48
  8.3 0.7 %collective-permute-start.2 = (f32[9,16,128]{2,1,0:T(8,128)S(1)}, f32[9,16,128]{2,1,0:T(8,128)S(1)}, u32[]{:S(2)}, u32[]{:S(2)}) collective-permute-start(f32[9,16,128]{2,1,0:T(8,128)S(1)} %get-tuple-element.24), channel_id=1, source_target_pairs={{1,2},{3,4},{5,6},{7,8},{9,10},{11,12},{13,14},{15,16},{17,18},{19... | collective-permute-start | bytes 221192 | tf_op jit(solution)/shard_map/ppermute | solution.py:402
  8.9 4.7 %collective-permute-start.3 = (f32[9,16,128]{2,1,0:T(8,128)S(1)}, f32[9,16,128]{2,1,0:T(8,128)S(1)}, u32[]{:S(2)}, u32[]{:S(2)}) collective-permute-start(f32[9,16,128]{2,1,0:T(8,128)S(1)} %get-tuple-element.25), channel_id=1, source_target_pairs={{0,1},{1,0},{2,3},{3,2},{4,5},{5,4},{6,7},{7,6},{8,9},{9,8},{10,11... | collective-permute-start | bytes 221192 | tf_op jit(solution)/shard_map/ppermute | solution.py:403
  13.6 2.7 %shard_map.47 = (f32[3,32,16,256]{3,2,1,0:T(8,128)S(1)}, f32[2,32,16,256]{3,2,1,0:T(8,128)S(1)}, f32[2,32,16,256]{3,2,1,0:T(8,128)S(1)}, f32[12,8,128]{2,1,0:T(8,128)S(1)}) custom-call(f32[3,32,16,128]{3,2,1,0:T(8,128)S(1)} %get-tuple-element.17.field_ref, f32[3,16,128]{2,1,0:T(8,128)S(1)} %collective-permute-done.y1_ref, ...), custom_call_target="tpu_custom_call" | custom-call | flops 20000000 | bytes 8000000 | tf_op jit(solution)/shard_map/pallas_call | solution.py:406
  16.4 0.0 collective-permute-done.2.x2_ref
  16.4 0.0 collective-permute-done.3.x1_ref
  16.4 0.0 copy-done.1
  16.4 0.0 copy-done
  16.4 0.7 %shard_map.49 = (f32[2,2,16,128]{3,2,1,0:T(8,128)S(1)}, f32[2,4,16,128]{3,2,1,0:T(8,128)S(1)}, f32[128,128]{1,0:T(8,128)S(1)}) custom-call(f32[2,2]{1,0:T(2,128)S(1)} %copy-done, f32[2,2]{1,0:T(2,128)S(1)} %copy-done.1, f32[3,32,16,256]{3,2,1,0:T(8,128)S(1)} %get-tuple-element.22.grown_ref, f32[2,32,16,256]{3,2,1,0:T(8,128)S(1)} %get-tuple-element.20.u1_ref, ...), custom_call_target="tpu_custom_call" | custom-call | tf_op jit(solution)/shard_map/pallas_call | solution.py:412
  17.1 21.8 %all_to_all.5 = f32[128,1,128]{2,1,0:T(1,128)S(1)} all-to-all(f32[128,1,128]{2,1,0:T(1,128)S(1)} %bitcast.5), channel_id=1, replica_groups=mesh['pole'=4,'tile'=32] {'pole','tile'}, dimensions={0} | all-to-all | bytes 131072 | tf_op jit(solution)/shard_map/all_to_all | solution.py:418
  39.0 1.2 %shard_map.50 = f32[2,32,16,128]{3,2,1,0:T(8,128)} custom-call(f32[3,32,16,128]{3,2,1,0:T(8,128)S(1)} %get-tuple-element.17.field_ref, f32[2,32,16,256]{3,2,1,0:T(8,128)S(1)} %get-tuple-element.20.u1_ref, f32[2,32,16,256]{3,2,1,0:T(8,128)S(1)} %get-tuple-element.21.u2_ref, f32[2,2,16,128]{3,2,1,0:T(8,128)S(1)} %get-tuple-element.26.b1_ref, ...), custom_call_target="tpu_custom_call" | custom-call | tf_op jit(solution)/shard_map/pallas_call | solution.py:420
Async XLA Ops:
  0.0 16.4 %copy-start.1 = (f32[2,2]{1,0:T(2,128)S(1)}, f32[2,2]{1,0:T(2,128)}, u32[]{:S(2)}) copy-start(f32[2,2]{1,0:T(2,128)} %weight_ref.1) | copy-start | bytes 52
  0.0 16.4 %copy-start = (f32[2,2]{1,0:T(2,128)S(1)}, f32[2,2]{1,0:T(2,128)}, u32[]{:S(2)}) copy-start(f32[2,2]{1,0:T(2,128)} %shift_ref.1) | copy-start | bytes 52
  1.5 4.6 %collective-permute-start = (f32[3,16,128]{2,1,0:T(8,128)S(1)}, f32[3,16,128]{2,1,0:T(8,128)S(1)}, u32[]{:S(2)}, u32[]{:S(2)}) collective-permute-start(f32[3,16,128]{2,1,0:T(8,128)S(1)} %get-tuple-element.18), channel_id=1, source_target_pairs={{0,32},{32,0},{64,96},{96,64},{1,33},{33,1},{65,97},{97,65},{2,34}... | collective-permute-start | bytes 73736 | tf_op jit(solution)/shard_map/ppermute | solution.py:397
  3.0 5.1 %collective-permute-start.1 = (f32[3,16,128]{2,1,0:T(8,128)S(1)}, f32[3,16,128]{2,1,0:T(8,128)S(1)}, u32[]{:S(2)}, u32[]{:S(2)}) collective-permute-start(f32[3,16,128]{2,1,0:T(8,128)S(1)} %get-tuple-element.19), channel_id=1, source_target_pairs={{32,64},{64,32},{33,65},{65,33},{34,66},{66,34},{35,67},{67,35},{3... | collective-permute-start | bytes 73736 | tf_op jit(solution)/shard_map/ppermute | solution.py:396
  8.3 8.1 %collective-permute-start.2 = (f32[9,16,128]{2,1,0:T(8,128)S(1)}, f32[9,16,128]{2,1,0:T(8,128)S(1)}, u32[]{:S(2)}, u32[]{:S(2)}) collective-permute-start(f32[9,16,128]{2,1,0:T(8,128)S(1)} %get-tuple-element.24), channel_id=1, source_target_pairs={{1,2},{3,4},{5,6},{7,8},{9,10},{11,12},{13,14},{15,16},{17,18},{19... | collective-permute-start | bytes 221192 | tf_op jit(solution)/shard_map/ppermute | solution.py:402
  8.9 7.4 %collective-permute-start.3 = (f32[9,16,128]{2,1,0:T(8,128)S(1)}, f32[9,16,128]{2,1,0:T(8,128)S(1)}, u32[]{:S(2)}, u32[]{:S(2)}) collective-permute-start(f32[9,16,128]{2,1,0:T(8,128)S(1)} %get-tuple-element.25), channel_id=1, source_target_pairs={{0,1},{1,0},{2,3},{3,2},{4,5},{5,4},{6,7},{7,6},{8,9},{9,8},{10,11... | collective-permute-start | bytes 221192 | tf_op jit(solution)/shard_map/ppermute | solution.py:403

commit v5 on v4

--- a/solution.py
+++ b/solution.py
@@ -70,8 +70,9 @@
 def merged(y1_ref, y2_ref, f, half):
     odd = is_odd(position()[1])
     first = lanes(y1_ref.shape[1:]) % 8 < HALO
-    left = jnp.where(odd, y1_ref[f], y2_ref[f])
-    right = jnp.where(odd, y2_ref[f], y1_ref[f])
+    pole, poles = position()[1], lax.axis_size("pole")
+    left = jnp.where(odd, y1_ref[f], y2_ref[f]) * (pole > 0).astype(jnp.float32)
+    right = jnp.where(odd, y2_ref[f], y1_ref[f]) * (pole < poles - 1).astype(jnp.float32)
     if half:
         return jnp.where(first, pltpu.roll(left, 128 - HALO, 1), right)
     return jnp.where(first, left, pltpu.roll(right, HALO, 1))
@@ -200,7 +201,7 @@
             value = jnp.concatenate([jnp.where(even, near[item], far[item]), spread(sides, item)], axis=1)
             place = HALO - 1 - row if high else row - (rows - HALO)
             if f < 2:
-                v[f][place] = value
+                v[f][place] = value * there.astype(jnp.float32)
             else:
                 diag[place] = value
         for i in range(HALO, 2 * HALO):
@@ -377,8 +378,7 @@
 
 def swaps(axis):
     size = lax.axis_size(axis)
-    gaps = [(i, i + 1) for i in range(1, size - 1, 2)]
-    return [(i, i ^ 1) for i in range(size)], gaps + [(b, a) for a, b in gaps]
+    return [(i, i ^ 1) for i in range(size)], [(i, (i + 1 - 2 * (i % 2 == 0)) % size) for i in range(size)]
 
 
 def on_device(psi, trap, pole_shift, pole_weight):

time: 40.3 us -> 38.2 us (0.948)
  blocking collectives: 21.8 us -> 17.7 us
  starting transfers between devices: 9.94 us -> 11.6 us
    ppermute x1, starting transfers between devices: 0.66 us -> 8.81 us  [on_device(): x2 = lax.ppermute(s2, 'tile', across)]
    ppermute x1, starting transfers between devices: 4.68 us -> 0.01 us  [on_device(): x1 = lax.ppermute(s1, 'tile', near)]
    all_to_all x1, blocking collectives: 21.8 us -> 17.7 us  [on_device(): lax.all_to_all(line.reshape(devices, 1, 128), ('pole', 'tile'), 0, 0, til...]
    ppermute x1, starting transfers between devices: 3.1 us -> 1.27 us  [on_device(): y2 = lax.ppermute(m2, 'pole', across)]
    ppermute x1, waiting for transfers between devices: 0.01 us -> 0.43 us  [on_device(): x1 = lax.ppermute(s1, 'tile', near)]
  transfers between devices with their start and end apart: 4 -> 4, of which waited for: 1 -> 2; matrix products, arithmetic and copies ran while one was open for 0% -> 0% of each run, Pallas kernels for 7% -> 7%
where the time goes in v5:
time: 38.2 us; the launch traced here: 38.1 us
  blocking collectives  17.7 us (46%)
  starting transfers between devices  11.6 us (30%)
  Pallas kernels  6.28 us (16%)
  waiting for transfers between devices  2.42 us (6%)
    all_to_all x1, blocking collectives, on_device(): lax.all_to_all(line.reshape(devices, 1, 128), ('pole', 'tile'), 0, 0, til...  17.7 us
    ppermute x1, starting transfers between devices, on_device(): x2 = lax.ppermute(s2, 'tile', across)  8.81 us
    pallas_call x1, Pallas kernels, on_device(): call(inner_kernel, (f32((3, rows, depth, 2 * width)), wide, wide, f32((2...  2.75 us
    ppermute x1, waiting for transfers between devices, on_device(): y2 = lax.ppermute(m2, 'pole', across)  1.99 us
    ppermute x1, starting transfers between devices, on_device(): y1 = lax.ppermute(m1, 'pole', near)  1.5 us
    pallas_call x1, Pallas kernels, on_device(): call(load_kernel, (message, message, f32((3, rows, depth, width))), [ANYW...  1.46 us
    ppermute x1, starting transfers between devices, on_device(): y2 = lax.ppermute(m2, 'pole', across)  1.27 us
    pallas_call x1, Pallas kernels, on_device(): call(combine, f32((2, rows, depth, width)), [VMEM] * 6, [pltpu.VMEM((2, r...  1.17 us
  transfers between devices with their start and end apart: 4, of which 2 were waited for; matrix products, arithmetic and copies ran while one was open for 0% of the time, Pallas kernels for 7%

profile of v5, /device:TPU:1, one launch (start us, length us, event | category | flops | bytes accessed | tf_op | source)
XLA Modules:
  0.0 38.1 jit_solution(2344262718834172261)
XLA Ops:
  0.0 0.0 copy-start.1
  0.0 0.0 copy-start
  0.0 1.5 %shard_map.46 = (f32[3,16,128]{2,1,0:T(8,128)S(1)}, f32[3,16,128]{2,1,0:T(8,128)S(1)}, f32[3,32,16,128]{3,2,1,0:T(8,128)S(1)}) custom-call(f32[2,32,16,128]{3,2,1,0:T(8,128)} %psi_ref.1, f32[32,16,128]{2,1,0:T(8,128)} %trap_ref.1), custom_call_target="tpu_custom_call" | custom-call | tf_op jit(solution)/shard_map/pallas_call | solution.py:391
  1.5 1.5 %collective-permute-start = (f32[3,16,128]{2,1,0:T(8,128)S(1)}, f32[3,16,128]{2,1,0:T(8,128)S(1)}, u32[]{:S(2)}, u32[]{:S(2)}) collective-permute-start(f32[3,16,128]{2,1,0:T(8,128)S(1)} %get-tuple-element.18), channel_id=1, source_target_pairs={{0,32},{32,0},{64,96},{96,64},{1,33},{33,1},{65,97},{97,65},{2,34}... | collective-permute-start | bytes 73736 | tf_op jit(solution)/shard_map/ppermute | solution.py:397
  3.0 1.3 %collective-permute-start.1 = (f32[3,16,128]{2,1,0:T(8,128)S(1)}, f32[3,16,128]{2,1,0:T(8,128)S(1)}, u32[]{:S(2)}, u32[]{:S(2)}) collective-permute-start(f32[3,16,128]{2,1,0:T(8,128)S(1)} %get-tuple-element.19), channel_id=1, source_target_pairs={{0,96},{32,64},{64,32},{96,0},{1,97},{33,65},{65,33},{97,1},{2,98}... | collective-permute-start | bytes 73736 | tf_op jit(solution)/shard_map/ppermute | solution.py:396
  4.2 0.0 collective-permute-done.y1_ref
  4.3 2.0 %collective-permute-done.1.y2_ref = f32[3,16,128]{2,1,0:T(8,128)S(1)} collective-permute-done((f32[3,16,128]{2,1,0:T(8,128)S(1)}, f32[3,16,128]{2,1,0:T(8,128)S(1)}, u32[]{:S(2)}, u32[]{:S(2)}) %collective-permute-start.1) | collective-permute-done | bytes 24608 | tf_op jit(solution)/shard_map/ppermute | solution.py:396
  6.2 0.2 shard_map.48
  6.4 8.8 %collective-permute-start.2 = (f32[9,16,128]{2,1,0:T(8,128)S(1)}, f32[9,16,128]{2,1,0:T(8,128)S(1)}, u32[]{:S(2)}, u32[]{:S(2)}) collective-permute-start(f32[9,16,128]{2,1,0:T(8,128)S(1)} %get-tuple-element.24), channel_id=1, source_target_pairs={{0,31},{1,2},{2,1},{3,4},{4,3},{5,6},{6,5},{7,8},{8,7},{9,10},{10,... | collective-permute-start | bytes 221192 | tf_op jit(solution)/shard_map/ppermute | solution.py:402
  15.2 0.0 collective-permute-start.3
  15.2 2.8 %shard_map.47 = (f32[3,32,16,256]{3,2,1,0:T(8,128)S(1)}, f32[2,32,16,256]{3,2,1,0:T(8,128)S(1)}, f32[2,32,16,256]{3,2,1,0:T(8,128)S(1)}, f32[12,8,128]{2,1,0:T(8,128)S(1)}) custom-call(f32[3,32,16,128]{3,2,1,0:T(8,128)S(1)} %get-tuple-element.17.field_ref, f32[3,16,128]{2,1,0:T(8,128)S(1)} %collective-permute-done.y1_ref, ...), custom_call_target="tpu_custom_call" | custom-call | flops 20000000 | bytes 8000000 | tf_op jit(solution)/shard_map/pallas_call | solution.py:406
  18.0 0.0 collective-permute-done.2.x2_ref
  18.0 0.4 %collective-permute-done.3.x1_ref = f32[9,16,128]{2,1,0:T(8,128)S(1)} collective-permute-done((f32[9,16,128]{2,1,0:T(8,128)S(1)}, f32[9,16,128]{2,1,0:T(8,128)S(1)}, u32[]{:S(2)}, u32[]{:S(2)}) %collective-permute-start.3) | collective-permute-done | bytes 73760 | tf_op jit(solution)/shard_map/ppermute | solution.py:403
  18.4 0.0 copy-done.1
  18.4 0.0 copy-done
  18.4 0.7 %shard_map.49 = (f32[2,2,16,128]{3,2,1,0:T(8,128)S(1)}, f32[2,4,16,128]{3,2,1,0:T(8,128)S(1)}, f32[128,128]{1,0:T(8,128)S(1)}) custom-call(f32[2,2]{1,0:T(2,128)S(1)} %copy-done, f32[2,2]{1,0:T(2,128)S(1)} %copy-done.1, f32[3,32,16,256]{3,2,1,0:T(8,128)S(1)} %get-tuple-element.22.grown_ref, f32[2,32,16,256]{3,2,1,0:T(8,128)S(1)} %get-tuple-element.20.u1_ref, ...), custom_call_target="tpu_custom_call" | custom-call | tf_op jit(solution)/shard_map/pallas_call | solution.py:412
  19.2 17.7 %all_to_all.5 = f32[128,1,128]{2,1,0:T(1,128)S(1)} all-to-all(f32[128,1,128]{2,1,0:T(1,128)S(1)} %bitcast.5), channel_id=1, replica_groups=mesh['pole'=4,'tile'=32] {'pole','tile'}, dimensions={0} | all-to-all | bytes 131072 | tf_op jit(solution)/shard_map/all_to_all | solution.py:418
  36.9 1.2 %shard_map.50 = f32[2,32,16,128]{3,2,1,0:T(8,128)} custom-call(f32[3,32,16,128]{3,2,1,0:T(8,128)S(1)} %get-tuple-element.17.field_ref, f32[2,32,16,256]{3,2,1,0:T(8,128)S(1)} %get-tuple-element.20.u1_ref, f32[2,32,16,256]{3,2,1,0:T(8,128)S(1)} %get-tuple-element.21.u2_ref, f32[2,2,16,128]{3,2,1,0:T(8,128)S(1)} %get-tuple-element.26.b1_ref, ...), custom_call_target="tpu_custom_call" | custom-call | tf_op jit(solution)/shard_map/pallas_call | solution.py:420
Async XLA Ops:
  0.0 18.4 %copy-start.1 = (f32[2,2]{1,0:T(2,128)S(1)}, f32[2,2]{1,0:T(2,128)}, u32[]{:S(2)}) copy-start(f32[2,2]{1,0:T(2,128)} %weight_ref.1) | copy-start | bytes 52
  0.0 18.4 %copy-start = (f32[2,2]{1,0:T(2,128)S(1)}, f32[2,2]{1,0:T(2,128)}, u32[]{:S(2)}) copy-start(f32[2,2]{1,0:T(2,128)} %shift_ref.1) | copy-start | bytes 52
  1.5 2.8 %collective-permute-start = (f32[3,16,128]{2,1,0:T(8,128)S(1)}, f32[3,16,128]{2,1,0:T(8,128)S(1)}, u32[]{:S(2)}, u32[]{:S(2)}) collective-permute-start(f32[3,16,128]{2,1,0:T(8,128)S(1)} %get-tuple-element.18), channel_id=1, source_target_pairs={{0,32},{32,0},{64,96},{96,64},{1,33},{33,1},{65,97},{97,65},{2,34}... | collective-permute-start | bytes 73736 | tf_op jit(solution)/shard_map/ppermute | solution.py:397
  3.0 3.3 %collective-permute-start.1 = (f32[3,16,128]{2,1,0:T(8,128)S(1)}, f32[3,16,128]{2,1,0:T(8,128)S(1)}, u32[]{:S(2)}, u32[]{:S(2)}) collective-permute-start(f32[3,16,128]{2,1,0:T(8,128)S(1)} %get-tuple-element.19), channel_id=1, source_target_pairs={{0,96},{32,64},{64,32},{96,0},{1,97},{33,65},{65,33},{97,1},{2,98}... | collective-permute-start | bytes 73736 | tf_op jit(solution)/shard_map/ppermute | solution.py:396
  6.4 11.6 %collective-permute-start.2 = (f32[9,16,128]{2,1,0:T(8,128)S(1)}, f32[9,16,128]{2,1,0:T(8,128)S(1)}, u32[]{:S(2)}, u32[]{:S(2)}) collective-permute-start(f32[9,16,128]{2,1,0:T(8,128)S(1)} %get-tuple-element.24), channel_id=1, source_target_pairs={{0,31},{1,2},{2,1},{3,4},{4,3},{5,6},{6,5},{7,8},{8,7},{9,10},{10,... | collective-permute-start | bytes 221192 | tf_op jit(solution)/shard_map/ppermute | solution.py:402
  15.2 3.2 %collective-permute-start.3 = (f32[9,16,128]{2,1,0:T(8,128)S(1)}, f32[9,16,128]{2,1,0:T(8,128)S(1)}, u32[]{:S(2)}, u32[]{:S(2)}) collective-permute-start(f32[9,16,128]{2,1,0:T(8,128)S(1)} %get-tuple-element.25), channel_id=1, source_target_pairs={{0,1},{1,0},{2,3},{3,2},{4,5},{5,4},{6,7},{7,6},{8,9},{9,8},{10,11... | collective-permute-start | bytes 221192 | tf_op jit(solution)/shard_map/ppermute | solution.py:403

commit v6 on v5

--- a/solution.py
+++ b/solution.py
@@ -82,29 +82,56 @@
     return pltpu.roll(pack, (128 - HALO - 8 * g) % 128, 1)
 
 
-def edge_items(rows, high):
-    start = rows - HALO if high else 0
+def cell(re, im, trap):
+    return trap + COUPLING * (re * re + im * im) + DIAGONAL
+
+
+def edge_items(high):
     skip = 1 if high else 0
-    return [(f, start + i) for f in range(2) for i in range(HALO)] + [(2, start + skip + i) for i in range(HALO - 1)]
-
-
-def edge_kernel(field_ref, y1_ref, y2_ref, s1_ref, s2_ref):
-    rows, depth = field_ref.shape[1:3]
+    return [(f, i) for f in range(2) for i in range(HALO)] + [(2, skip + i) for i in range(HALO - 1)]
+
+
+def end_kernel(psi_ref, trap_ref, s2_ref, s1_ref, raw, sems):
+    rows = trap_ref.shape[0]
+    copies = []
+    for end in range(2):
+        at = pl.ds((rows - HALO) * end, HALO)
+        copies.append(pltpu.make_async_copy(psi_ref.at[:, at], raw.at[end, 0:2], sems.at[end, 0]))
+        copies.append(pltpu.make_async_copy(trap_ref.at[at], raw.at[end, 2], sems.at[end, 1]))
+    for copy in copies:
+        copy.start()
+    for copy in copies:
+        copy.wait()
+    even = jnp.logical_not(is_odd(position()[0]))
+    for item, pair in enumerate(zip(edge_items(False), edge_items(True))):
+        low, high = (
+            raw[end, f, i] if f < 2 else cell(raw[end, 0, i], raw[end, 1, i], raw[end, 2, i])
+            for end, (f, i) in enumerate(pair)
+        )
+        s1_ref[item] = jnp.where(even, high, low)
+        s2_ref[item] = jnp.where(even, low, high)
+
+
+def corner_kernel(x2_ref, x1_ref, corner_ref):
+    items, depth = x1_ref.shape[:2]
     even = jnp.logical_not(is_odd(position()[0]))
     group = lanes((depth, 128)) // 8
-    ends = []
+    pack = jnp.zeros((depth, 128), jnp.float32)
     for high in (False, True):
-        items = edge_items(rows, high)
-        sides = jnp.zeros((depth, 128), jnp.float32)
-        for f, first in ((0, 0), (1, HALO), (2, 2 * HALO)):
-            row = items[first][1]
-            pack = merged(y1_ref, y2_ref, f, row // 16)
-            moved = pltpu.roll(pack, (8 * (first - row)) % 128, 1)
-            sides = jnp.where(group >= first, moved, sides)
-        ends.append([field_ref[f, row] for f, row in items] + [sides])
-    for i, (low, high) in enumerate(zip(*ends)):
-        s1_ref[i] = jnp.where(even, high, low)
-        s2_ref[i] = jnp.where(even, low, high)
+        near, far = (x1_ref, x2_ref) if high else (x2_ref, x1_ref)
+        for item in range(items):
+            g = items + item if high else item
+            moved = pltpu.roll(jnp.where(even, near[item], far[item]), (8 * g + HALO) % 128, 1)
+            pack = jnp.where(group == g, moved, pack)
+    corner_ref[...] = pack
+
+
+def merged_corners(c1_ref, c2_ref):
+    pole, poles = position()[1], lax.axis_size("pole")
+    odd = is_odd(pole).astype(jnp.int32)
+    first = lanes(c1_ref.shape) % 8 < HALO
+    inside = jnp.where(first, (pole > 0).astype(jnp.float32), (pole < poles - 1).astype(jnp.float32))
+    return jnp.where(first.astype(jnp.int32) == odd, c1_ref[...], c2_ref[...]) * inside
 
 
 def neighbours_z(b):
@@ -145,7 +172,23 @@
     return fold(a[0] * b[0] - a[1] * b[1]), fold(a[0] * b[1] + a[1] * b[0])
 
 
-def inner_kernel(field_ref, y1_ref, y2_ref, grown_ref, u1_ref, u2_ref, sums_ref):
+def sweep(source, target, diag_ref, inside, reach):
+    rows = source.shape[1]
+
+    def step(i, sums):
+        x = reach + i
+        old = [source[c, x] for c in range(2)]
+        new = [image(source[c, x - 1], old[c], source[c, x + 1], diag_ref[2, x], inside) for c in range(2)]
+        if target is not None:
+            for c in range(2):
+                target[c, x] = new[c]
+        return tuple(a + b for a, b in zip(sums, forms(old, old) + forms(old, new)))
+
+    zero = jnp.zeros((8, 128), jnp.float32)
+    return lax.fori_loop(0, rows - 2 * reach, step, (zero,) * 4, unroll=True)
+
+
+def first_kernel(field_ref, y1_ref, y2_ref, grown_ref, u1_ref, sums_ref):
     rows, depth = field_ref.shape[1:3]
     for half in range(2):
         packs = [merged(y1_ref, y2_ref, f, half) for f in range(3)]
@@ -155,34 +198,29 @@
                 grown_ref[f, row, :, 0:128] = field_ref[f, row]
                 grown_ref[f, row, :, 128:256] = spread(packs[f], g)
     inside = inside_mask(depth)
-
-    def sweep(source, target, reach):
-        def step(i, sums):
-            x = reach + i
-            old = [source[c, x] for c in range(2)]
-            new = [image(source[c, x - 1], old[c], source[c, x + 1], grown_ref[2, x], inside) for c in range(2)]
-            if target is not None:
-                for c in range(2):
-                    target[c, x] = new[c]
-            return tuple(a + b for a, b in zip(sums, forms(old, old) + forms(old, new)))
-
-        zero = jnp.zeros((8, 128), jnp.float32)
-        return lax.fori_loop(0, rows - 2 * reach, step, (zero,) * 4, unroll=True)
-
-    sums = sweep(grown_ref, u1_ref, 1) + sweep(u1_ref, u2_ref, 2) + sweep(u2_ref, None, 3)
+    sums = sweep(grown_ref, u1_ref, grown_ref, inside, 1)
     for j, part in enumerate(sums):
         sums_ref[j] = part
 
 
+def second_kernel(grown_ref, u1_ref, u2_ref, sums_ref):
+    inside = inside_mask(grown_ref.shape[2])
+    sums = sweep(u1_ref, u2_ref, grown_ref, inside, 2) + sweep(u2_ref, None, grown_ref, inside, 3)
+    for j, part in enumerate(sums):
+        sums_ref[j] = part
+
+
 def outer_kernel(
-    shift_ref, weight_ref, grown_ref, u1_ref, u2_ref, sums_ref, x2_ref, x1_ref, b1_ref, b2_ref, line_ref,
+    shift_ref, weight_ref, grown_ref, u1_ref, u2_ref, sums1_ref, sums2_ref, x2_ref, x1_ref, c2_ref, c1_ref,
+    b1_ref, b2_ref, line_ref,
 ):
     rows, depth = grown_ref.shape[1:3]
     tile, pole = position()
     tiles = lax.axis_size("tile")
     even = jnp.logical_not(is_odd(tile))
     inside = inside_mask(depth)
-    sums = [sums_ref[j] for j in range(2 * MOMENTS)]
+    sums = [ref[j] for ref in (sums1_ref, sums2_ref) for j in range(ref.shape[0])]
+    corners = merged_corners(c1_ref, c2_ref)
 
     def count(j, parts):
         for i, part in enumerate(parts):
@@ -195,11 +233,12 @@
         keep = jnp.concatenate([jnp.broadcast_to(there.astype(jnp.float32), inside.shape), keep], axis=1)
         ones = jnp.concatenate([jnp.ones_like(inside), inside], axis=1)
         near, far = (x1_ref, x2_ref) if high else (x2_ref, x1_ref)
-        sides = jnp.where(even, near[8], far[8])
         v, diag = [{}, {}], {}
-        for item, (f, row) in enumerate(edge_items(rows, not high)):
-            value = jnp.concatenate([jnp.where(even, near[item], far[item]), spread(sides, item)], axis=1)
-            place = HALO - 1 - row if high else row - (rows - HALO)
+        items = edge_items(not high)
+        for item, (f, i) in enumerate(items):
+            side = spread(corners, len(items) + item if high else item)
+            value = jnp.concatenate([jnp.where(even, near[item], far[item]), side], axis=1)
+            place = HALO - 1 - i if high else i
             if f < 2:
                 v[f][place] = value * there.astype(jnp.float32)
             else:
@@ -387,33 +426,49 @@
     f32 = functools.partial(jax.ShapeDtypeStruct, dtype=jnp.float32)
 
     psi, trap = (pltpu.with_memory_space_constraint(x, pltpu.HBM) for x in (psi, trap))
+    edge = f32((3 * HALO - 1, depth, width))
+    s2, s1 = call(
+        end_kernel, (edge, edge), [ANYWHERE] * 2,
+        [pltpu.VMEM((2, 3, HALO, depth, width), jnp.float32), pltpu.SemaphoreType.DMA((2, 2))],
+    )(psi, trap)
+    near, across = swaps("tile")
+    pairs = []
+    for pole in range(poles):
+        for tile, other in across:
+            pairs.append((pole * tiles + tile, (pole * tiles + other) if abs(tile - other) == 1 else ((pole ^ 1) * tiles + tile)))
+    x2 = lax.ppermute(s2, ("pole", "tile"), pairs)
+    x1 = lax.ppermute(s1, "tile", near)
+
     message = f32((3, depth, 128))
     m1, m2, field = call(
         load_kernel, (message, message, f32((3, rows, depth, width))), [ANYWHERE] * 2,
         [pltpu.SemaphoreType.DMA((2, 2))],
     )(psi, trap)
-    near, across = swaps("pole")
-    y2 = lax.ppermute(m2, "pole", across)
-    y1 = lax.ppermute(m1, "pole", near)
-
-    edge = f32((3 * HALO, depth, 128))
-    s1, s2 = call(edge_kernel, (edge, edge), [VMEM] * 3)(field, y1, y2)
-    near, across = swaps("tile")
-    x2 = lax.ppermute(s2, "tile", across)
-    x1 = lax.ppermute(s1, "tile", near)
+    pole_near, pole_across = swaps("pole")
+    y2 = lax.ppermute(m2, "pole", pole_across)
+    y1 = lax.ppermute(m1, "pole", pole_near)
 
     wide = f32((2, rows, depth, 2 * width))
-    grown, u1, u2, sums = call(
-        inner_kernel,
-        (f32((3, rows, depth, 2 * width)), wide, wide, f32((2 * MOMENTS, 8, 128))),
-        [VMEM] * 3, flops=20_000_000, bytes_accessed=8_000_000,
+    grown, u1, sums1 = call(
+        first_kernel,
+        (f32((3, rows, depth, 2 * width)), wide, f32((4, 8, 128))),
+        [VMEM] * 3, flops=8_000_000, bytes_accessed=3_000_000,
     )(field, y1, y2)
+    x2, x1, sums1 = lax.optimization_barrier((x2, x1, sums1))
+    corner = call(corner_kernel, f32((depth, 128)), [VMEM] * 2)(x2, x1)
+    c2 = lax.ppermute(corner, "pole", pole_across)
+    c1 = lax.ppermute(corner, "pole", pole_near)
+
+    u2, sums2 = call(
+        second_kernel, (wide, f32((8, 8, 128))), [VMEM] * 2, flops=12_000_000, bytes_accessed=5_000_000,
+    )(grown, u1)
+
     devices = tiles * poles
     b1, b2, line = call(
         outer_kernel,
         (f32((2, 2, depth, width)), f32((2, 4, depth, width)), f32((devices, 128))),
-        [VMEM] * 8,
-    )(pole_shift, pole_weight, grown, u1, u2, sums, x2, x1)
+        [VMEM] * 11,
+    )(pole_shift, pole_weight, grown, u1, u2, sums1, sums2, x2, x1, c2, c1)
 
     lines = lax.all_to_all(line.reshape(devices, 1, 128), ("pole", "tile"), 0, 0, tiled=True)
     combine = functools.partial(combine_kernel, pole_shift.shape[0] * poles)

time: 38.2 us -> 36.4 us (0.953)
  starting transfers between devices: 11.6 us -> 8.37 us
  Pallas kernels: 6.28 us -> 7.17 us
  blocking collectives: 17.7 us -> 18.4 us
    ppermute x3 -> x5, starting transfers between devices: 11.6 us -> 5.69 us  [the longest x1 1.53 us: on_device(): c2 = lax.ppermute(corner, 'pole', pole_across)]
    ppermute x1, starting transfers between devices: 0.01 us -> 2.68 us  [on_device(): x1 = lax.ppermute(s1, 'tile', near)]
    pallas_call x2 -> x4, Pallas kernels: 2.91 us -> 3.8 us  [the longest x1 1.6 us: on_device(): call(second_kernel, (wide, f32((8, 8, 128))), [VMEM] * 2, flops=12000000,...]
    all_to_all x1, blocking collectives: 17.7 us -> 18.4 us  [on_device(): lax.all_to_all(line.reshape(devices, 1, 128), ('pole', 'tile'), 0, 0, til...]
    ppermute x1, waiting for transfers between devices: 0.43 us -> 0.01 us  [on_device(): x1 = lax.ppermute(s1, 'tile', near)]
    ppermute x3 -> x5, waiting for transfers between devices: 2 us -> 2.08 us  [the longest x1 2.07 us: on_device(): y2 = lax.ppermute(m2, 'pole', pole_across)]
  transfers between devices with their start and end apart: 4 -> 6, of which waited for: 2 -> 1; matrix products, arithmetic and copies ran while one was open for 0% -> 0% of each run, Pallas kernels for 7% -> 12%
where the time goes in v6:
time: 36.4 us; the launch traced here: 36.2 us
  blocking collectives  18.4 us (51%)
  starting transfers between devices  8.37 us (23%)
  Pallas kernels  7.17 us (20%)
  waiting for transfers between devices  2.09 us (6%)
    all_to_all x1, blocking collectives, on_device(): lax.all_to_all(line.reshape(devices, 1, 128), ('pole', 'tile'), 0, 0, til...  18.4 us
    ppermute x1, starting transfers between devices, on_device(): x1 = lax.ppermute(s1, 'tile', near)  2.68 us
    ppermute x1, waiting for transfers between devices, on_device(): y2 = lax.ppermute(m2, 'pole', pole_across)  2.07 us
    pallas_call x1, Pallas kernels, on_device(): call(second_kernel, (wide, f32((8, 8, 128))), [VMEM] * 2, flops=12000000,...  1.6 us
    ppermute x1, starting transfers between devices, on_device(): c2 = lax.ppermute(corner, 'pole', pole_across)  1.53 us
    ppermute x1, starting transfers between devices, on_device(): x2 = lax.ppermute(s2, ('pole', 'tile'), pairs)  1.5 us
    pallas_call x1, Pallas kernels, on_device(): call(load_kernel, (message, message, f32((3, rows, depth, width))), [ANYW...  1.44 us
    ppermute x1, starting transfers between devices, on_device(): y1 = lax.ppermute(m1, 'pole', pole_near)  1.31 us
  transfers between devices with their start and end apart: 6, of which 1 were waited for; matrix products, arithmetic and copies ran while one was open for 0% of the time, Pallas kernels for 12%

profile of v6, /device:TPU:1, one launch (start us, length us, event | category | flops | bytes accessed | tf_op | source)
XLA Modules:
  0.0 36.2 jit_solution(2240698694658467885)
XLA Ops:
  0.0 0.9 %shard_map.49 = (f32[8,16,128]{2,1,0:T(8,128)S(1)}, f32[8,16,128]{2,1,0:T(8,128)S(1)}) custom-call(f32[2,32,16,128]{3,2,1,0:T(8,128)} %psi_ref.3, f32[32,16,128]{2,1,0:T(8,128)} %trap_ref.3), custom_call_target="tpu_custom_call" | custom-call | tf_op jit(solution)/shard_map/pallas_call | solution.py:430
  0.9 1.5 %collective-permute-start.2 = (f32[8,16,128]{2,1,0:T(8,128)S(1)}, f32[8,16,128]{2,1,0:T(8,128)S(1)}, u32[]{:S(2)}, u32[]{:S(2)}) collective-permute-start(f32[8,16,128]{2,1,0:T(8,128)S(1)} %get-tuple-element.27), channel_id=1, source_target_pairs={{0,32},{1,2},{2,1},{3,4},{4,3},{5,6},{6,5},{7,8},{8,7},{9,10},{10,... | collective-permute-start | bytes 196616 | tf_op jit(solution)/shard_map/ppermute | solution.py:439
  2.4 2.7 %collective-permute-start.3 = (f32[8,16,128]{2,1,0:T(8,128)S(1)}, f32[8,16,128]{2,1,0:T(8,128)S(1)}, u32[]{:S(2)}, u32[]{:S(2)}) collective-permute-start(f32[8,16,128]{2,1,0:T(8,128)S(1)} %get-tuple-element.28), channel_id=1, source_target_pairs={{0,1},{1,0},{2,3},{3,2},{4,5},{5,4},{6,7},{7,6},{8,9},{9,8},{10,11... | collective-permute-start | bytes 196616 | tf_op jit(solution)/shard_map/ppermute | solution.py:440
  5.1 1.4 %shard_map.46 = (f32[3,16,128]{2,1,0:T(8,128)S(1)}, f32[3,16,128]{2,1,0:T(8,128)S(1)}, f32[3,32,16,128]{3,2,1,0:T(8,128)S(1)}) custom-call(f32[2,32,16,128]{3,2,1,0:T(8,128)} %psi_ref.3, f32[32,16,128]{2,1,0:T(8,128)} %trap_ref.3), custom_call_target="tpu_custom_call" | custom-call | tf_op jit(solution)/shard_map/pallas_call | solution.py:443
  6.5 1.3 %collective-permute-start = (f32[3,16,128]{2,1,0:T(8,128)S(1)}, f32[3,16,128]{2,1,0:T(8,128)S(1)}, u32[]{:S(2)}, u32[]{:S(2)}) collective-permute-start(f32[3,16,128]{2,1,0:T(8,128)S(1)} %get-tuple-element.22), channel_id=1, source_target_pairs={{0,32},{32,0},{64,96},{96,64},{1,33},{33,1},{65,97},{97,65},{2,34}... | collective-permute-start | bytes 73736 | tf_op jit(solution)/shard_map/ppermute | solution.py:449
  7.8 1.2 %collective-permute-start.1 = (f32[3,16,128]{2,1,0:T(8,128)S(1)}, f32[3,16,128]{2,1,0:T(8,128)S(1)}, u32[]{:S(2)}, u32[]{:S(2)}) collective-permute-start(f32[3,16,128]{2,1,0:T(8,128)S(1)} %get-tuple-element.23), channel_id=1, source_target_pairs={{0,96},{32,64},{64,32},{96,0},{1,97},{33,65},{65,33},{97,1},{2,98}... | collective-permute-start | bytes 73736 | tf_op jit(solution)/shard_map/ppermute | solution.py:448
  9.0 0.0 collective-permute-done.y1_ref
  9.0 2.1 %collective-permute-done.1.y2_ref = f32[3,16,128]{2,1,0:T(8,128)S(1)} collective-permute-done((f32[3,16,128]{2,1,0:T(8,128)S(1)}, f32[3,16,128]{2,1,0:T(8,128)S(1)}, u32[]{:S(2)}, u32[]{:S(2)}) %collective-permute-start.1) | collective-permute-done | bytes 24608 | tf_op jit(solution)/shard_map/ppermute | solution.py:448
  11.1 1.2 %shard_map.47 = (f32[3,32,16,256]{3,2,1,0:T(8,128)S(1)}, f32[2,32,16,256]{3,2,1,0:T(8,128)S(1)}, f32[4,8,128]{2,1,0:T(8,128)S(1)}) custom-call(f32[3,32,16,128]{3,2,1,0:T(8,128)S(1)} %get-tuple-element.21.field_ref, f32[3,16,128]{2,1,0:T(8,128)S(1)} %collective-permute-done.y1_ref, f32[3,16,128]{2,1,0:T(8,128)S(1)} %collective-permute-done.1.y2_ref), custom_call_target="tpu_custom_call" | custom-call | flops 8000000 | bytes 3000000 | tf_op jit(solution)/shard_map/pallas_call | solution.py:452
  12.3 0.0 copy-start
  12.3 0.0 copy-start.1
  12.4 0.0 collective-permute-done.2.x2_ref
  12.4 0.0 collective-permute-done.3.x1_ref
  12.4 0.1 shard_map.50
  12.5 0.2 collective-permute-start.5
  12.6 1.5 %collective-permute-start.4 = (f32[16,128]{1,0:T(8,128)S(1)}, f32[16,128]{1,0:T(8,128)S(1)}, u32[]{:S(2)}, u32[]{:S(2)}) collective-permute-start(f32[16,128]{1,0:T(8,128)S(1)} %shard_map.50), channel_id=1, source_target_pairs={{0,96},{32,64},{64,32},{96,0},{1,97},{33,65},{65,33},{97,1},{2,98}... | collective-permute-start | bytes 24584 | tf_op jit(solution)/shard_map/ppermute | solution.py:459
  14.2 1.6 %shard_map.48 = (f32[2,32,16,256]{3,2,1,0:T(8,128)S(1)}, f32[8,8,128]{2,1,0:T(8,128)S(1)}) custom-call(f32[3,32,16,256]{3,2,1,0:T(8,128)S(1)} %get-tuple-element.25.grown_ref, f32[2,32,16,256]{3,2,1,0:T(8,128)S(1)} %get-tuple-element.24.u1_ref), custom_call_target="tpu_custom_call" | custom-call | flops 12000000 | bytes 5000000 | tf_op jit(solution)/shard_map/pallas_call | solution.py:462
  15.8 0.0 collective-permute-done.5.c1_ref
  15.8 0.0 collective-permute-done.4.c2_ref
  15.8 0.0 copy-done
  15.8 0.0 copy-done.1
  15.8 0.7 %shard_map.51 = (f32[2,2,16,128]{3,2,1,0:T(8,128)S(1)}, f32[2,4,16,128]{3,2,1,0:T(8,128)S(1)}, f32[128,128]{1,0:T(8,128)S(1)}) custom-call(f32[2,2]{1,0:T(2,128)S(1)} %copy-done, f32[2,2]{1,0:T(2,128)S(1)} %copy-done.1, f32[3,32,16,256]{3,2,1,0:T(8,128)S(1)} %get-tuple-element.25.grown_ref, f32[2,32,16,256]{3,2,1,0:T(8,128)S(1)} %get-tuple-element.24.u1_ref, ...), custom_call_target="tpu_custom_call" | custom-call | tf_op jit(solution)/shard_map/pallas_call | solution.py:467
  16.6 18.4 %all_to_all.5 = f32[128,1,128]{2,1,0:T(1,128)S(1)} all-to-all(f32[128,1,128]{2,1,0:T(1,128)S(1)} %bitcast.5), channel_id=1, replica_groups=mesh['pole'=4,'tile'=32] {'pole','tile'}, dimensions={0} | all-to-all | bytes 131072 | tf_op jit(solution)/shard_map/all_to_all | solution.py:473
  35.0 1.2 %shard_map.52 = f32[2,32,16,128]{3,2,1,0:T(8,128)} custom-call(f32[3,32,16,128]{3,2,1,0:T(8,128)S(1)} %get-tuple-element.21.field_ref, f32[2,32,16,256]{3,2,1,0:T(8,128)S(1)} %get-tuple-element.24.u1_ref, f32[2,32,16,256]{3,2,1,0:T(8,128)S(1)} %get-tuple-element.26.u2_ref, f32[2,2,16,128]{3,2,1,0:T(8,128)S(1)} %get-tuple-element.34.b1_ref, ...), custom_call_target="tpu_custom_call" | custom-call | tf_op jit(solution)/shard_map/pallas_call | solution.py:475
Async XLA Ops:
  0.9 11.5 %collective-permute-start.2 = (f32[8,16,128]{2,1,0:T(8,128)S(1)}, f32[8,16,128]{2,1,0:T(8,128)S(1)}, u32[]{:S(2)}, u32[]{:S(2)}) collective-permute-start(f32[8,16,128]{2,1,0:T(8,128)S(1)} %get-tuple-element.27), channel_id=1, source_target_pairs={{0,32},{1,2},{2,1},{3,4},{4,3},{5,6},{6,5},{7,8},{8,7},{9,10},{10,... | collective-permute-start | bytes 196616 | tf_op jit(solution)/shard_map/ppermute | solution.py:439
  2.4 10.0 %collective-permute-start.3 = (f32[8,16,128]{2,1,0:T(8,128)S(1)}, f32[8,16,128]{2,1,0:T(8,128)S(1)}, u32[]{:S(2)}, u32[]{:S(2)}) collective-permute-start(f32[8,16,128]{2,1,0:T(8,128)S(1)} %get-tuple-element.28), channel_id=1, source_target_pairs={{0,1},{1,0},{2,3},{3,2},{4,5},{5,4},{6,7},{7,6},{8,9},{9,8},{10,11... | collective-permute-start | bytes 196616 | tf_op jit(solution)/shard_map/ppermute | solution.py:440
  6.5 2.5 %collective-permute-start = (f32[3,16,128]{2,1,0:T(8,128)S(1)}, f32[3,16,128]{2,1,0:T(8,128)S(1)}, u32[]{:S(2)}, u32[]{:S(2)}) collective-permute-start(f32[3,16,128]{2,1,0:T(8,128)S(1)} %get-tuple-element.22), channel_id=1, source_target_pairs={{0,32},{32,0},{64,96},{96,64},{1,33},{33,1},{65,97},{97,65},{2,34}... | collective-permute-start | bytes 73736 | tf_op jit(solution)/shard_map/ppermute | solution.py:449
  7.8 3.3 %collective-permute-start.1 = (f32[3,16,128]{2,1,0:T(8,128)S(1)}, f32[3,16,128]{2,1,0:T(8,128)S(1)}, u32[]{:S(2)}, u32[]{:S(2)}) collective-permute-start(f32[3,16,128]{2,1,0:T(8,128)S(1)} %get-tuple-element.23), channel_id=1, source_target_pairs={{0,96},{32,64},{64,32},{96,0},{1,97},{33,65},{65,33},{97,1},{2,98}... | collective-permute-start | bytes 73736 | tf_op jit(solution)/shard_map/ppermute | solution.py:448
  12.3 3.5 %copy-start = (f32[2,2]{1,0:T(2,128)S(1)}, f32[2,2]{1,0:T(2,128)}, u32[]{:S(2)}) copy-start(f32[2,2]{1,0:T(2,128)} %shift_ref.1) | copy-start | bytes 52
  12.3 3.5 %copy-start.1 = (f32[2,2]{1,0:T(2,128)S(1)}, f32[2,2]{1,0:T(2,128)}, u32[]{:S(2)}) copy-start(f32[2,2]{1,0:T(2,128)} %weight_ref.1) | copy-start | bytes 52
  12.5 3.3 %collective-permute-start.5 = (f32[16,128]{1,0:T(8,128)S(1)}, f32[16,128]{1,0:T(8,128)S(1)}, u32[]{:S(2)}, u32[]{:S(2)}) collective-permute-start(f32[16,128]{1,0:T(8,128)S(1)} %shard_map.50), channel_id=1, source_target_pairs={{0,32},{32,0},{64,96},{96,64},{1,33},{33,1},{65,97},{97,65},{2,34}... | collective-permute-start | bytes 24584 | tf_op jit(solution)/shard_map/ppermute | solution.py:460
  12.6 3.1 %collective-permute-start.4 = (f32[16,128]{1,0:T(8,128)S(1)}, f32[16,128]{1,0:T(8,128)S(1)}, u32[]{:S(2)}, u32[]{:S(2)}) collective-permute-start(f32[16,128]{1,0:T(8,128)S(1)} %shard_map.50), channel_id=1, source_target_pairs={{0,96},{32,64},{64,32},{96,0},{1,97},{33,65},{65,33},{97,1},{2,98}... | collective-permute-start | bytes 24584 | tf_op jit(solution)/shard_map/ppermute | solution.py:459

commit v7 on v6

--- a/solution.py
+++ b/solution.py
@@ -31,30 +31,17 @@
     return lax.rem(index, 2) == 1
 
 
-def load_kernel(psi_ref, trap_ref, s1_ref, s2_ref, field_ref, sems):
+def load_kernel(psi_ref, trap_ref, s1_ref, s2_ref, field_ref):
     rows, depth = trap_ref.shape[:2]
-    half_rows, part_rows = rows // 2, rows // 2
-    copies = []
-    for part in range(2):
-        at = pl.ds(part * part_rows, part_rows)
-        pair = (
-            pltpu.make_async_copy(psi_ref.at[:, at], field_ref.at[0:2, at], sems.at[part, 0]),
-            pltpu.make_async_copy(trap_ref.at[at], field_ref.at[2, at], sems.at[part, 1]),
-        )
-        for copy in pair:
-            copy.start()
-        copies.append(pair)
+    half_rows = rows // 2
     group = lanes((depth, 128)) // 8
     packs = [[jnp.zeros((depth, 128), jnp.float32)] * 2 for _ in range(3)]
     for row in range(rows):
         half, g = divmod(row, half_rows)
-        if g == 0:
-            for copy in copies[half]:
-                copy.wait()
-        re, im = field_ref[0, row], field_ref[1, row]
-        diag = field_ref[2, row] + COUPLING * (re * re + im * im) + DIAGONAL
-        field_ref[2, row] = diag
+        re, im = psi_ref[0, row], psi_ref[1, row]
+        diag = cell(re, im, trap_ref[row])
         for f, field in enumerate((re, im, diag)):
+            field_ref[f, row] = field
             moved = pltpu.roll(field, (8 * g + HALO) % 128, 1)
             packs[f][half] = jnp.where(group == g, moved, packs[f][half])
     first = lanes((depth, 128)) % 8 < HALO
@@ -188,7 +175,7 @@
     return lax.fori_loop(0, rows - 2 * reach, step, (zero,) * 4, unroll=True)
 
 
-def first_kernel(field_ref, y1_ref, y2_ref, grown_ref, u1_ref, sums_ref):
+def first_kernel(field_ref, y2_ref, y1_ref, grown_ref, u1_ref, sums_ref):
     rows, depth = field_ref.shape[1:3]
     for half in range(2):
         packs = [merged(y1_ref, y2_ref, f, half) for f in range(3)]
@@ -211,7 +198,7 @@
 
 
 def outer_kernel(
-    shift_ref, weight_ref, grown_ref, u1_ref, u2_ref, sums1_ref, sums2_ref, x2_ref, x1_ref, c2_ref, c1_ref,
+    shift_ref, weight_ref, grown_ref, u1_ref, u2_ref, sums1_ref, sums2_ref, x2_ref, x1_ref, c1_ref, c2_ref,
     b1_ref, b2_ref, line_ref,
 ):
     rows, depth = grown_ref.shape[1:3]
@@ -425,12 +412,12 @@
     rows, depth, width = trap.shape
     f32 = functools.partial(jax.ShapeDtypeStruct, dtype=jnp.float32)
 
-    psi, trap = (pltpu.with_memory_space_constraint(x, pltpu.HBM) for x in (psi, trap))
     edge = f32((3 * HALO - 1, depth, width))
     s2, s1 = call(
         end_kernel, (edge, edge), [ANYWHERE] * 2,
         [pltpu.VMEM((2, 3, HALO, depth, width), jnp.float32), pltpu.SemaphoreType.DMA((2, 2))],
-    )(psi, trap)
+        flops=2_000_000_000, bytes_accessed=40_000_000,
+    )(*(pltpu.with_memory_space_constraint(x, pltpu.HBM) for x in (psi, trap)))
     near, across = swaps("tile")
     pairs = []
     for pole in range(poles):
@@ -441,8 +428,7 @@
 
     message = f32((3, depth, 128))
     m1, m2, field = call(
-        load_kernel, (message, message, f32((3, rows, depth, width))), [ANYWHERE] * 2,
-        [pltpu.SemaphoreType.DMA((2, 2))],
+        load_kernel, (message, message, f32((3, rows, depth, width))), [VMEM] * 2,
     )(psi, trap)
     pole_near, pole_across = swaps("pole")
     y2 = lax.ppermute(m2, "pole", pole_across)
@@ -453,7 +439,7 @@
         first_kernel,
         (f32((3, rows, depth, 2 * width)), wide, f32((4, 8, 128))),
         [VMEM] * 3, flops=8_000_000, bytes_accessed=3_000_000,
-    )(field, y1, y2)
+    )(field, y2, y1)
     x2, x1, sums1 = lax.optimization_barrier((x2, x1, sums1))
     corner = call(corner_kernel, f32((depth, 128)), [VMEM] * 2)(x2, x1)
     c2 = lax.ppermute(corner, "pole", pole_across)
@@ -468,7 +454,7 @@
         outer_kernel,
         (f32((2, 2, depth, width)), f32((2, 4, depth, width)), f32((devices, 128))),
         [VMEM] * 11,
-    )(pole_shift, pole_weight, grown, u1, u2, sums1, sums2, x2, x1, c2, c1)
+    )(pole_shift, pole_weight, grown, u1, u2, sums1, sums2, x2, x1, c1, c2)
 
     lines = lax.all_to_all(line.reshape(devices, 1, 128), ("pole", "tile"), 0, 0, tiled=True)
     combine = functools.partial(combine_kernel, pole_shift.shape[0] * poles)

time: 36.4 us -> 36.3 us (level)
  blocking collectives: 18.4 us -> 19.8 us
  Pallas kernels: 7.17 us -> 6.16 us
  starting transfers between devices: 8.37 us -> 7.96 us
    all_to_all x1, blocking collectives: 18.4 us -> 19.8 us  [on_device(): lax.all_to_all(line.reshape(devices, 1, 128), ('pole', 'tile'), 0, 0, til...]
    ppermute x1, starting transfers between devices: 1.31 us -> 0.01 us  [on_device(): y1 = lax.ppermute(m1, 'pole', pole_near)]
    ppermute x1, starting transfers between devices: 1.19 us -> 2.41 us  [on_device(): y2 = lax.ppermute(m2, 'pole', pole_across)]
    pallas_call x1, Pallas kernels: 1.44 us -> 0.35 us  [on_device(): call(load_kernel, (message, message, f32((3, rows, depth, width))), [VMEM...]
  transfers between devices with their start and end apart: 6 -> 6, of which waited for: 1 -> 2; matrix products, arithmetic and copies ran while one was open for 0% -> 0% of each run, Pallas kernels for 12% -> 9%
where the time goes in v7:
time: 36.3 us; the launch traced here: 36.2 us
  blocking collectives  19.8 us (55%)
  starting transfers between devices  7.96 us (22%)
  Pallas kernels  6.16 us (17%)
  waiting for transfers between devices  2.17 us (6%)
    all_to_all x1, blocking collectives, on_device(): lax.all_to_all(line.reshape(devices, 1, 128), ('pole', 'tile'), 0, 0, til...  19.8 us
    ppermute x1, starting transfers between devices, on_device(): x1 = lax.ppermute(s1, 'tile', near)  2.68 us
    ppermute x1, starting transfers between devices, on_device(): y2 = lax.ppermute(m2, 'pole', pole_across)  2.41 us
    ppermute x1, waiting for transfers between devices, on_device(): y2 = lax.ppermute(m2, 'pole', pole_across)  1.97 us
    pallas_call x1, Pallas kernels, on_device(): call(second_kernel, (wide, f32((8, 8, 128))), [VMEM] * 2, flops=12000000,...  1.6 us
    ppermute x1, starting transfers between devices, on_device(): x2 = lax.ppermute(s2, ('pole', 'tile'), pairs)  1.5 us
    ppermute x1, starting transfers between devices, on_device(): c2 = lax.ppermute(corner, 'pole', pole_across)  1.36 us
    pallas_call x1, Pallas kernels, on_device(): call(first_kernel, (f32((3, rows, depth, 2 * width)), wide, f32((4, 8, 12...  1.21 us
  transfers between devices with their start and end apart: 6, of which 2 were waited for; matrix products, arithmetic and copies ran while one was open for 0% of the time, Pallas kernels for 9%

profile of v7, /device:TPU:1, one launch (start us, length us, event | category | flops | bytes accessed | tf_op | source)
XLA Modules:
  0.0 36.2 jit_solution(2780359313070540989)
XLA Ops:
  0.0 0.0 copy-start.1
  0.0 0.0 copy-start
  0.0 1.0 %shard_map.49 = (f32[8,16,128]{2,1,0:T(8,128)S(1)}, f32[8,16,128]{2,1,0:T(8,128)S(1)}) custom-call(f32[2,32,16,128]{3,2,1,0:T(8,128)} %psi_ref.3, f32[32,16,128]{2,1,0:T(8,128)} %trap_ref.3), custom_call_target="tpu_custom_call" | custom-call | flops 2000000000 | bytes 40000000 | tf_op jit(solution)/shard_map/pallas_call | solution.py:416
  1.0 1.5 %collective-permute-start.2 = (f32[8,16,128]{2,1,0:T(8,128)S(1)}, f32[8,16,128]{2,1,0:T(8,128)S(1)}, u32[]{:S(2)}, u32[]{:S(2)}) collective-permute-start(f32[8,16,128]{2,1,0:T(8,128)S(1)} %get-tuple-element.27), channel_id=1, source_target_pairs={{0,32},{1,2},{2,1},{3,4},{4,3},{5,6},{6,5},{7,8},{8,7},{9,10},{10,... | collective-permute-start | bytes 196616 | tf_op jit(solution)/shard_map/ppermute | solution.py:426
  2.5 2.7 %collective-permute-start.3 = (f32[8,16,128]{2,1,0:T(8,128)S(1)}, f32[8,16,128]{2,1,0:T(8,128)S(1)}, u32[]{:S(2)}, u32[]{:S(2)}) collective-permute-start(f32[8,16,128]{2,1,0:T(8,128)S(1)} %get-tuple-element.28), channel_id=1, source_target_pairs={{0,1},{1,0},{2,3},{3,2},{4,5},{5,4},{6,7},{7,6},{8,9},{9,8},{10,11... | collective-permute-start | bytes 196616 | tf_op jit(solution)/shard_map/ppermute | solution.py:427
  5.2 0.0 copy-done.1
  5.2 0.0 copy-done
  5.2 0.4 shard_map.46
  5.5 2.4 %collective-permute-start = (f32[3,16,128]{2,1,0:T(8,128)S(1)}, f32[3,16,128]{2,1,0:T(8,128)S(1)}, u32[]{:S(2)}, u32[]{:S(2)}) collective-permute-start(f32[3,16,128]{2,1,0:T(8,128)S(1)} %get-tuple-element.22), channel_id=1, source_target_pairs={{0,96},{32,64},{64,32},{96,0},{1,97},{33,65},{65,33},{97,1},{2,98}... | collective-permute-start | bytes 73736 | tf_op jit(solution)/shard_map/ppermute | solution.py:434
  7.9 0.0 collective-permute-start.1
  7.9 2.0 %collective-permute-done.y2_ref = f32[3,16,128]{2,1,0:T(8,128)S(1)} collective-permute-done((f32[3,16,128]{2,1,0:T(8,128)S(1)}, f32[3,16,128]{2,1,0:T(8,128)S(1)}, u32[]{:S(2)}, u32[]{:S(2)}) %collective-permute-start) | collective-permute-done | bytes 24608 | tf_op jit(solution)/shard_map/ppermute | solution.py:434
  9.9 0.0 collective-permute-done.1.y1_ref
  9.9 1.2 %shard_map.47 = (f32[3,32,16,256]{3,2,1,0:T(8,128)S(1)}, f32[2,32,16,256]{3,2,1,0:T(8,128)S(1)}, f32[4,8,128]{2,1,0:T(8,128)S(1)}) custom-call(f32[3,32,16,128]{3,2,1,0:T(8,128)S(1)} %get-tuple-element.21.field_ref, f32[3,16,128]{2,1,0:T(8,128)S(1)} %collective-permute-done.y2_ref, f32[3,16,128]{2,1,0:T(8,128)S(1)} %collective-permute-done.1.y1_ref), custom_call_target="tpu_custom_call" | custom-call | flops 8000000 | bytes 3000000 | tf_op jit(solution)/shard_map/pallas_call | solution.py:438
  11.1 0.0 copy-start.2
  11.1 0.0 copy-start.3
  11.2 0.0 collective-permute-done.2.x2_ref
  11.2 0.0 collective-permute-done.3.x1_ref
  11.2 0.1 shard_map.50
  11.3 1.4 %collective-permute-start.5 = (f32[16,128]{1,0:T(8,128)S(1)}, f32[16,128]{1,0:T(8,128)S(1)}, u32[]{:S(2)}, u32[]{:S(2)}) collective-permute-start(f32[16,128]{1,0:T(8,128)S(1)} %shard_map.50), channel_id=1, source_target_pairs={{0,96},{32,64},{64,32},{96,0},{1,97},{33,65},{65,33},{97,1},{2,98}... | collective-permute-start | bytes 24584 | tf_op jit(solution)/shard_map/ppermute | solution.py:445
  12.6 0.0 collective-permute-start.4
  12.6 1.6 %shard_map.48 = (f32[2,32,16,256]{3,2,1,0:T(8,128)S(1)}, f32[8,8,128]{2,1,0:T(8,128)S(1)}) custom-call(f32[3,32,16,256]{3,2,1,0:T(8,128)S(1)} %get-tuple-element.25.grown_ref, f32[2,32,16,256]{3,2,1,0:T(8,128)S(1)} %get-tuple-element.24.u1_ref), custom_call_target="tpu_custom_call" | custom-call | flops 12000000 | bytes 5000000 | tf_op jit(solution)/shard_map/pallas_call | solution.py:448
  14.3 0.2 collective-permute-done.5.c2_ref
  14.4 0.0 collective-permute-done.4.c1_ref
  14.4 0.0 copy-done.2
  14.4 0.0 copy-done.3
  14.4 0.8 %shard_map.51 = (f32[2,2,16,128]{3,2,1,0:T(8,128)S(1)}, f32[2,4,16,128]{3,2,1,0:T(8,128)S(1)}, f32[128,128]{1,0:T(8,128)S(1)}) custom-call(f32[2,2]{1,0:T(2,128)S(1)} %copy-done.2, f32[2,2]{1,0:T(2,128)S(1)} %copy-done.3, f32[3,32,16,256]{3,2,1,0:T(8,128)S(1)} %get-tuple-element.25.grown_ref, f32[2,32,16,256]{3,2,1,0:T(8,128)S(1)} %get-tuple-element.24.u1_ref, ...), custom_call_target="tpu_custom_call" | custom-call | tf_op jit(solution)/shard_map/pallas_call | solution.py:453
  15.2 19.8 %all_to_all.5 = f32[128,1,128]{2,1,0:T(1,128)S(1)} all-to-all(f32[128,1,128]{2,1,0:T(1,128)S(1)} %bitcast.5), channel_id=1, replica_groups=mesh['pole'=4,'tile'=32] {'pole','tile'}, dimensions={0} | all-to-all | bytes 131072 | tf_op jit(solution)/shard_map/all_to_all | solution.py:459
  35.0 1.2 %shard_map.52 = f32[2,32,16,128]{3,2,1,0:T(8,128)} custom-call(f32[3,32,16,128]{3,2,1,0:T(8,128)S(1)} %get-tuple-element.21.field_ref, f32[2,32,16,256]{3,2,1,0:T(8,128)S(1)} %get-tuple-element.24.u1_ref, f32[2,32,16,256]{3,2,1,0:T(8,128)S(1)} %get-tuple-element.26.u2_ref, f32[2,2,16,128]{3,2,1,0:T(8,128)S(1)} %get-tuple-element.34.b1_ref, ...), custom_call_target="tpu_custom_call" | custom-call | tf_op jit(solution)/shard_map/pallas_call | solution.py:461
Async XLA Ops:
  0.0 5.2 %copy-start.1 = (f32[32,16,128]{2,1,0:T(8,128)S(1)}, f32[32,16,128]{2,1,0:T(8,128)}, u32[]{:S(2)}) copy-start(f32[32,16,128]{2,1,0:T(8,128)} %trap_ref.3) | copy-start | bytes 786436
  0.0 5.2 %copy-start = (f32[2,32,16,128]{3,2,1,0:T(8,128)S(1)}, f32[2,32,16,128]{3,2,1,0:T(8,128)}, u32[]{:S(2)}) copy-start(f32[2,32,16,128]{3,2,1,0:T(8,128)} %psi_ref.3) | copy-start | bytes 1572868
  1.0 10.2 %collective-permute-start.2 = (f32[8,16,128]{2,1,0:T(8,128)S(1)}, f32[8,16,128]{2,1,0:T(8,128)S(1)}, u32[]{:S(2)}, u32[]{:S(2)}) collective-permute-start(f32[8,16,128]{2,1,0:T(8,128)S(1)} %get-tuple-element.27), channel_id=1, source_target_pairs={{0,32},{1,2},{2,1},{3,4},{4,3},{5,6},{6,5},{7,8},{8,7},{9,10},{10,... | collective-permute-start | bytes 196616 | tf_op jit(solution)/shard_map/ppermute | solution.py:426
  2.5 8.7 %collective-permute-start.3 = (f32[8,16,128]{2,1,0:T(8,128)S(1)}, f32[8,16,128]{2,1,0:T(8,128)S(1)}, u32[]{:S(2)}, u32[]{:S(2)}) collective-permute-start(f32[8,16,128]{2,1,0:T(8,128)S(1)} %get-tuple-element.28), channel_id=1, source_target_pairs={{0,1},{1,0},{2,3},{3,2},{4,5},{5,4},{6,7},{7,6},{8,9},{9,8},{10,11... | collective-permute-start | bytes 196616 | tf_op jit(solution)/shard_map/ppermute | solution.py:427
  5.5 4.4 %collective-permute-start = (f32[3,16,128]{2,1,0:T(8,128)S(1)}, f32[3,16,128]{2,1,0:T(8,128)S(1)}, u32[]{:S(2)}, u32[]{:S(2)}) collective-permute-start(f32[3,16,128]{2,1,0:T(8,128)S(1)} %get-tuple-element.22), channel_id=1, source_target_pairs={{0,96},{32,64},{64,32},{96,0},{1,97},{33,65},{65,33},{97,1},{2,98}... | collective-permute-start | bytes 73736 | tf_op jit(solution)/shard_map/ppermute | solution.py:434
  7.9 2.0 %collective-permute-start.1 = (f32[3,16,128]{2,1,0:T(8,128)S(1)}, f32[3,16,128]{2,1,0:T(8,128)S(1)}, u32[]{:S(2)}, u32[]{:S(2)}) collective-permute-start(f32[3,16,128]{2,1,0:T(8,128)S(1)} %get-tuple-element.23), channel_id=1, source_target_pairs={{0,32},{32,0},{64,96},{96,64},{1,33},{33,1},{65,97},{97,65},{2,34}... | collective-permute-start | bytes 73736 | tf_op jit(solution)/shard_map/ppermute | solution.py:435
  11.1 3.3 %copy-start.2 = (f32[2,2]{1,0:T(2,128)S(1)}, f32[2,2]{1,0:T(2,128)}, u32[]{:S(2)}) copy-start(f32[2,2]{1,0:T(2,128)} %shift_ref.1) | copy-start | bytes 52
  11.1 3.3 %copy-start.3 = (f32[2,2]{1,0:T(2,128)S(1)}, f32[2,2]{1,0:T(2,128)}, u32[]{:S(2)}) copy-start(f32[2,2]{1,0:T(2,128)} %weight_ref.1) | copy-start | bytes 52
  11.3 3.2 %collective-permute-start.5 = (f32[16,128]{1,0:T(8,128)S(1)}, f32[16,128]{1,0:T(8,128)S(1)}, u32[]{:S(2)}, u32[]{:S(2)}) collective-permute-start(f32[16,128]{1,0:T(8,128)S(1)} %shard_map.50), channel_id=1, source_target_pairs={{0,96},{32,64},{64,32},{96,0},{1,97},{33,65},{65,33},{97,1},{2,98}... | collective-permute-start | bytes 24584 | tf_op jit(solution)/shard_map/ppermute | solution.py:445
  12.6 1.8 %collective-permute-start.4 = (f32[16,128]{1,0:T(8,128)S(1)}, f32[16,128]{1,0:T(8,128)S(1)}, u32[]{:S(2)}, u32[]{:S(2)}) collective-permute-start(f32[16,128]{1,0:T(8,128)S(1)} %shard_map.50), channel_id=1, source_target_pairs={{0,32},{32,0},{64,96},{96,64},{1,33},{33,1},{65,97},{97,65},{2,34}... | collective-permute-start | bytes 24584 | tf_op jit(solution)/shard_map/ppermute | solution.py:446

commit v8 on v7

--- a/solution.py
+++ b/solution.py
@@ -175,7 +175,7 @@
     return lax.fori_loop(0, rows - 2 * reach, step, (zero,) * 4, unroll=True)
 
 
-def first_kernel(field_ref, y2_ref, y1_ref, grown_ref, u1_ref, sums_ref):
+def first_kernel(field_ref, y1_ref, y2_ref, grown_ref, u1_ref, sums_ref):
     rows, depth = field_ref.shape[1:3]
     for half in range(2):
         packs = [merged(y1_ref, y2_ref, f, half) for f in range(3)]
@@ -431,7 +431,11 @@
         load_kernel, (message, message, f32((3, rows, depth, width))), [VMEM] * 2,
     )(psi, trap)
     pole_near, pole_across = swaps("pole")
-    y2 = lax.ppermute(m2, "pole", pole_across)
+    sides = []
+    for pole, other in pole_across:
+        for tile in range(tiles):
+            sides.append((pole * tiles + tile, (other * tiles + tile) if abs(pole - other) == 1 else (pole * tiles + (tile ^ 1))))
+    y2 = lax.ppermute(m2, ("pole", "tile"), sides)
     y1 = lax.ppermute(m1, "pole", pole_near)
 
     wide = f32((2, rows, depth, 2 * width))
@@ -439,10 +443,10 @@
         first_kernel,
         (f32((3, rows, depth, 2 * width)), wide, f32((4, 8, 128))),
         [VMEM] * 3, flops=8_000_000, bytes_accessed=3_000_000,
-    )(field, y2, y1)
+    )(field, y1, y2)
     x2, x1, sums1 = lax.optimization_barrier((x2, x1, sums1))
     corner = call(corner_kernel, f32((depth, 128)), [VMEM] * 2)(x2, x1)
-    c2 = lax.ppermute(corner, "pole", pole_across)
+    c2 = lax.ppermute(corner, ("pole", "tile"), sides)
     c1 = lax.ppermute(corner, "pole", pole_near)
 
     u2, sums2 = call(

time: 36.3 us -> 36.8 us (1.014)
  waiting for transfers between devices: 2.17 us -> 2.89 us
    ppermute x2, starting transfers between devices: 3.77 us -> 2.19 us  [the longest x1 1.19 us: on_device(): y2 = lax.ppermute(m2, ('pole', 'tile'), sides)]
    ppermute x1, starting transfers between devices: 0.01 us -> 1.31 us  [on_device(): y1 = lax.ppermute(m1, 'pole', pole_near)]
    ppermute x2, waiting for transfers between devices: 2.16 us -> 2.88 us  [the longest x1 2.33 us: on_device(): y2 = lax.ppermute(m2, ('pole', 'tile'), sides)]
where the time goes in v8:
time: 36.8 us; the launch traced here: 36.7 us
  blocking collectives  19.8 us (54%)
  starting transfers between devices  7.69 us (21%)
  Pallas kernels  6.16 us (17%)
  waiting for transfers between devices  2.89 us (8%)
    all_to_all x1, blocking collectives, on_device(): lax.all_to_all(line.reshape(devices, 1, 128), ('pole', 'tile'), 0, 0, til...  19.8 us
    ppermute x1, starting transfers between devices, on_device(): x1 = lax.ppermute(s1, 'tile', near)  2.68 us
    ppermute x1, waiting for transfers between devices, on_device(): y2 = lax.ppermute(m2, ('pole', 'tile'), sides)  2.33 us
    pallas_call x1, Pallas kernels, on_device(): call(second_kernel, (wide, f32((8, 8, 128))), [VMEM] * 2, flops=12000000,...  1.6 us
    ppermute x1, starting transfers between devices, on_device(): x2 = lax.ppermute(s2, ('pole', 'tile'), pairs)  1.5 us
    ppermute x1, starting transfers between devices, on_device(): y1 = lax.ppermute(m1, 'pole', pole_near)  1.31 us
    pallas_call x1, Pallas kernels, on_device(): call(first_kernel, (f32((3, rows, depth, 2 * width)), wide, f32((4, 8, 12...  1.21 us
    ppermute x1, starting transfers between devices, on_device(): y2 = lax.ppermute(m2, ('pole', 'tile'), sides)  1.19 us
  transfers between devices with their start and end apart: 6, of which 2 were waited for; matrix products, arithmetic and copies ran while one was open for 0% of the time, Pallas kernels for 9%

profile of v8, /device:TPU:1, one launch (start us, length us, event | category | flops | bytes accessed | tf_op | source)
XLA Modules:
  0.0 36.7 jit_solution(3400777987322907428)
XLA Ops:
  0.0 0.0 copy-start.1
  0.0 0.0 copy-start
  0.0 1.0 %shard_map.49 = (f32[8,16,128]{2,1,0:T(8,128)S(1)}, f32[8,16,128]{2,1,0:T(8,128)S(1)}) custom-call(f32[2,32,16,128]{3,2,1,0:T(8,128)} %psi_ref.3, f32[32,16,128]{2,1,0:T(8,128)} %trap_ref.3), custom_call_target="tpu_custom_call" | custom-call | flops 2000000000 | bytes 40000000 | tf_op jit(solution)/shard_map/pallas_call | solution.py:416
  1.0 1.5 %collective-permute-start.2 = (f32[8,16,128]{2,1,0:T(8,128)S(1)}, f32[8,16,128]{2,1,0:T(8,128)S(1)}, u32[]{:S(2)}, u32[]{:S(2)}) collective-permute-start(f32[8,16,128]{2,1,0:T(8,128)S(1)} %get-tuple-element.27), channel_id=1, source_target_pairs={{0,32},{1,2},{2,1},{3,4},{4,3},{5,6},{6,5},{7,8},{8,7},{9,10},{10,... | collective-permute-start | bytes 196616 | tf_op jit(solution)/shard_map/ppermute | solution.py:426
  2.5 2.7 %collective-permute-start.3 = (f32[8,16,128]{2,1,0:T(8,128)S(1)}, f32[8,16,128]{2,1,0:T(8,128)S(1)}, u32[]{:S(2)}, u32[]{:S(2)}) collective-permute-start(f32[8,16,128]{2,1,0:T(8,128)S(1)} %get-tuple-element.28), channel_id=1, source_target_pairs={{0,1},{1,0},{2,3},{3,2},{4,5},{5,4},{6,7},{7,6},{8,9},{9,8},{10,11... | collective-permute-start | bytes 196616 | tf_op jit(solution)/shard_map/ppermute | solution.py:427
  5.2 0.0 copy-done.1
  5.2 0.0 copy-done
  5.2 0.4 shard_map.46
  5.5 1.3 %collective-permute-start = (f32[3,16,128]{2,1,0:T(8,128)S(1)}, f32[3,16,128]{2,1,0:T(8,128)S(1)}, u32[]{:S(2)}, u32[]{:S(2)}) collective-permute-start(f32[3,16,128]{2,1,0:T(8,128)S(1)} %get-tuple-element.22), channel_id=1, source_target_pairs={{0,32},{32,0},{64,96},{96,64},{1,33},{33,1},{65,97},{97,65},{2,34}... | collective-permute-start | bytes 73736 | tf_op jit(solution)/shard_map/ppermute | solution.py:439
  6.8 1.2 %collective-permute-start.1 = (f32[3,16,128]{2,1,0:T(8,128)S(1)}, f32[3,16,128]{2,1,0:T(8,128)S(1)}, u32[]{:S(2)}, u32[]{:S(2)}) collective-permute-start(f32[3,16,128]{2,1,0:T(8,128)S(1)} %get-tuple-element.23), channel_id=1, source_target_pairs={{0,1},{1,0},{2,3},{3,2},{4,5},{5,4},{6,7},{7,6},{8,9},{9,8},{10,11... | collective-permute-start | bytes 73736 | tf_op jit(solution)/shard_map/ppermute | solution.py:438
  8.0 0.0 collective-permute-done.y1_ref
  8.0 2.3 %collective-permute-done.1.y2_ref = f32[3,16,128]{2,1,0:T(8,128)S(1)} collective-permute-done((f32[3,16,128]{2,1,0:T(8,128)S(1)}, f32[3,16,128]{2,1,0:T(8,128)S(1)}, u32[]{:S(2)}, u32[]{:S(2)}) %collective-permute-start.1) | collective-permute-done | bytes 24608 | tf_op jit(solution)/shard_map/ppermute | solution.py:438
  10.4 1.2 %shard_map.47 = (f32[3,32,16,256]{3,2,1,0:T(8,128)S(1)}, f32[2,32,16,256]{3,2,1,0:T(8,128)S(1)}, f32[4,8,128]{2,1,0:T(8,128)S(1)}) custom-call(f32[3,32,16,128]{3,2,1,0:T(8,128)S(1)} %get-tuple-element.21.field_ref, f32[3,16,128]{2,1,0:T(8,128)S(1)} %collective-permute-done.y1_ref, f32[3,16,128]{2,1,0:T(8,128)S(1)} %collective-permute-done.1.y2_ref), custom_call_target="tpu_custom_call" | custom-call | flops 8000000 | bytes 3000000 | tf_op jit(solution)/shard_map/pallas_call | solution.py:442
  11.6 0.0 copy-start.2
  11.6 0.0 copy-start.3
  11.6 0.0 collective-permute-done.2.x2_ref
  11.6 0.0 collective-permute-done.3.x1_ref
  11.6 0.1 shard_map.50
  11.7 1.0 %collective-permute-start.5 = (f32[16,128]{1,0:T(8,128)S(1)}, f32[16,128]{1,0:T(8,128)S(1)}, u32[]{:S(2)}, u32[]{:S(2)}) collective-permute-start(f32[16,128]{1,0:T(8,128)S(1)} %shard_map.50), channel_id=1, source_target_pairs={{0,1},{1,0},{2,3},{3,2},{4,5},{5,4},{6,7},{7,6},{8,9},{9,8},{10,11... | collective-permute-start | bytes 24584 | tf_op jit(solution)/shard_map/ppermute | solution.py:449
  12.7 0.0 collective-permute-start.4
  12.7 1.6 %shard_map.48 = (f32[2,32,16,256]{3,2,1,0:T(8,128)S(1)}, f32[8,8,128]{2,1,0:T(8,128)S(1)}) custom-call(f32[3,32,16,256]{3,2,1,0:T(8,128)S(1)} %get-tuple-element.25.grown_ref, f32[2,32,16,256]{3,2,1,0:T(8,128)S(1)} %get-tuple-element.24.u1_ref), custom_call_target="tpu_custom_call" | custom-call | flops 12000000 | bytes 5000000 | tf_op jit(solution)/shard_map/pallas_call | solution.py:452
  14.3 0.5 %collective-permute-done.5.c2_ref = f32[16,128]{1,0:T(8,128)S(1)} collective-permute-done((f32[16,128]{1,0:T(8,128)S(1)}, f32[16,128]{1,0:T(8,128)S(1)}, u32[]{:S(2)}, u32[]{:S(2)}) %collective-permute-start.5) | collective-permute-done | bytes 8224 | tf_op jit(solution)/shard_map/ppermute | solution.py:449
  14.9 0.0 collective-permute-done.4.c1_ref
  14.9 0.0 copy-done.2
  14.9 0.0 copy-done.3
  14.9 0.8 %shard_map.51 = (f32[2,2,16,128]{3,2,1,0:T(8,128)S(1)}, f32[2,4,16,128]{3,2,1,0:T(8,128)S(1)}, f32[128,128]{1,0:T(8,128)S(1)}) custom-call(f32[2,2]{1,0:T(2,128)S(1)} %copy-done.2, f32[2,2]{1,0:T(2,128)S(1)} %copy-done.3, f32[3,32,16,256]{3,2,1,0:T(8,128)S(1)} %get-tuple-element.25.grown_ref, f32[2,32,16,256]{3,2,1,0:T(8,128)S(1)} %get-tuple-element.24.u1_ref, ...), custom_call_target="tpu_custom_call" | custom-call | tf_op jit(solution)/shard_map/pallas_call | solution.py:457
  15.7 19.8 %all_to_all.5 = f32[128,1,128]{2,1,0:T(1,128)S(1)} all-to-all(f32[128,1,128]{2,1,0:T(1,128)S(1)} %bitcast.5), channel_id=1, replica_groups=mesh['pole'=4,'tile'=32] {'pole','tile'}, dimensions={0} | all-to-all | bytes 131072 | tf_op jit(solution)/shard_map/all_to_all | solution.py:463
  35.5 1.2 %shard_map.52 = f32[2,32,16,128]{3,2,1,0:T(8,128)} custom-call(f32[3,32,16,128]{3,2,1,0:T(8,128)S(1)} %get-tuple-element.21.field_ref, f32[2,32,16,256]{3,2,1,0:T(8,128)S(1)} %get-tuple-element.24.u1_ref, f32[2,32,16,256]{3,2,1,0:T(8,128)S(1)} %get-tuple-element.26.u2_ref, f32[2,2,16,128]{3,2,1,0:T(8,128)S(1)} %get-tuple-element.34.b1_ref, ...), custom_call_target="tpu_custom_call" | custom-call | tf_op jit(solution)/shard_map/pallas_call | solution.py:465
Async XLA Ops:
  0.0 5.2 %copy-start.1 = (f32[32,16,128]{2,1,0:T(8,128)S(1)}, f32[32,16,128]{2,1,0:T(8,128)}, u32[]{:S(2)}) copy-start(f32[32,16,128]{2,1,0:T(8,128)} %trap_ref.3) | copy-start | bytes 786436
  0.0 5.2 %copy-start = (f32[2,32,16,128]{3,2,1,0:T(8,128)S(1)}, f32[2,32,16,128]{3,2,1,0:T(8,128)}, u32[]{:S(2)}) copy-start(f32[2,32,16,128]{3,2,1,0:T(8,128)} %psi_ref.3) | copy-start | bytes 1572868
  1.0 10.6 %collective-permute-start.2 = (f32[8,16,128]{2,1,0:T(8,128)S(1)}, f32[8,16,128]{2,1,0:T(8,128)S(1)}, u32[]{:S(2)}, u32[]{:S(2)}) collective-permute-start(f32[8,16,128]{2,1,0:T(8,128)S(1)} %get-tuple-element.27), channel_id=1, source_target_pairs={{0,32},{1,2},{2,1},{3,4},{4,3},{5,6},{6,5},{7,8},{8,7},{9,10},{10,... | collective-permute-start | bytes 196616 | tf_op jit(solution)/shard_map/ppermute | solution.py:426
  2.5 9.1 %collective-permute-start.3 = (f32[8,16,128]{2,1,0:T(8,128)S(1)}, f32[8,16,128]{2,1,0:T(8,128)S(1)}, u32[]{:S(2)}, u32[]{:S(2)}) collective-permute-start(f32[8,16,128]{2,1,0:T(8,128)S(1)} %get-tuple-element.28), channel_id=1, source_target_pairs={{0,1},{1,0},{2,3},{3,2},{4,5},{5,4},{6,7},{7,6},{8,9},{9,8},{10,11... | collective-permute-start | bytes 196616 | tf_op jit(solution)/shard_map/ppermute | solution.py:427
  5.5 2.5 %collective-permute-start = (f32[3,16,128]{2,1,0:T(8,128)S(1)}, f32[3,16,128]{2,1,0:T(8,128)S(1)}, u32[]{:S(2)}, u32[]{:S(2)}) collective-permute-start(f32[3,16,128]{2,1,0:T(8,128)S(1)} %get-tuple-element.22), channel_id=1, source_target_pairs={{0,32},{32,0},{64,96},{96,64},{1,33},{33,1},{65,97},{97,65},{2,34}... | collective-permute-start | bytes 73736 | tf_op jit(solution)/shard_map/ppermute | solution.py:439
  6.8 3.5 %collective-permute-start.1 = (f32[3,16,128]{2,1,0:T(8,128)S(1)}, f32[3,16,128]{2,1,0:T(8,128)S(1)}, u32[]{:S(2)}, u32[]{:S(2)}) collective-permute-start(f32[3,16,128]{2,1,0:T(8,128)S(1)} %get-tuple-element.23), channel_id=1, source_target_pairs={{0,1},{1,0},{2,3},{3,2},{4,5},{5,4},{6,7},{7,6},{8,9},{9,8},{10,11... | collective-permute-start | bytes 73736 | tf_op jit(solution)/shard_map/ppermute | solution.py:438
  11.6 3.3 %copy-start.2 = (f32[2,2]{1,0:T(2,128)S(1)}, f32[2,2]{1,0:T(2,128)}, u32[]{:S(2)}) copy-start(f32[2,2]{1,0:T(2,128)} %shift_ref.1) | copy-start | bytes 52
  11.6 3.3 %copy-start.3 = (f32[2,2]{1,0:T(2,128)S(1)}, f32[2,2]{1,0:T(2,128)}, u32[]{:S(2)}) copy-start(f32[2,2]{1,0:T(2,128)} %weight_ref.1) | copy-start | bytes 52
  11.7 3.2 %collective-permute-start.5 = (f32[16,128]{1,0:T(8,128)S(1)}, f32[16,128]{1,0:T(8,128)S(1)}, u32[]{:S(2)}, u32[]{:S(2)}) collective-permute-start(f32[16,128]{1,0:T(8,128)S(1)} %shard_map.50), channel_id=1, source_target_pairs={{0,1},{1,0},{2,3},{3,2},{4,5},{5,4},{6,7},{7,6},{8,9},{9,8},{10,11... | collective-permute-start | bytes 24584 | tf_op jit(solution)/shard_map/ppermute | solution.py:449
  12.7 2.2 %collective-permute-start.4 = (f32[16,128]{1,0:T(8,128)S(1)}, f32[16,128]{1,0:T(8,128)S(1)}, u32[]{:S(2)}, u32[]{:S(2)}) collective-permute-start(f32[16,128]{1,0:T(8,128)S(1)} %shard_map.50), channel_id=1, source_target_pairs={{0,32},{32,0},{64,96},{96,64},{1,33},{33,1},{65,97},{97,65},{2,34}... | collective-permute-start | bytes 24584 | tf_op jit(solution)/shard_map/ppermute | solution.py:450

commit v9 on v7

--- a/solution.py
+++ b/solution.py
@@ -175,7 +175,7 @@
     return lax.fori_loop(0, rows - 2 * reach, step, (zero,) * 4, unroll=True)
 
 
-def first_kernel(field_ref, y2_ref, y1_ref, grown_ref, u1_ref, sums_ref):
+def first_kernel(field_ref, y1_ref, y2_ref, grown_ref, u1_ref, sums_ref):
     rows, depth = field_ref.shape[1:3]
     for half in range(2):
         packs = [merged(y1_ref, y2_ref, f, half) for f in range(3)]
@@ -198,7 +198,7 @@
 
 
 def outer_kernel(
-    shift_ref, weight_ref, grown_ref, u1_ref, u2_ref, sums1_ref, sums2_ref, x2_ref, x1_ref, c1_ref, c2_ref,
+    shift_ref, weight_ref, grown_ref, u1_ref, u2_ref, sums1_ref, sums2_ref, x2_ref, x1_ref, c2_ref, c1_ref,
     b1_ref, b2_ref, line_ref,
 ):
     rows, depth = grown_ref.shape[1:3]
@@ -439,7 +439,7 @@
         first_kernel,
         (f32((3, rows, depth, 2 * width)), wide, f32((4, 8, 128))),
         [VMEM] * 3, flops=8_000_000, bytes_accessed=3_000_000,
-    )(field, y2, y1)
+    )(field, y1, y2)
     x2, x1, sums1 = lax.optimization_barrier((x2, x1, sums1))
     corner = call(corner_kernel, f32((depth, 128)), [VMEM] * 2)(x2, x1)
     c2 = lax.ppermute(corner, "pole", pole_across)
@@ -454,7 +454,7 @@
         outer_kernel,
         (f32((2, 2, depth, width)), f32((2, 4, depth, width)), f32((devices, 128))),
         [VMEM] * 11,
-    )(pole_shift, pole_weight, grown, u1, u2, sums1, sums2, x2, x1, c1, c2)
+    )(pole_shift, pole_weight, grown, u1, u2, sums1, sums2, x2, x1, c2, c1)
 
     lines = lax.all_to_all(line.reshape(devices, 1, 128), ("pole", "tile"), 0, 0, tiled=True)
     combine = functools.partial(combine_kernel, pole_shift.shape[0] * poles)

time: 36.3 us -> 36.4 us (level)
  starting transfers between devices: 7.96 us -> 8.37 us
    ppermute x1, starting transfers between devices: 0.01 us -> 1.31 us  [on_device(): y1 = lax.ppermute(m1, 'pole', pole_near)]
    ppermute x1, starting transfers between devices: 2.41 us -> 1.19 us  [on_device(): y2 = lax.ppermute(m2, 'pole', pole_across)]
  transfers between devices with their start and end apart: 6 -> 6, of which waited for: 2 -> 1; matrix products, arithmetic and copies ran while one was open for 0% -> 0% of each run, Pallas kernels for 9% -> 9%
where the time goes in v9:
time: 36.4 us; the launch traced here: 36.2 us
  blocking collectives  19.5 us (54%)
  starting transfers between devices  8.37 us (23%)
  Pallas kernels  6.16 us (17%)
  waiting for transfers between devices  2.09 us (6%)
    all_to_all x1, blocking collectives, on_device(): lax.all_to_all(line.reshape(devices, 1, 128), ('pole', 'tile'), 0, 0, til...  19.5 us
    ppermute x1, starting transfers between devices, on_device(): x1 = lax.ppermute(s1, 'tile', near)  2.68 us
    ppermute x1, waiting for transfers between devices, on_device(): y2 = lax.ppermute(m2, 'pole', pole_across)  2.07 us
    pallas_call x1, Pallas kernels, on_device(): call(second_kernel, (wide, f32((8, 8, 128))), [VMEM] * 2, flops=12000000,...  1.6 us
    ppermute x1, starting transfers between devices, on_device(): c2 = lax.ppermute(corner, 'pole', pole_across)  1.53 us
    ppermute x1, starting transfers between devices, on_device(): x2 = lax.ppermute(s2, ('pole', 'tile'), pairs)  1.5 us
    ppermute x1, starting transfers between devices, on_device(): y1 = lax.ppermute(m1, 'pole', pole_near)  1.31 us
    pallas_call x1, Pallas kernels, on_device(): call(first_kernel, (f32((3, rows, depth, 2 * width)), wide, f32((4, 8, 12...  1.21 us
  transfers between devices with their start and end apart: 6, of which 1 were waited for; matrix products, arithmetic and copies ran while one was open for 0% of the time, Pallas kernels for 9%

profile of v9, /device:TPU:1, one launch (start us, length us, event | category | flops | bytes accessed | tf_op | source)
XLA Modules:
  0.0 36.2 jit_solution(2194483214305807162)
XLA Ops:
  0.0 0.0 copy-start.1
  0.0 0.0 copy-start
  0.0 1.0 %shard_map.49 = (f32[8,16,128]{2,1,0:T(8,128)S(1)}, f32[8,16,128]{2,1,0:T(8,128)S(1)}) custom-call(f32[2,32,16,128]{3,2,1,0:T(8,128)} %psi_ref.3, f32[32,16,128]{2,1,0:T(8,128)} %trap_ref.3), custom_call_target="tpu_custom_call" | custom-call | flops 2000000000 | bytes 40000000 | tf_op jit(solution)/shard_map/pallas_call | solution.py:416
  1.0 1.5 %collective-permute-start.2 = (f32[8,16,128]{2,1,0:T(8,128)S(1)}, f32[8,16,128]{2,1,0:T(8,128)S(1)}, u32[]{:S(2)}, u32[]{:S(2)}) collective-permute-start(f32[8,16,128]{2,1,0:T(8,128)S(1)} %get-tuple-element.27), channel_id=1, source_target_pairs={{0,32},{1,2},{2,1},{3,4},{4,3},{5,6},{6,5},{7,8},{8,7},{9,10},{10,... | collective-permute-start | bytes 196616 | tf_op jit(solution)/shard_map/ppermute | solution.py:426
  2.5 2.7 %collective-permute-start.3 = (f32[8,16,128]{2,1,0:T(8,128)S(1)}, f32[8,16,128]{2,1,0:T(8,128)S(1)}, u32[]{:S(2)}, u32[]{:S(2)}) collective-permute-start(f32[8,16,128]{2,1,0:T(8,128)S(1)} %get-tuple-element.28), channel_id=1, source_target_pairs={{0,1},{1,0},{2,3},{3,2},{4,5},{5,4},{6,7},{7,6},{8,9},{9,8},{10,11... | collective-permute-start | bytes 196616 | tf_op jit(solution)/shard_map/ppermute | solution.py:427
  5.2 0.0 copy-done.1
  5.2 0.0 copy-done
  5.2 0.4 shard_map.46
  5.5 1.3 %collective-permute-start = (f32[3,16,128]{2,1,0:T(8,128)S(1)}, f32[3,16,128]{2,1,0:T(8,128)S(1)}, u32[]{:S(2)}, u32[]{:S(2)}) collective-permute-start(f32[3,16,128]{2,1,0:T(8,128)S(1)} %get-tuple-element.22), channel_id=1, source_target_pairs={{0,32},{32,0},{64,96},{96,64},{1,33},{33,1},{65,97},{97,65},{2,34}... | collective-permute-start | bytes 73736 | tf_op jit(solution)/shard_map/ppermute | solution.py:435
  6.8 1.2 %collective-permute-start.1 = (f32[3,16,128]{2,1,0:T(8,128)S(1)}, f32[3,16,128]{2,1,0:T(8,128)S(1)}, u32[]{:S(2)}, u32[]{:S(2)}) collective-permute-start(f32[3,16,128]{2,1,0:T(8,128)S(1)} %get-tuple-element.23), channel_id=1, source_target_pairs={{0,96},{32,64},{64,32},{96,0},{1,97},{33,65},{65,33},{97,1},{2,98}... | collective-permute-start | bytes 73736 | tf_op jit(solution)/shard_map/ppermute | solution.py:434
  8.0 0.0 collective-permute-done.y1_ref
  8.0 2.1 %collective-permute-done.1.y2_ref = f32[3,16,128]{2,1,0:T(8,128)S(1)} collective-permute-done((f32[3,16,128]{2,1,0:T(8,128)S(1)}, f32[3,16,128]{2,1,0:T(8,128)S(1)}, u32[]{:S(2)}, u32[]{:S(2)}) %collective-permute-start.1) | collective-permute-done | bytes 24608 | tf_op jit(solution)/shard_map/ppermute | solution.py:434
  10.1 1.2 %shard_map.47 = (f32[3,32,16,256]{3,2,1,0:T(8,128)S(1)}, f32[2,32,16,256]{3,2,1,0:T(8,128)S(1)}, f32[4,8,128]{2,1,0:T(8,128)S(1)}) custom-call(f32[3,32,16,128]{3,2,1,0:T(8,128)S(1)} %get-tuple-element.21.field_ref, f32[3,16,128]{2,1,0:T(8,128)S(1)} %collective-permute-done.y1_ref, f32[3,16,128]{2,1,0:T(8,128)S(1)} %collective-permute-done.1.y2_ref), custom_call_target="tpu_custom_call" | custom-call | flops 8000000 | bytes 3000000 | tf_op jit(solution)/shard_map/pallas_call | solution.py:438
  11.3 0.0 copy-start.2
  11.3 0.0 copy-start.3
  11.3 0.0 collective-permute-done.2.x2_ref
  11.4 0.0 collective-permute-done.3.x1_ref
  11.4 0.1 shard_map.50
  11.5 0.2 collective-permute-start.5
  11.6 1.5 %collective-permute-start.4 = (f32[16,128]{1,0:T(8,128)S(1)}, f32[16,128]{1,0:T(8,128)S(1)}, u32[]{:S(2)}, u32[]{:S(2)}) collective-permute-start(f32[16,128]{1,0:T(8,128)S(1)} %shard_map.50), channel_id=1, source_target_pairs={{0,96},{32,64},{64,32},{96,0},{1,97},{33,65},{65,33},{97,1},{2,98}... | collective-permute-start | bytes 24584 | tf_op jit(solution)/shard_map/ppermute | solution.py:445
  13.2 1.6 %shard_map.48 = (f32[2,32,16,256]{3,2,1,0:T(8,128)S(1)}, f32[8,8,128]{2,1,0:T(8,128)S(1)}) custom-call(f32[3,32,16,256]{3,2,1,0:T(8,128)S(1)} %get-tuple-element.25.grown_ref, f32[2,32,16,256]{3,2,1,0:T(8,128)S(1)} %get-tuple-element.24.u1_ref), custom_call_target="tpu_custom_call" | custom-call | flops 12000000 | bytes 5000000 | tf_op jit(solution)/shard_map/pallas_call | solution.py:448
  14.8 0.0 collective-permute-done.5.c1_ref
  14.8 0.0 collective-permute-done.4.c2_ref
  14.8 0.0 copy-done.2
  14.8 0.0 copy-done.3
  14.8 0.8 %shard_map.51 = (f32[2,2,16,128]{3,2,1,0:T(8,128)S(1)}, f32[2,4,16,128]{3,2,1,0:T(8,128)S(1)}, f32[128,128]{1,0:T(8,128)S(1)}) custom-call(f32[2,2]{1,0:T(2,128)S(1)} %copy-done.2, f32[2,2]{1,0:T(2,128)S(1)} %copy-done.3, f32[3,32,16,256]{3,2,1,0:T(8,128)S(1)} %get-tuple-element.25.grown_ref, f32[2,32,16,256]{3,2,1,0:T(8,128)S(1)} %get-tuple-element.24.u1_ref, ...), custom_call_target="tpu_custom_call" | custom-call | tf_op jit(solution)/shard_map/pallas_call | solution.py:453
  15.6 19.5 %all_to_all.5 = f32[128,1,128]{2,1,0:T(1,128)S(1)} all-to-all(f32[128,1,128]{2,1,0:T(1,128)S(1)} %bitcast.5), channel_id=1, replica_groups=mesh['pole'=4,'tile'=32] {'pole','tile'}, dimensions={0} | all-to-all | bytes 131072 | tf_op jit(solution)/shard_map/all_to_all | solution.py:459
  35.1 1.2 %shard_map.52 = f32[2,32,16,128]{3,2,1,0:T(8,128)} custom-call(f32[3,32,16,128]{3,2,1,0:T(8,128)S(1)} %get-tuple-element.21.field_ref, f32[2,32,16,256]{3,2,1,0:T(8,128)S(1)} %get-tuple-element.24.u1_ref, f32[2,32,16,256]{3,2,1,0:T(8,128)S(1)} %get-tuple-element.26.u2_ref, f32[2,2,16,128]{3,2,1,0:T(8,128)S(1)} %get-tuple-element.34.b1_ref, ...), custom_call_target="tpu_custom_call" | custom-call | tf_op jit(solution)/shard_map/pallas_call | solution.py:461
Async XLA Ops:
  0.0 5.2 %copy-start.1 = (f32[32,16,128]{2,1,0:T(8,128)S(1)}, f32[32,16,128]{2,1,0:T(8,128)}, u32[]{:S(2)}) copy-start(f32[32,16,128]{2,1,0:T(8,128)} %trap_ref.3) | copy-start | bytes 786436
  0.0 5.2 %copy-start = (f32[2,32,16,128]{3,2,1,0:T(8,128)S(1)}, f32[2,32,16,128]{3,2,1,0:T(8,128)}, u32[]{:S(2)}) copy-start(f32[2,32,16,128]{3,2,1,0:T(8,128)} %psi_ref.3) | copy-start | bytes 1572868
  1.0 10.4 %collective-permute-start.2 = (f32[8,16,128]{2,1,0:T(8,128)S(1)}, f32[8,16,128]{2,1,0:T(8,128)S(1)}, u32[]{:S(2)}, u32[]{:S(2)}) collective-permute-start(f32[8,16,128]{2,1,0:T(8,128)S(1)} %get-tuple-element.27), channel_id=1, source_target_pairs={{0,32},{1,2},{2,1},{3,4},{4,3},{5,6},{6,5},{7,8},{8,7},{9,10},{10,... | collective-permute-start | bytes 196616 | tf_op jit(solution)/shard_map/ppermute | solution.py:426
  2.5 8.9 %collective-permute-start.3 = (f32[8,16,128]{2,1,0:T(8,128)S(1)}, f32[8,16,128]{2,1,0:T(8,128)S(1)}, u32[]{:S(2)}, u32[]{:S(2)}) collective-permute-start(f32[8,16,128]{2,1,0:T(8,128)S(1)} %get-tuple-element.28), channel_id=1, source_target_pairs={{0,1},{1,0},{2,3},{3,2},{4,5},{5,4},{6,7},{7,6},{8,9},{9,8},{10,11... | collective-permute-start | bytes 196616 | tf_op jit(solution)/shard_map/ppermute | solution.py:427
  5.5 2.5 %collective-permute-start = (f32[3,16,128]{2,1,0:T(8,128)S(1)}, f32[3,16,128]{2,1,0:T(8,128)S(1)}, u32[]{:S(2)}, u32[]{:S(2)}) collective-permute-start(f32[3,16,128]{2,1,0:T(8,128)S(1)} %get-tuple-element.22), channel_id=1, source_target_pairs={{0,32},{32,0},{64,96},{96,64},{1,33},{33,1},{65,97},{97,65},{2,34}... | collective-permute-start | bytes 73736 | tf_op jit(solution)/shard_map/ppermute | solution.py:435
  6.8 3.3 %collective-permute-start.1 = (f32[3,16,128]{2,1,0:T(8,128)S(1)}, f32[3,16,128]{2,1,0:T(8,128)S(1)}, u32[]{:S(2)}, u32[]{:S(2)}) collective-permute-start(f32[3,16,128]{2,1,0:T(8,128)S(1)} %get-tuple-element.23), channel_id=1, source_target_pairs={{0,96},{32,64},{64,32},{96,0},{1,97},{33,65},{65,33},{97,1},{2,98}... | collective-permute-start | bytes 73736 | tf_op jit(solution)/shard_map/ppermute | solution.py:434
  11.3 3.5 %copy-start.2 = (f32[2,2]{1,0:T(2,128)S(1)}, f32[2,2]{1,0:T(2,128)}, u32[]{:S(2)}) copy-start(f32[2,2]{1,0:T(2,128)} %shift_ref.1) | copy-start | bytes 52
  11.3 3.5 %copy-start.3 = (f32[2,2]{1,0:T(2,128)S(1)}, f32[2,2]{1,0:T(2,128)}, u32[]{:S(2)}) copy-start(f32[2,2]{1,0:T(2,128)} %weight_ref.1) | copy-start | bytes 52
  11.5 3.3 %collective-permute-start.5 = (f32[16,128]{1,0:T(8,128)S(1)}, f32[16,128]{1,0:T(8,128)S(1)}, u32[]{:S(2)}, u32[]{:S(2)}) collective-permute-start(f32[16,128]{1,0:T(8,128)S(1)} %shard_map.50), channel_id=1, source_target_pairs={{0,32},{32,0},{64,96},{96,64},{1,33},{33,1},{65,97},{97,65},{2,34}... | collective-permute-start | bytes 24584 | tf_op jit(solution)/shard_map/ppermute | solution.py:446
  11.6 3.1 %collective-permute-start.4 = (f32[16,128]{1,0:T(8,128)S(1)}, f32[16,128]{1,0:T(8,128)S(1)}, u32[]{:S(2)}, u32[]{:S(2)}) collective-permute-start(f32[16,128]{1,0:T(8,128)S(1)} %shard_map.50), channel_id=1, source_target_pairs={{0,96},{32,64},{64,32},{96,0},{1,97},{33,65},{65,33},{97,1},{2,98}... | collective-permute-start | bytes 24584 | tf_op jit(solution)/shard_map/ppermute | solution.py:445

commit v10 on v9

--- a/solution.py
+++ b/solution.py
@@ -198,7 +198,7 @@
 
 
 def outer_kernel(
-    shift_ref, weight_ref, grown_ref, u1_ref, u2_ref, sums1_ref, sums2_ref, x2_ref, x1_ref, c2_ref, c1_ref,
+    shift_ref, weight_ref, grown_ref, u1_ref, u2_ref, sums1_ref, sums2_ref, x2_ref, x1_ref, c1_ref, c2_ref,
     b1_ref, b2_ref, line_ref,
 ):
     rows, depth = grown_ref.shape[1:3]
@@ -454,7 +454,7 @@
         outer_kernel,
         (f32((2, 2, depth, width)), f32((2, 4, depth, width)), f32((devices, 128))),
         [VMEM] * 11,
-    )(pole_shift, pole_weight, grown, u1, u2, sums1, sums2, x2, x1, c2, c1)
+    )(pole_shift, pole_weight, grown, u1, u2, sums1, sums2, x2, x1, c1, c2)
 
     lines = lax.all_to_all(line.reshape(devices, 1, 128), ("pole", "tile"), 0, 0, tiled=True)
     combine = functools.partial(combine_kernel, pole_shift.shape[0] * poles)

time: 36.4 us -> 36.2 us (level)
  no operation moved by 1% of the time
where the time goes in v10:
time: 36.2 us; the launch traced here: 36.1 us
  blocking collectives  19.3 us (53%)
  starting transfers between devices  8.39 us (23%)
  Pallas kernels  6.16 us (17%)
  waiting for transfers between devices  2.09 us (6%)
    all_to_all x1, blocking collectives, on_device(): lax.all_to_all(line.reshape(devices, 1, 128), ('pole', 'tile'), 0, 0, til...  19.3 us
    ppermute x1, starting transfers between devices, on_device(): x1 = lax.ppermute(s1, 'tile', near)  2.68 us
    ppermute x1, waiting for transfers between devices, on_device(): y2 = lax.ppermute(m2, 'pole', pole_across)  2.07 us
    pallas_call x1, Pallas kernels, on_device(): call(second_kernel, (wide, f32((8, 8, 128))), [VMEM] * 2, flops=12000000,...  1.6 us
    ppermute x1, starting transfers between devices, on_device(): x2 = lax.ppermute(s2, ('pole', 'tile'), pairs)  1.5 us
    ppermute x1, starting transfers between devices, on_device(): y1 = lax.ppermute(m1, 'pole', pole_near)  1.31 us
    ppermute x1, starting transfers between devices, on_device(): c2 = lax.ppermute(corner, 'pole', pole_across)  1.25 us
    pallas_call x1, Pallas kernels, on_device(): call(first_kernel, (f32((3, rows, depth, 2 * width)), wide, f32((4, 8, 12...  1.21 us
  transfers between devices with their start and end apart: 6, of which 1 were waited for; matrix products, arithmetic and copies ran while one was open for 0% of the time, Pallas kernels for 9%

profile of v10, /device:TPU:1, one launch (start us, length us, event | category | flops | bytes accessed | tf_op | source)
XLA Modules:
  0.0 36.1 jit_solution(12734406063665991211)
XLA Ops:
  0.0 0.0 copy-start.1
  0.0 0.0 copy-start
  0.0 1.0 %shard_map.49 = (f32[8,16,128]{2,1,0:T(8,128)S(1)}, f32[8,16,128]{2,1,0:T(8,128)S(1)}) custom-call(f32[2,32,16,128]{3,2,1,0:T(8,128)} %psi_ref.3, f32[32,16,128]{2,1,0:T(8,128)} %trap_ref.3), custom_call_target="tpu_custom_call" | custom-call | flops 2000000000 | bytes 40000000 | tf_op jit(solution)/shard_map/pallas_call | solution.py:416
  1.0 1.5 %collective-permute-start.2 = (f32[8,16,128]{2,1,0:T(8,128)S(1)}, f32[8,16,128]{2,1,0:T(8,128)S(1)}, u32[]{:S(2)}, u32[]{:S(2)}) collective-permute-start(f32[8,16,128]{2,1,0:T(8,128)S(1)} %get-tuple-element.27), channel_id=1, source_target_pairs={{0,32},{1,2},{2,1},{3,4},{4,3},{5,6},{6,5},{7,8},{8,7},{9,10},{10,... | collective-permute-start | bytes 196616 | tf_op jit(solution)/shard_map/ppermute | solution.py:426
  2.5 2.7 %collective-permute-start.3 = (f32[8,16,128]{2,1,0:T(8,128)S(1)}, f32[8,16,128]{2,1,0:T(8,128)S(1)}, u32[]{:S(2)}, u32[]{:S(2)}) collective-permute-start(f32[8,16,128]{2,1,0:T(8,128)S(1)} %get-tuple-element.28), channel_id=1, source_target_pairs={{0,1},{1,0},{2,3},{3,2},{4,5},{5,4},{6,7},{7,6},{8,9},{9,8},{10,11... | collective-permute-start | bytes 196616 | tf_op jit(solution)/shard_map/ppermute | solution.py:427
  5.2 0.0 copy-done.1
  5.2 0.0 copy-done
  5.2 0.4 shard_map.46
  5.5 1.3 %collective-permute-start = (f32[3,16,128]{2,1,0:T(8,128)S(1)}, f32[3,16,128]{2,1,0:T(8,128)S(1)}, u32[]{:S(2)}, u32[]{:S(2)}) collective-permute-start(f32[3,16,128]{2,1,0:T(8,128)S(1)} %get-tuple-element.22), channel_id=1, source_target_pairs={{0,32},{32,0},{64,96},{96,64},{1,33},{33,1},{65,97},{97,65},{2,34}... | collective-permute-start | bytes 73736 | tf_op jit(solution)/shard_map/ppermute | solution.py:435
  6.8 1.2 %collective-permute-start.1 = (f32[3,16,128]{2,1,0:T(8,128)S(1)}, f32[3,16,128]{2,1,0:T(8,128)S(1)}, u32[]{:S(2)}, u32[]{:S(2)}) collective-permute-start(f32[3,16,128]{2,1,0:T(8,128)S(1)} %get-tuple-element.23), channel_id=1, source_target_pairs={{0,96},{32,64},{64,32},{96,0},{1,97},{33,65},{65,33},{97,1},{2,98}... | collective-permute-start | bytes 73736 | tf_op jit(solution)/shard_map/ppermute | solution.py:434
  8.0 0.0 collective-permute-done.y1_ref
  8.0 2.1 %collective-permute-done.1.y2_ref = f32[3,16,128]{2,1,0:T(8,128)S(1)} collective-permute-done((f32[3,16,128]{2,1,0:T(8,128)S(1)}, f32[3,16,128]{2,1,0:T(8,128)S(1)}, u32[]{:S(2)}, u32[]{:S(2)}) %collective-permute-start.1) | collective-permute-done | bytes 24608 | tf_op jit(solution)/shard_map/ppermute | solution.py:434
  10.1 1.2 %shard_map.47 = (f32[3,32,16,256]{3,2,1,0:T(8,128)S(1)}, f32[2,32,16,256]{3,2,1,0:T(8,128)S(1)}, f32[4,8,128]{2,1,0:T(8,128)S(1)}) custom-call(f32[3,32,16,128]{3,2,1,0:T(8,128)S(1)} %get-tuple-element.21.field_ref, f32[3,16,128]{2,1,0:T(8,128)S(1)} %collective-permute-done.y1_ref, f32[3,16,128]{2,1,0:T(8,128)S(1)} %collective-permute-done.1.y2_ref), custom_call_target="tpu_custom_call" | custom-call | flops 8000000 | bytes 3000000 | tf_op jit(solution)/shard_map/pallas_call | solution.py:438
  11.3 0.0 copy-start.2
  11.3 0.0 copy-start.3
  11.3 0.0 collective-permute-done.2.x2_ref
  11.4 0.0 collective-permute-done.3.x1_ref
  11.4 0.1 shard_map.50
  11.5 1.3 %collective-permute-start.5 = (f32[16,128]{1,0:T(8,128)S(1)}, f32[16,128]{1,0:T(8,128)S(1)}, u32[]{:S(2)}, u32[]{:S(2)}) collective-permute-start(f32[16,128]{1,0:T(8,128)S(1)} %shard_map.50), channel_id=1, source_target_pairs={{0,96},{32,64},{64,32},{96,0},{1,97},{33,65},{65,33},{97,1},{2,98}... | collective-permute-start | bytes 24584 | tf_op jit(solution)/shard_map/ppermute | solution.py:445
  12.7 0.4 %collective-permute-start.4 = (f32[16,128]{1,0:T(8,128)S(1)}, f32[16,128]{1,0:T(8,128)S(1)}, u32[]{:S(2)}, u32[]{:S(2)}) collective-permute-start(f32[16,128]{1,0:T(8,128)S(1)} %shard_map.50), channel_id=1, source_target_pairs={{0,32},{32,0},{64,96},{96,64},{1,33},{33,1},{65,97},{97,65},{2,34}... | collective-permute-start | bytes 24584 | tf_op jit(solution)/shard_map/ppermute | solution.py:446
  13.2 1.6 %shard_map.48 = (f32[2,32,16,256]{3,2,1,0:T(8,128)S(1)}, f32[8,8,128]{2,1,0:T(8,128)S(1)}) custom-call(f32[3,32,16,256]{3,2,1,0:T(8,128)S(1)} %get-tuple-element.25.grown_ref, f32[2,32,16,256]{3,2,1,0:T(8,128)S(1)} %get-tuple-element.24.u1_ref), custom_call_target="tpu_custom_call" | custom-call | flops 12000000 | bytes 5000000 | tf_op jit(solution)/shard_map/pallas_call | solution.py:448
  14.8 0.0 collective-permute-done.5.c2_ref
  14.8 0.0 collective-permute-done.4.c1_ref
  14.8 0.0 copy-done.2
  14.8 0.0 copy-done.3
  14.8 0.8 %shard_map.51 = (f32[2,2,16,128]{3,2,1,0:T(8,128)S(1)}, f32[2,4,16,128]{3,2,1,0:T(8,128)S(1)}, f32[128,128]{1,0:T(8,128)S(1)}) custom-call(f32[2,2]{1,0:T(2,128)S(1)} %copy-done.2, f32[2,2]{1,0:T(2,128)S(1)} %copy-done.3, f32[3,32,16,256]{3,2,1,0:T(8,128)S(1)} %get-tuple-element.25.grown_ref, f32[2,32,16,256]{3,2,1,0:T(8,128)S(1)} %get-tuple-element.24.u1_ref, ...), custom_call_target="tpu_custom_call" | custom-call | tf_op jit(solution)/shard_map/pallas_call | solution.py:453
  15.6 19.3 %all_to_all.5 = f32[128,1,128]{2,1,0:T(1,128)S(1)} all-to-all(f32[128,1,128]{2,1,0:T(1,128)S(1)} %bitcast.5), channel_id=1, replica_groups=mesh['pole'=4,'tile'=32] {'pole','tile'}, dimensions={0} | all-to-all | bytes 131072 | tf_op jit(solution)/shard_map/all_to_all | solution.py:459
  34.9 1.2 %shard_map.52 = f32[2,32,16,128]{3,2,1,0:T(8,128)} custom-call(f32[3,32,16,128]{3,2,1,0:T(8,128)S(1)} %get-tuple-element.21.field_ref, f32[2,32,16,256]{3,2,1,0:T(8,128)S(1)} %get-tuple-element.24.u1_ref, f32[2,32,16,256]{3,2,1,0:T(8,128)S(1)} %get-tuple-element.26.u2_ref, f32[2,2,16,128]{3,2,1,0:T(8,128)S(1)} %get-tuple-element.34.b1_ref, ...), custom_call_target="tpu_custom_call" | custom-call | tf_op jit(solution)/shard_map/pallas_call | solution.py:461
Async XLA Ops:
  0.0 5.2 %copy-start.1 = (f32[32,16,128]{2,1,0:T(8,128)S(1)}, f32[32,16,128]{2,1,0:T(8,128)}, u32[]{:S(2)}) copy-start(f32[32,16,128]{2,1,0:T(8,128)} %trap_ref.3) | copy-start | bytes 786436
  0.0 5.2 %copy-start = (f32[2,32,16,128]{3,2,1,0:T(8,128)S(1)}, f32[2,32,16,128]{3,2,1,0:T(8,128)}, u32[]{:S(2)}) copy-start(f32[2,32,16,128]{3,2,1,0:T(8,128)} %psi_ref.3) | copy-start | bytes 1572868
  1.0 10.4 %collective-permute-start.2 = (f32[8,16,128]{2,1,0:T(8,128)S(1)}, f32[8,16,128]{2,1,0:T(8,128)S(1)}, u32[]{:S(2)}, u32[]{:S(2)}) collective-permute-start(f32[8,16,128]{2,1,0:T(8,128)S(1)} %get-tuple-element.27), channel_id=1, source_target_pairs={{0,32},{1,2},{2,1},{3,4},{4,3},{5,6},{6,5},{7,8},{8,7},{9,10},{10,... | collective-permute-start | bytes 196616 | tf_op jit(solution)/shard_map/ppermute | solution.py:426
  2.5 8.9 %collective-permute-start.3 = (f32[8,16,128]{2,1,0:T(8,128)S(1)}, f32[8,16,128]{2,1,0:T(8,128)S(1)}, u32[]{:S(2)}, u32[]{:S(2)}) collective-permute-start(f32[8,16,128]{2,1,0:T(8,128)S(1)} %get-tuple-element.28), channel_id=1, source_target_pairs={{0,1},{1,0},{2,3},{3,2},{4,5},{5,4},{6,7},{7,6},{8,9},{9,8},{10,11... | collective-permute-start | bytes 196616 | tf_op jit(solution)/shard_map/ppermute | solution.py:427
  5.5 2.5 %collective-permute-start = (f32[3,16,128]{2,1,0:T(8,128)S(1)}, f32[3,16,128]{2,1,0:T(8,128)S(1)}, u32[]{:S(2)}, u32[]{:S(2)}) collective-permute-start(f32[3,16,128]{2,1,0:T(8,128)S(1)} %get-tuple-element.22), channel_id=1, source_target_pairs={{0,32},{32,0},{64,96},{96,64},{1,33},{33,1},{65,97},{97,65},{2,34}... | collective-permute-start | bytes 73736 | tf_op jit(solution)/shard_map/ppermute | solution.py:435
  6.8 3.3 %collective-permute-start.1 = (f32[3,16,128]{2,1,0:T(8,128)S(1)}, f32[3,16,128]{2,1,0:T(8,128)S(1)}, u32[]{:S(2)}, u32[]{:S(2)}) collective-permute-start(f32[3,16,128]{2,1,0:T(8,128)S(1)} %get-tuple-element.23), channel_id=1, source_target_pairs={{0,96},{32,64},{64,32},{96,0},{1,97},{33,65},{65,33},{97,1},{2,98}... | collective-permute-start | bytes 73736 | tf_op jit(solution)/shard_map/ppermute | solution.py:434
  11.3 3.5 %copy-start.2 = (f32[2,2]{1,0:T(2,128)S(1)}, f32[2,2]{1,0:T(2,128)}, u32[]{:S(2)}) copy-start(f32[2,2]{1,0:T(2,128)} %shift_ref.1) | copy-start | bytes 52
  11.3 3.5 %copy-start.3 = (f32[2,2]{1,0:T(2,128)S(1)}, f32[2,2]{1,0:T(2,128)}, u32[]{:S(2)}) copy-start(f32[2,2]{1,0:T(2,128)} %weight_ref.1) | copy-start | bytes 52
  11.5 3.3 %collective-permute-start.5 = (f32[16,128]{1,0:T(8,128)S(1)}, f32[16,128]{1,0:T(8,128)S(1)}, u32[]{:S(2)}, u32[]{:S(2)}) collective-permute-start(f32[16,128]{1,0:T(8,128)S(1)} %shard_map.50), channel_id=1, source_target_pairs={{0,96},{32,64},{64,32},{96,0},{1,97},{33,65},{65,33},{97,1},{2,98}... | collective-permute-start | bytes 24584 | tf_op jit(solution)/shard_map/ppermute | solution.py:445
  12.7 2.1 %collective-permute-start.4 = (f32[16,128]{1,0:T(8,128)S(1)}, f32[16,128]{1,0:T(8,128)S(1)}, u32[]{:S(2)}, u32[]{:S(2)}) collective-permute-start(f32[16,128]{1,0:T(8,128)S(1)} %shard_map.50), channel_id=1, source_target_pairs={{0,32},{32,0},{64,96},{96,64},{1,33},{33,1},{65,97},{97,65},{2,34}... | collective-permute-start | bytes 24584 | tf_op jit(solution)/shard_map/ppermute | solution.py:446
